TPU v7x, 128 devices: a whole 4x4x4 slice. The times are simulated.
128 devices in a mesh: rep: 8 (over z, x_lo), feat: 16 (over x_hi, y, core).
Axes of the slice: x: 4 (x_hi: 2, x_lo: 2; x = x_hi * 2 + x_lo), y: 4, z: 4, core: 2. Of those that a mesh axis runs over, the one named last changes fastest.
Arguments:
- hidden: bfloat16 [4, 8192, 4096], P(None, 'rep', 'feat'), may hold values from -6 to 6
- labels: int32 [4, 8192, 1024], P(None, 'rep'), may hold values 0 or 1
- weights: float32 [8, 4096, 1024], P('rep', 'feat'), may hold values from -0.09375 to 0.09375
Outputs:
- trained: float32 [8, 4096, 1024], P('rep', 'feat')
All inputs are finite; a program needn't handle non-finite values. No bound on the sum of `labels` on one device may be relied on, other than what follows from the above.
Results may differ from a plain program's by a relative error of at most 0.0009.
Values sent between devices are 32-bit elements; how exact they have to be, the bound alone decides.
No kernel may reach another device: no remote copies, remote signals or barrier semaphores. Data moves between devices by JAX's collectives and lax.ppermute only.
A program may use at most 128 MiB of HBM per device.

v0:
```python
import jax
import jax.numpy as jnp
from jax import lax
from jax.sharding import PartitionSpec as P

STEPS = 4


def from_partner(x, axis, bit):
    return lax.ppermute(x, axis, [(i, i ^ 1 << bit) for i in range(lax.axis_size(axis))])


def local(hidden, labels, weights):
    bits = lax.axis_size("rep").bit_length() - 1
    state = weights[0]
    for step in range(STEPS):
        rows = hidden[step].astype(jnp.float32)
        partial_margin = jnp.dot(
            rows, state, precision=lax.Precision.HIGHEST, preferred_element_type=jnp.float32
        )
        margin = lax.psum(partial_margin, "feat")
        residual = jax.nn.sigmoid(margin) - labels[step].astype(jnp.float32)
        grad = lax.dot_general(
            rows,
            residual,
            (((0,), (0,)), ((), ())),
            precision=lax.Precision.HIGHEST,
            preferred_element_type=jnp.float32,
        )
        update = state - 2.0 / rows.shape[0] * grad
        partner = from_partner(update, "rep", step % bits)
        state = 0.5 * (update + partner)
    return state[None]


def solution(mesh):
    in_specs = (P(None, "rep", "feat"), P(None, "rep", None), P("rep", "feat", None))
    out_specs = P("rep", "feat", None)
    return jax.shard_map(local, mesh=mesh, in_specs=in_specs, out_specs=out_specs, check_vma=False)
```

profile of v0, /device:TPU:1, one launch (start us, length us, event | category | flops | bytes accessed | tf_op | source)
XLA Modules:
  0.0 759.6 jit_solution(10053166524131454700)
XLA Ops:
  6.5 5.3 fusion.44
  11.9 1.3 copy.4
  13.2 151.9 %all-reduce.5.cloned.1.call-done = f32[1024,1024]{1,0:T(8,128)} async-done(((f32[1024,1024]{1,0:T(8,128)}), f32[1024,1024]{1,0:T(8,128)}) %all-reduce.5.cloned.1.call-update) | async-done | bytes 4194320 | tf_op jit(solution)/shard_map/psum | solution.py:21
  165.1 7.5 fusion.43
  172.7 0.4 collective-permute-start
  173.0 23.0 %collective-permute-done = f32[256,1024]{0,1:T(8,128)S(1)} collective-permute-done((f32[256,1024]{0,1:T(8,128)S(1)}, f32[256,1024]{0,1:T(8,128)S(1)}, u32[]{:S(2)}, u32[]{:S(2)}) %collective-permute-start) | collective-permute-done | bytes 1048608 | tf_op jit(solution)/shard_map/ppermute | solution.py:10
  196.0 1.1 copy-done.5
  197.1 3.9 convolution_bitcast_fusion.2
  201.2 148.6 %all-reduce.7.cloned.1.call-done = f32[1024,1024]{1,0:T(8,128)} async-done(((f32[1024,1024]{1,0:T(8,128)}), f32[1024,1024]{1,0:T(8,128)}) %all-reduce.7.cloned.1.call-update) | async-done | bytes 4194320 | tf_op jit(solution)/shard_map/psum | solution.py:21
  349.9 7.8 %fusion.42 = f32[256,1024]{0,1:T(8,128)S(1)} fusion(s32[4,1024,1024]{2,1,0:T(8,128)} %param.4, f32[1024,1024]{1,0:T(8,128)} %all-reduce.7.cloned.1.call-done, bf16[4,1024,256]{2,1,0:T(8,128)(2,1)S(1)} %copy-done.1, f32[256,1024]{0,1:T(8,128)} %copy-done.2, f32[256,1024]{0,1:T(8,128)} %copy-done.5), kind=kOutput, calls=%fused_computation.49 | convolution fusion | flops 3227516928 | bytes 12058624 | tf_op jit(solution)/shard_map/dot_general | solution.py:23
  357.6 1.4 collective-permute-start.1
  359.0 22.0 %collective-permute-done.1 = f32[256,1024]{0,1:T(8,128)S(1)} collective-permute-done((f32[256,1024]{0,1:T(8,128)S(1)}, f32[256,1024]{0,1:T(8,128)S(1)}, u32[]{:S(2)}, u32[]{:S(2)}) %collective-permute-start.1) | collective-permute-done | bytes 1048608 | tf_op jit(solution)/shard_map/ppermute | solution.py:10
  381.0 1.0 copy-done.6
  382.0 3.9 convolution_bitcast_fusion.1
  385.9 148.6 %all-reduce.9.cloned.1.call-done = f32[1024,1024]{1,0:T(8,128)} async-done(((f32[1024,1024]{1,0:T(8,128)}), f32[1024,1024]{1,0:T(8,128)}) %all-reduce.9.cloned.1.call-update) | async-done | bytes 4194320 | tf_op jit(solution)/shard_map/psum | solution.py:21
  534.5 7.5 fusion.41
  542.0 3.2 collective-permute-start.2
  545.2 21.9 %collective-permute-done.2 = f32[256,1024]{0,1:T(8,128)S(1)} collective-permute-done((f32[256,1024]{0,1:T(8,128)S(1)}, f32[256,1024]{0,1:T(8,128)S(1)}, u32[]{:S(2)}, u32[]{:S(2)}) %collective-permute-start.2) | collective-permute-done | bytes 1048608 | tf_op jit(solution)/shard_map/ppermute | solution.py:10
  567.1 1.1 copy-done.7
  568.2 3.9 convolution_bitcast_fusion
  572.1 148.7 %all-reduce.11.cloned.1.call-done = f32[1024,1024]{1,0:T(8,128)} async-done(((f32[1024,1024]{1,0:T(8,128)}), f32[1024,1024]{1,0:T(8,128)}) %all-reduce.11.cloned.1.call-update) | async-done | bytes 4194320 | tf_op jit(solution)/shard_map/psum | solution.py:21
  720.7 7.5 fusion.40
  728.6 23.0 %collective-permute-done.3 = f32[256,1024]{0,1:T(8,128)S(1)} collective-permute-done((f32[256,1024]{0,1:T(8,128)S(1)}, f32[256,1024]{0,1:T(8,128)S(1)}, u32[]{:S(2)}, u32[]{:S(2)}) %collective-permute-start.3) | collective-permute-done | bytes 1048608 | tf_op jit(solution)/shard_map/ppermute | solution.py:10
  751.7 1.3 copy.5
  (23 shorter events, 0.9 us)
Async XLA Ops:
  6.5 5.4 copy-start
  6.5 158.6 %all-reduce.5.cloned.1.call-start = ((), (), s32[]{:S(2)}) async-start(), calls=%async_computation | async-start | bytes 8388608 | tf_op jit(solution)/shard_map/psum | solution.py:21
  11.8 153.3 %copy-start.1 = (bf16[4,1024,256]{2,1,0:T(8,128)(2,1)S(1)}, bf16[4,1024,256]{2,1,0:T(8,128)(2,1)}, u32[]{:S(2)}) copy-start(bf16[4,1024,256]{2,1,0:T(8,128)(2,1)} %param.3) | copy-start | bytes 6291460
  11.9 338.0 %all-reduce.7.cloned.1.call-start = ((), (), s32[]{:S(2)}) async-start(), calls=%async_computation.1 | async-start | bytes 8388608 | tf_op jit(solution)/shard_map/psum | solution.py:21
  172.6 23.4 %copy-start.2 = (f32[256,1024]{0,1:T(8,128)}, f32[256,1024]{0,1:T(8,128)S(1)}, u32[]{:S(2)}) copy-start(f32[256,1024]{0,1:T(8,128)S(1)} %fusion.43) | copy-start | bytes 3145732
  172.7 23.3 %collective-permute-start = (f32[256,1024]{0,1:T(8,128)S(1)}, f32[256,1024]{0,1:T(8,128)S(1)}, u32[]{:S(2)}, u32[]{:S(2)}) collective-permute-start(f32[256,1024]{0,1:T(8,128)S(1)} %fusion.43), channel_id=1, source_target_pairs={{0,16},{16,0},{32,48},{48,32},{64,80},{80,64},{96,112},{112,96},{1... | collective-permute-start | bytes 3145736 | tf_op jit(solution)/shard_map/ppermute | solution.py:10
  196.0 1.1 copy-start.5
  201.0 333.6 %all-reduce.9.cloned.1.call-start = ((), (), s32[]{:S(2)}) async-start(), calls=%async_computation.2 | async-start | bytes 8388608 | tf_op jit(solution)/shard_map/psum | solution.py:21
  357.6 23.3 %collective-permute-start.1 = (f32[256,1024]{0,1:T(8,128)S(1)}, f32[256,1024]{0,1:T(8,128)S(1)}, u32[]{:S(2)}, u32[]{:S(2)}) collective-permute-start(f32[256,1024]{0,1:T(8,128)S(1)} %fusion.42), channel_id=1, source_target_pairs={{0,32},{16,48},{32,0},{48,16},{64,96},{80,112},{96,64},{112,80},{1... | collective-permute-start | bytes 3145736 | tf_op jit(solution)/shard_map/ppermute | solution.py:10
  381.0 1.0 copy-start.6
  385.9 334.9 %all-reduce.11.cloned.1.call-start = ((), (), s32[]{:S(2)}) async-start(), calls=%async_computation.3 | async-start | bytes 8388608 | tf_op jit(solution)/shard_map/psum | solution.py:21
  542.0 25.1 %copy-start.3 = (f32[256,1024]{0,1:T(8,128)}, f32[256,1024]{0,1:T(8,128)S(1)}, u32[]{:S(2)}) copy-start(f32[256,1024]{0,1:T(8,128)S(1)} %fusion.41) | copy-start | bytes 3145732
  542.0 25.1 %collective-permute-start.2 = (f32[256,1024]{0,1:T(8,128)S(1)}, f32[256,1024]{0,1:T(8,128)S(1)}, u32[]{:S(2)}, u32[]{:S(2)}) collective-permute-start(f32[256,1024]{0,1:T(8,128)S(1)} %fusion.41), channel_id=1, source_target_pairs={{0,64},{16,80},{32,96},{48,112},{64,0},{80,16},{96,32},{112,48},{1... | collective-permute-start | bytes 3145736 | tf_op jit(solution)/shard_map/ppermute | solution.py:10
  567.1 1.1 copy-start.7
  572.1 148.7 %copy-start.4 = (f32[256,1024]{0,1:T(8,128)S(1)}, f32[256,1024]{0,1:T(8,128)}, u32[]{:S(2)}) copy-start(f32[256,1024]{0,1:T(8,128)} %copy-done.3) | copy-start | bytes 3145732
  728.2 23.3 %collective-permute-start.3 = (f32[256,1024]{0,1:T(8,128)S(1)}, f32[256,1024]{0,1:T(8,128)S(1)}, u32[]{:S(2)}, u32[]{:S(2)}) collective-permute-start(f32[256,1024]{0,1:T(8,128)S(1)} %fusion.40), channel_id=1, source_target_pairs={{0,16},{16,0},{32,48},{48,32},{64,80},{80,64},{96,112},{112,96},{1... | collective-permute-start | bytes 3145736 | tf_op jit(solution)/shard_map/ppermute | solution.py:10
Sparse Core Ops, SparseCore 0:
  12.0 153.1 all-reduce.4
  201.1 148.7 all-reduce.6
  386.0 148.5 all-reduce.8
  572.2 148.5 all-reduce.10
where the time goes:
time: 761 us; the launch traced here: 760 us
  waiting for transfers between devices  688 us (90%)
  matrix products  47.2 us (6%)
  between operations  13.2 us (2%)
    psum x4, waiting for transfers between devices, local(): margin = lax.psum(partial_margin, 'feat')  598 us
    ppermute x4, waiting for transfers between devices, from_partner(): lax.ppermute(x, axis, [(i, i ^ 1 << bit) for i in range(lax.axis_size(axi...  89.8 us
    dot_general x4, matrix products, local(): lax.dot_general(rows, residual, (((0,), (0,)), ((), ())), precision=lax.P...  30.2 us
    dot_general x4, matrix products, local(): jnp.dot(rows, state, precision=lax.Precision.HIGHEST, preferred_element_t...  17 us
  transfers between devices with their start and end apart: 8, of which 8 were waited for; matrix products, arithmetic and copies ran while one was open for 0% of the time, Pallas kernels for 0%

commit v1 on v0

v1 whole, which is shorter than its diff:
```python
import jax
import jax.numpy as jnp
import numpy as np
from jax import lax
from jax.experimental import pallas as pl
from jax.experimental.pallas import tpu as pltpu
from jax.sharding import Mesh, PartitionSpec as P

STEPS = 4
Y, CORES = 4, 2
LANES = Y * CORES


def xor_perm(size, mask):
    return [(i, i ^ mask) for i in range(size)]


def widen(hidden):
    steps, rows, feats = hidden.shape

    def body(x_ref, o_ref):
        o_ref[...] = x_ref[...].astype(jnp.float32)

    spec = pl.BlockSpec((1, rows, feats), lambda s: (s, 0, 0))
    return pl.pallas_call(
        body,
        grid=(steps,),
        in_specs=[spec],
        out_specs=spec,
        out_shape=jax.ShapeDtypeStruct(hidden.shape, jnp.float32),
    )(hidden)


def narrow(blocks, order):
    count, rows, feats = blocks.shape

    def body(order_ref, x_ref, o_ref):
        o_ref[...] = x_ref[0].astype(jnp.bfloat16)

    return pl.pallas_call(
        body,
        grid_spec=pltpu.PrefetchScalarGridSpec(
            num_scalar_prefetch=1,
            grid=(count,),
            in_specs=[pl.BlockSpec((1, rows, feats), lambda i, order: (order[i], 0, 0))],
            out_specs=pl.BlockSpec((rows, feats), lambda i, order: (0, i)),
        ),
        out_shape=jax.ShapeDtypeStruct((rows, count * feats), jnp.bfloat16),
    )(order, blocks)


def weights_in(weights, order):
    feats, probes = weights.shape
    width = probes // LANES

    def body(order_ref, w_ref, o_ref):
        o_ref[0] = w_ref[...].T

    return pl.pallas_call(
        body,
        grid_spec=pltpu.PrefetchScalarGridSpec(
            num_scalar_prefetch=1,
            grid=(LANES,),
            in_specs=[pl.BlockSpec((feats, width), lambda i, order: (0, order[i]))],
            out_specs=pl.BlockSpec((1, width, feats), lambda i, order: (i, 0, 0)),
        ),
        out_shape=jax.ShapeDtypeStruct((LANES, width, feats), jnp.float32),
    )(order, weights)


def weights_out(blocks, order):
    _, width, feats = blocks.shape

    def body(order_ref, w_ref, o_ref):
        o_ref[...] = w_ref[0].T

    return pl.pallas_call(
        body,
        grid_spec=pltpu.PrefetchScalarGridSpec(
            num_scalar_prefetch=1,
            grid=(LANES,),
            in_specs=[pl.BlockSpec((1, width, feats), lambda i, order: (i, 0, 0))],
            out_specs=pl.BlockSpec((feats, width), lambda i, order: (0, order[i])),
        ),
        out_shape=jax.ShapeDtypeStruct((feats, LANES * width), jnp.float32),
    )(order, blocks)


def labels_in(labels, order):
    steps, rows, probes = labels.shape
    width = probes // LANES

    def body(order_ref, l_ref, o_ref):
        o_ref[0] = l_ref[0].astype(jnp.float32).T

    return pl.pallas_call(
        body,
        grid_spec=pltpu.PrefetchScalarGridSpec(
            num_scalar_prefetch=1,
            grid=(steps,),
            in_specs=[pl.BlockSpec((1, rows, width), lambda s, order: (s, 0, order[0]))],
            out_specs=pl.BlockSpec((1, width, rows), lambda s, order: (s, 0, 0)),
        ),
        out_shape=jax.ShapeDtypeStruct((steps, width, rows), jnp.float32),
    )(order, labels)


def pieces(x):
    high = lax.reduce_precision(x, 8, 7)
    return jnp.concatenate([high.astype(jnp.bfloat16), (x - high).astype(jnp.bfloat16)])


def two_pass(x, y, dims):
    n = x.shape[0]
    out = lax.dot_general(pieces(x), y, dims, preferred_element_type=jnp.float32)
    return out[:n] + out[n:]


def gather_first(x):
    half = x.shape[0] // 2
    one = lax.ppermute(x, "y", xor_perm(Y, 1))
    three = lax.ppermute(x, "y", xor_perm(Y, 3))
    two = jnp.concatenate(
        [
            lax.ppermute(one[:half], "y", xor_perm(Y, 3)),
            lax.ppermute(three[half:], "y", xor_perm(Y, 1)),
        ]
    )
    own = jnp.stack([x, one, two, three])
    other = lax.ppermute(own, "core", xor_perm(CORES, 1))
    return jnp.stack([own, other], axis=1).reshape((LANES,) + x.shape)


def local(hidden, labels, weights):
    rows, feats = hidden.shape[1:]
    y, core = lax.axis_index("y"), lax.axis_index("core")
    order = jnp.stack(
        [(y ^ k) * CORES + (core ^ j) for k in range(Y) for j in range(CORES)]
    ).astype(jnp.int32)
    straight = jnp.arange(LANES, dtype=jnp.int32)

    wide = widen(hidden)
    first = gather_first(wide[0])

    blocks = weights_in(weights[0], order).reshape(Y, CORES, -1, feats)
    width = blocks.shape[2]
    other = lax.ppermute(blocks[:, 1], "core", xor_perm(CORES, 1))
    blocks = jnp.concatenate([blocks[:, 0], other], axis=-1)
    state = jnp.concatenate(
        [blocks[0]] + [lax.ppermute(blocks[k], "y", xor_perm(Y, k)) for k in (1, 2, 3)], axis=-1
    )

    targets = labels_in(labels, order)
    later = [lax.all_gather(wide[s], ("y", "core")) for s in range(1, STEPS)]

    for step in range(STEPS):
        x = narrow(first, straight) if step == 0 else narrow(later[step - 1], order)
        partial_margin = two_pass(state, x, (((1,), (1,)), ((), ())))
        margin = partial_margin + lax.ppermute(partial_margin, "x_hi", xor_perm(2, 1))
        residual = jax.nn.sigmoid(margin) - targets[step]
        grad = two_pass(residual, x, (((1,), (0,)), ((), ())))
        update = state - 2.0 / rows * grad
        bit = step % 3
        if bit == 0:
            partner = lax.ppermute(update, "x_lo", xor_perm(2, 1))
        else:
            partner = lax.ppermute(update, "z", xor_perm(4, bit))
        state = 0.5 * (update + partner)

    blocks = state.reshape(width, Y, CORES * feats)
    blocks = jnp.stack(
        [blocks[:, 0]] + [lax.ppermute(blocks[:, k], "y", xor_perm(Y, k)) for k in (1, 2, 3)]
    ).reshape(Y, width, CORES, feats)
    other = lax.ppermute(blocks[:, :, 1], "core", xor_perm(CORES, 1))
    blocks = jnp.stack([blocks[:, :, 0], other], axis=1).reshape(LANES, width, feats)
    return weights_out(blocks, order)[None]


def solution(mesh):
    devices = np.asarray(mesh.devices).reshape(4, 2, 2, Y, CORES)
    fine = Mesh(devices, ("z", "x_lo", "x_hi", "y", "core"))
    rep, feat = ("z", "x_lo"), ("x_hi", "y", "core")
    in_specs = (P(None, rep, feat), P(None, rep, None), P(rep, feat, None))
    return jax.shard_map(
        local, mesh=fine, in_specs=in_specs, out_specs=P(rep, feat, None), check_vma=False
    )
```

time: 761 us -> 333 us (0.44)
  waiting for transfers between devices: 688 us -> 158 us
  Pallas kernels: 0 us -> 55.2 us
  starting transfers between devices: 5.57 us -> 54.7 us
  matrix products: 47.2 us -> 21.6 us
  other arithmetic: 0.14 us -> 15.7 us
    psum x4 -> x0, waiting for transfers between devices: 598 us -> none  [local(): margin = lax.psum(partial_margin, 'feat')]
    ppermute x4 -> x21, waiting for transfers between devices: 89.8 us -> 157 us  [the longest x2 36 us: local(): partner = lax.ppermute(update, 'x_lo', xor_perm(2, 1))]
    pallas_call x0 -> x8, Pallas kernels: none -> 55.2 us  [the longest x4 33.8 us: narrow(): pl.pallas_call(body, grid_spec=pltpu.PrefetchScalarGridSpec(num_scalar_pr...]
    ppermute x4 -> x21, starting transfers between devices: 5.26 us -> 54.6 us  [the longest x4 11.9 us: local(): lax.ppermute(partial_margin, 'x_hi', xor_perm(2, 1))]
    dot_general x8, matrix products: 47.2 us -> 21.6 us  [two_pass(): lax.dot_general(pieces(x), y, dims, preferred_element_type=jnp.float32)]
  transfers between devices with their start and end apart: 8 -> 24, of which waited for: 8 -> 18; matrix products, arithmetic and copies ran while one was open for 0% -> 11% of each run, Pallas kernels for 0% -> 14%
where the time goes in v1:
time: 333 us; the launch traced here: 331 us
  waiting for transfers between devices  158 us (47%)
  Pallas kernels  55.2 us (17%)
  starting transfers between devices  54.7 us (16%)
  matrix products  21.6 us (6%)
  other arithmetic  15.7 us (5%)
  between operations  13.5 us (4%)
  local copies, waits for them, and re-layouts  12.3 us (4%)
    ppermute x2, waiting for transfers between devices, local(): partner = lax.ppermute(update, 'x_lo', xor_perm(2, 1))  36 us
    pallas_call x4, Pallas kernels, narrow(): pl.pallas_call(body, grid_spec=pltpu.PrefetchScalarGridSpec(num_scalar_pr...  33.8 us
    ppermute x1, waiting for transfers between devices, gather_first(): one = lax.ppermute(x, 'y', xor_perm(Y, 1))  30.2 us
    ppermute x4, waiting for transfers between devices, local(): lax.ppermute(partial_margin, 'x_hi', xor_perm(2, 1))  23.9 us
    ppermute x1, waiting for transfers between devices, gather_first(): lax.ppermute(one[:half], 'y', xor_perm(Y, 3))  23.4 us
    dot_general x8, matrix products, two_pass(): lax.dot_general(pieces(x), y, dims, preferred_element_type=jnp.float32)  21.6 us
    ppermute x2, waiting for transfers between devices, local(): partner = lax.ppermute(update, 'z', xor_perm(4, bit))  15.6 us
    ppermute x3, waiting for transfers between devices, local(): lax.ppermute(blocks[k], 'y', xor_perm(Y, k))  15.3 us
  transfers between devices with their start and end apart: 24, of which 18 were waited for; matrix products, arithmetic and copies ran while one was open for 11% of the time, Pallas kernels for 14%

profile of v1, /device:TPU:1, one launch (start us, length us, event | category | flops | bytes accessed | tf_op | source)
XLA Modules:
  0.0 331.0 jit_solution(11835205399598073934)
XLA Ops:
  6.5 4.2 %shard_map.38 = f32[4,1024,256]{2,1,0:T(8,128)} custom-call(bf16[4,1024,256]{2,1,0:T(8,128)(2,1)} %x_ref.1), custom_call_target="tpu_custom_call" | custom-call | tf_op jit(solution)/shard_map/pallas_call | solution.py:25
  19.6 30.2 %collective-permute-done.4 = f32[1024,256]{1,0:T(8,128)S(1)} collective-permute-done((f32[1024,256]{1,0:T(8,128)S(1)}, f32[1024,256]{1,0:T(8,128)S(1)}, u32[]{:S(2)}, u32[]{:S(2)}) %collective-permute-start.4) | collective-permute-done | bytes 1048608 | tf_op jit(solution)/shard_map/ppermute | solution.py:121
  53.5 23.4 %collective-permute-done.5 = f32[512,256]{1,0:T(8,128)S(1)} collective-permute-done((f32[512,256]{1,0:T(8,128)S(1)}, f32[512,256]{1,0:T(8,128)S(1)}, u32[]{:S(2)}, u32[]{:S(2)}) %collective-permute-start.5) | collective-permute-done | bytes 524320 | tf_op jit(solution)/shard_map/ppermute | solution.py:125
  77.1 4.2 %fusion.67 = (f32[4,1,1024,256]{3,2,0,1:T(8,128)}, f32[4,1024,256]{2,1,0:T(8,128)}) fusion(f32[1,1024,256]{2,1,0:T(8,128)S(1)} %bitcast.89, f32[1,1024,256]{2,1,0:T(8,128)S(1)} %maximum_bitcast_fusion, f32[1,1024,256]{2,1,0:T(8,128)S(1)} %bitcast.88, f32[1,1024,256]{2,1,0:T(8,128)S(1)} %get-tuple-element.15), kind=kLoop, calls=%fused_computation.120 | loop fusion | flops 3145728 | bytes 12582912 | tf_op jit(solution)/shard_map/stack | solution.py:131
  81.3 5.7 %collective-permute-start.8 = (f32[4,1024,256]{2,1,0:T(8,128)}, f32[4,1024,256]{2,1,0:T(8,128)}, u32[]{:S(2)}, u32[]{:S(2)}) collective-permute-start(f32[4,1024,256]{2,1,0:T(8,128)} %get-tuple-element.14), channel_id=1, source_target_pairs={{0,1},{1,0},{2,3},{3,2},{4,5},{5,4},{6,7},{7,6},{8,9},{9,8},{10,11... | collective-permute-start | bytes 12582920 | tf_op jit(solution)/shard_map/ppermute | solution.py:130
  87.6 6.2 %shard_map.37 = f32[8,128,256]{2,1,0:T(8,128)} custom-call(s32[8]{0:T(128)} %stack.76.order_ref, f32[256,1024]{1,0:T(8,128)} %bitcast.90), custom_call_target="tpu_custom_call" | custom-call | tf_op jit(solution)/shard_map/pallas_call | solution.py:59
  97.6 4.1 %collective-permute-start.2 = (f32[128,512]{1,0:T(8,128)S(1)}, f32[128,512]{1,0:T(8,128)S(1)}, u32[]{:S(2)}, u32[]{:S(2)}) collective-permute-start(f32[128,512]{1,0:T(8,128)S(1)} %get-tuple-element.37), channel_id=1, source_target_pairs={{0,4},{2,6},{4,0},{6,2},{1,5},{3,7},{5,1},{7,3},{8,12},{10,14},{12... | collective-permute-start | bytes 786440 | tf_op jit(solution)/shard_map/ppermute | solution.py:150
  105.2 8.7 %collective-permute-done.2 = f32[128,512]{1,0:T(8,128)S(1)} collective-permute-done((f32[128,512]{1,0:T(8,128)S(1)}, f32[128,512]{1,0:T(8,128)S(1)}, u32[]{:S(2)}, u32[]{:S(2)}) %collective-permute-start.2) | collective-permute-done | bytes 262176 | tf_op jit(solution)/shard_map/ppermute | solution.py:150
  124.4 8.5 %shard_map.39 = bf16[1024,2048]{1,0:T(8,128)(2,1)} custom-call(s32[8]{0:T(128)} %iota.3.order_ref, f32[8,1024,256]{2,1,0:T(8,128)} %bitcast.84), custom_call_target="tpu_custom_call" | custom-call | tf_op jit(solution)/shard_map/pallas_call | solution.py:40
  139.0 4.9 %shard_map.40 = f32[4,128,1024]{2,1,0:T(8,128)} custom-call(s32[8]{0:T(128)} %stack.76.order_ref, s32[4,1024,1024]{2,1,0:T(8,128)} %l_ref.1), custom_call_target="tpu_custom_call" | custom-call | tf_op jit(solution)/shard_map/pallas_call | solution.py:96
  153.3 18.7 %collective-permute-done.10 = f32[128,2048]{1,0:T(8,128)S(1)} collective-permute-done((f32[128,2048]{1,0:T(8,128)S(1)}, f32[128,2048]{1,0:T(8,128)S(1)}, u32[]{:S(2)}, u32[]{:S(2)}) %collective-permute-start.10) | collective-permute-done | bytes 1048608 | tf_op jit(solution)/shard_map/ppermute | solution.py:165
  173.3 8.4 %shard_map.41 = bf16[1024,2048]{1,0:T(8,128)(2,1)} custom-call(s32[8]{0:T(128)} %stack.76.order_ref, f32[8,1024,256]{2,1,0:T(8,128)} %all-gather.4.cloned.1.call-done.x_ref), custom_call_target="tpu_custom_call" | custom-call | tf_op jit(solution)/shard_map/pallas_call | solution.py:40
  188.6 7.0 %collective-permute-done.11 = f32[128,1024]{1,0:T(8,128)S(1)} collective-permute-done((f32[128,1024]{1,0:T(8,128)S(1)}, f32[128,1024]{1,0:T(8,128)S(1)}, u32[]{:S(2)}, u32[]{:S(2)}) %collective-permute-start.11) | collective-permute-done | bytes 524320 | tf_op jit(solution)/shard_map/ppermute | solution.py:159
  200.5 8.5 %shard_map.42 = bf16[1024,2048]{1,0:T(8,128)(2,1)} custom-call(s32[8]{0:T(128)} %stack.76.order_ref, f32[8,1024,256]{2,1,0:T(8,128)} %all-gather.6.cloned.1.call-done.x_ref), custom_call_target="tpu_custom_call" | custom-call | tf_op jit(solution)/shard_map/pallas_call | solution.py:40
  209.0 8.4 %collective-permute-done.12 = f32[128,2048]{1,0:T(8,128)S(1)} collective-permute-done((f32[128,2048]{1,0:T(8,128)S(1)}, f32[128,2048]{1,0:T(8,128)S(1)}, u32[]{:S(2)}, u32[]{:S(2)}) %collective-permute-start.12) | collective-permute-done | bytes 1048608 | tf_op jit(solution)/shard_map/ppermute | solution.py:167
  225.0 6.6 %collective-permute-done.13 = f32[128,1024]{1,0:T(8,128)S(1)} collective-permute-done((f32[128,1024]{1,0:T(8,128)S(1)}, f32[128,1024]{1,0:T(8,128)S(1)}, u32[]{:S(2)}, u32[]{:S(2)}) %collective-permute-start.13) | collective-permute-done | bytes 524320 | tf_op jit(solution)/shard_map/ppermute | solution.py:159
  237.1 8.4 %shard_map.43 = bf16[1024,2048]{1,0:T(8,128)(2,1)} custom-call(s32[8]{0:T(128)} %stack.76.order_ref, f32[8,1024,256]{2,1,0:T(8,128)} %all-gather.8.cloned.1.call-done.x_ref), custom_call_target="tpu_custom_call" | custom-call | tf_op jit(solution)/shard_map/pallas_call | solution.py:40
  245.5 7.3 %collective-permute-done.14 = f32[128,2048]{1,0:T(8,128)S(1)} collective-permute-done((f32[128,2048]{1,0:T(8,128)S(1)}, f32[128,2048]{1,0:T(8,128)S(1)}, u32[]{:S(2)}, u32[]{:S(2)}) %collective-permute-start.14) | collective-permute-done | bytes 1048608 | tf_op jit(solution)/shard_map/ppermute | solution.py:167
  259.3 6.8 %collective-permute-done.15 = f32[128,1024]{1,0:T(8,128)S(1)} collective-permute-done((f32[128,1024]{1,0:T(8,128)S(1)}, f32[128,1024]{1,0:T(8,128)S(1)}, u32[]{:S(2)}, u32[]{:S(2)}) %collective-permute-start.15) | collective-permute-done | bytes 524320 | tf_op jit(solution)/shard_map/ppermute | solution.py:159
  270.3 17.2 %collective-permute-done.16 = f32[128,2048]{1,0:T(8,128)S(1)} collective-permute-done((f32[128,2048]{1,0:T(8,128)S(1)}, f32[128,2048]{1,0:T(8,128)S(1)}, u32[]{:S(2)}, u32[]{:S(2)}) %collective-permute-start.16) | collective-permute-done | bytes 1048608 | tf_op jit(solution)/shard_map/ppermute | solution.py:165
  288.2 6.8 %collective-permute-start.18 = (f32[128,512]{0,1:T(8,128)S(1)}, f32[128,512]{0,1:T(8,128)S(1)}, u32[]{:S(2)}, u32[]{:S(2)}) collective-permute-start(f32[128,512]{0,1:T(8,128)S(1)} %get-tuple-element.30), channel_id=1, source_target_pairs={{0,4},{2,6},{4,0},{6,2},{1,5},{3,7},{5,1},{7,3},{8,12},{10,14},{12... | collective-permute-start | bytes 786440 | tf_op jit(solution)/shard_map/ppermute | solution.py:172
  295.1 6.7 %collective-permute-done.18 = f32[128,512]{0,1:T(8,128)S(1)} collective-permute-done((f32[128,512]{0,1:T(8,128)S(1)}, f32[128,512]{0,1:T(8,128)S(1)}, u32[]{:S(2)}, u32[]{:S(2)}) %collective-permute-start.18) | collective-permute-done | bytes 262176 | tf_op jit(solution)/shard_map/ppermute | solution.py:172
  304.5 10.8 %collective-permute-start.20 = (f32[4,128,256]{1,2,0:T(8,128)S(1)}, f32[4,128,256]{1,2,0:T(8,128)S(1)}, u32[]{:S(2)}, u32[]{:S(2)}) collective-permute-start(f32[4,128,256]{1,2,0:T(8,128)S(1)} %get-tuple-element.27), channel_id=1, source_target_pairs={{0,1},{1,0},{2,3},{3,2},{4,5},{5,4},{6,7},{7,6},{8,9},{9,8},{10,11... | collective-permute-start | bytes 1572872 | tf_op jit(solution)/shard_map/ppermute | solution.py:174
  318.3 6.2 %shard_map.44 = f32[256,1024]{1,0:T(8,128)} custom-call(s32[8]{0:T(128)} %stack.76.order_ref, f32[8,128,256]{2,1,0:T(8,128)} %bitcast.86), custom_call_target="tpu_custom_call" | custom-call | tf_op jit(solution)/shard_map/pallas_call | solution.py:77
  (89 shorter events, 89.6 us)
Async XLA Ops:
  6.5 166.8 %all-gather.4.cloned.1.call-start = ((), (), s32[]{:S(2)}) async-start(), calls=%async_computation | async-start | bytes 9437184 | tf_op jit(solution)/shard_map/all_gather | solution.py:154
  14.7 185.8 %all-gather.6.cloned.1.call-start = ((), (), s32[]{:S(2)}) async-start(), calls=%async_computation.1 | async-start | bytes 9437184 | tf_op jit(solution)/shard_map/all_gather | solution.py:154
  15.5 221.6 %all-gather.8.cloned.1.call-start = ((), (), s32[]{:S(2)}) async-start(), calls=%async_computation.2 | async-start | bytes 9437184 | tf_op jit(solution)/shard_map/all_gather | solution.py:154
  15.5 34.3 %collective-permute-start.4 = (f32[1024,256]{1,0:T(8,128)S(1)}, f32[1024,256]{1,0:T(8,128)S(1)}, u32[]{:S(2)}, u32[]{:S(2)}) collective-permute-start(f32[1024,256]{1,0:T(8,128)S(1)} %get-tuple-element.16), channel_id=1, source_target_pairs={{0,2},{2,0},{4,6},{6,4},{1,3},{3,1},{5,7},{7,5},{8,10},{10,8},{12,... | collective-permute-start | bytes 3145736 | tf_op jit(solution)/shard_map/ppermute | solution.py:121
  17.7 35.6 %collective-permute-start.6 = (f32[1024,256]{1,0:T(8,128)S(1)}, f32[1024,256]{1,0:T(8,128)S(1)}, u32[]{:S(2)}, u32[]{:S(2)}) collective-permute-start(f32[1024,256]{1,0:T(8,128)S(1)} %get-tuple-element.16), channel_id=1, source_target_pairs={{0,6},{2,4},{4,2},{6,0},{1,7},{3,5},{5,3},{7,1},{8,14},{10,12},{12... | collective-permute-start | bytes 3145736 | tf_op jit(solution)/shard_map/ppermute | solution.py:122
  49.9 27.0 %collective-permute-start.5 = (f32[512,256]{1,0:T(8,128)S(1)}, f32[512,256]{1,0:T(8,128)S(1)}, u32[]{:S(2)}, u32[]{:S(2)}) collective-permute-start(f32[512,256]{1,0:T(8,128)S(1)} %slice.161), channel_id=1, source_target_pairs={{0,6},{2,4},{4,2},{6,0},{1,7},{3,5},{5,3},{7,1},{8,14},{10,12},{12... | collective-permute-start | bytes 1572872 | tf_op jit(solution)/shard_map/ppermute | solution.py:125
  53.4 23.5 %collective-permute-start.7 = (f32[512,256]{1,0:T(8,128)S(1)}, f32[512,256]{1,0:T(8,128)S(1)}, u32[]{:S(2)}, u32[]{:S(2)}) collective-permute-start(f32[512,256]{1,0:T(8,128)S(1)} %slice.162), channel_id=1, source_target_pairs={{0,2},{2,0},{4,6},{6,4},{1,3},{3,1},{5,7},{7,5},{8,10},{10,8},{12,... | collective-permute-start | bytes 1572872 | tf_op jit(solution)/shard_map/ppermute | solution.py:126
  81.3 36.0 %collective-permute-start.8 = (f32[4,1024,256]{2,1,0:T(8,128)}, f32[4,1024,256]{2,1,0:T(8,128)}, u32[]{:S(2)}, u32[]{:S(2)}) collective-permute-start(f32[4,1024,256]{2,1,0:T(8,128)} %get-tuple-element.14), channel_id=1, source_target_pairs={{0,1},{1,0},{2,3},{3,2},{4,5},{5,4},{6,7},{7,6},{8,9},{9,8},{10,11... | collective-permute-start | bytes 12582920 | tf_op jit(solution)/shard_map/ppermute | solution.py:130
  95.2 2.0 collective-permute-start
  97.3 7.8 %collective-permute-start.1 = (f32[128,512]{1,0:T(8,128)S(1)}, f32[128,512]{1,0:T(8,128)S(1)}, u32[]{:S(2)}, u32[]{:S(2)}) collective-permute-start(f32[128,512]{1,0:T(8,128)S(1)} %get-tuple-element.35), channel_id=1, source_target_pairs={{0,2},{2,0},{4,6},{6,4},{1,3},{3,1},{5,7},{7,5},{8,10},{10,8},{12,... | collective-permute-start | bytes 786440 | tf_op jit(solution)/shard_map/ppermute | solution.py:150
  97.6 16.3 %collective-permute-start.2 = (f32[128,512]{1,0:T(8,128)S(1)}, f32[128,512]{1,0:T(8,128)S(1)}, u32[]{:S(2)}, u32[]{:S(2)}) collective-permute-start(f32[128,512]{1,0:T(8,128)S(1)} %get-tuple-element.37), channel_id=1, source_target_pairs={{0,4},{2,6},{4,0},{6,2},{1,5},{3,7},{5,1},{7,3},{8,12},{10,14},{12... | collective-permute-start | bytes 786440 | tf_op jit(solution)/shard_map/ppermute | solution.py:150
  101.7 15.3 %collective-permute-start.3 = (f32[128,512]{1,0:T(8,128)S(1)}, f32[128,512]{1,0:T(8,128)S(1)}, u32[]{:S(2)}, u32[]{:S(2)}) collective-permute-start(f32[128,512]{1,0:T(8,128)S(1)} %get-tuple-element.36), channel_id=1, source_target_pairs={{0,6},{2,4},{4,2},{6,0},{1,7},{3,5},{5,3},{7,1},{8,14},{10,12},{12... | collective-permute-start | bytes 786440 | tf_op jit(solution)/shard_map/ppermute | solution.py:150
  136.4 10.9 %collective-permute-start.9 = (f32[128,1024]{1,0:T(8,128)S(1)}, f32[128,1024]{1,0:T(8,128)S(1)}, u32[]{:S(2)}, u32[]{:S(2)}) collective-permute-start(f32[128,1024]{1,0:T(8,128)S(1)} %slice_add_fusion.7), channel_id=1, source_target_pairs={{0,8},{8,0},{1,9},{9,1},{2,10},{10,2},{3,11},{11,3},{4,12},{12,4},... | collective-permute-start | bytes 1572872 | tf_op jit(solution)/shard_map/ppermute | solution.py:159
  152.3 19.8 %collective-permute-start.10 = (f32[128,2048]{1,0:T(8,128)S(1)}, f32[128,2048]{1,0:T(8,128)S(1)}, u32[]{:S(2)}, u32[]{:S(2)}) collective-permute-start(f32[128,2048]{1,0:T(8,128)S(1)} %fusion.11), channel_id=1, source_target_pairs={{0,16},{16,0},{1,17},{17,1},{2,18},{18,2},{3,19},{19,3},{4,20},{20... | collective-permute-start | bytes 3145736 | tf_op jit(solution)/shard_map/ppermute | solution.py:165
  185.7 9.8 %collective-permute-start.11 = (f32[128,1024]{1,0:T(8,128)S(1)}, f32[128,1024]{1,0:T(8,128)S(1)}, u32[]{:S(2)}, u32[]{:S(2)}) collective-permute-start(f32[128,1024]{1,0:T(8,128)S(1)} %slice_add_fusion.6), channel_id=1, source_target_pairs={{0,8},{8,0},{1,9},{9,1},{2,10},{10,2},{3,11},{11,3},{4,12},{12,4},... | collective-permute-start | bytes 1572872 | tf_op jit(solution)/shard_map/ppermute | solution.py:159
  198.5 18.9 %collective-permute-start.12 = (f32[128,2048]{1,0:T(8,128)S(1)}, f32[128,2048]{1,0:T(8,128)S(1)}, u32[]{:S(2)}, u32[]{:S(2)}) collective-permute-start(f32[128,2048]{1,0:T(8,128)S(1)} %fusion.9), channel_id=1, source_target_pairs={{0,32},{32,0},{64,96},{96,64},{1,33},{33,1},{65,97},{97,65},{2,34}... | collective-permute-start | bytes 3145736 | tf_op jit(solution)/shard_map/ppermute | solution.py:167
  221.2 10.4 %collective-permute-start.13 = (f32[128,1024]{1,0:T(8,128)S(1)}, f32[128,1024]{1,0:T(8,128)S(1)}, u32[]{:S(2)}, u32[]{:S(2)}) collective-permute-start(f32[128,1024]{1,0:T(8,128)S(1)} %slice_add_fusion.5), channel_id=1, source_target_pairs={{0,8},{8,0},{1,9},{9,1},{2,10},{10,2},{3,11},{11,3},{4,12},{12,4},... | collective-permute-start | bytes 1572872 | tf_op jit(solution)/shard_map/ppermute | solution.py:159
  234.4 18.3 %collective-permute-start.14 = (f32[128,2048]{1,0:T(8,128)S(1)}, f32[128,2048]{1,0:T(8,128)S(1)}, u32[]{:S(2)}, u32[]{:S(2)}) collective-permute-start(f32[128,2048]{1,0:T(8,128)S(1)} %fusion.7), channel_id=1, source_target_pairs={{0,64},{32,96},{64,0},{96,32},{1,65},{33,97},{65,1},{97,33},{2,66}... | collective-permute-start | bytes 3145736 | tf_op jit(solution)/shard_map/ppermute | solution.py:167
  256.5 9.6 %collective-permute-start.15 = (f32[128,1024]{1,0:T(8,128)S(1)}, f32[128,1024]{1,0:T(8,128)S(1)}, u32[]{:S(2)}, u32[]{:S(2)}) collective-permute-start(f32[128,1024]{1,0:T(8,128)S(1)} %slice_add_fusion.4), channel_id=1, source_target_pairs={{0,8},{8,0},{1,9},{9,1},{2,10},{10,2},{3,11},{11,3},{4,12},{12,4},... | collective-permute-start | bytes 1572872 | tf_op jit(solution)/shard_map/ppermute | solution.py:159
  269.0 18.6 %collective-permute-start.16 = (f32[128,2048]{1,0:T(8,128)S(1)}, f32[128,2048]{1,0:T(8,128)S(1)}, u32[]{:S(2)}, u32[]{:S(2)}) collective-permute-start(f32[128,2048]{1,0:T(8,128)S(1)} %fusion.5), channel_id=1, source_target_pairs={{0,16},{16,0},{1,17},{17,1},{2,18},{18,2},{3,19},{19,3},{4,20},{20... | collective-permute-start | bytes 3145736 | tf_op jit(solution)/shard_map/ppermute | solution.py:165
  288.1 6.9 %collective-permute-start.17 = (f32[128,512]{0,1:T(8,128)S(1)}, f32[128,512]{0,1:T(8,128)S(1)}, u32[]{:S(2)}, u32[]{:S(2)}) collective-permute-start(f32[128,512]{0,1:T(8,128)S(1)} %get-tuple-element.31), channel_id=1, source_target_pairs={{0,2},{2,0},{4,6},{6,4},{1,3},{3,1},{5,7},{7,5},{8,10},{10,8},{12,... | collective-permute-start | bytes 786440 | tf_op jit(solution)/shard_map/ppermute | solution.py:172
  288.2 13.5 %collective-permute-start.18 = (f32[128,512]{0,1:T(8,128)S(1)}, f32[128,512]{0,1:T(8,128)S(1)}, u32[]{:S(2)}, u32[]{:S(2)}) collective-permute-start(f32[128,512]{0,1:T(8,128)S(1)} %get-tuple-element.30), channel_id=1, source_target_pairs={{0,4},{2,6},{4,0},{6,2},{1,5},{3,7},{5,1},{7,3},{8,12},{10,14},{12... | collective-permute-start | bytes 786440 | tf_op jit(solution)/shard_map/ppermute | solution.py:172
  295.1 9.2 %collective-permute-start.19 = (f32[128,512]{0,1:T(8,128)S(1)}, f32[128,512]{0,1:T(8,128)S(1)}, u32[]{:S(2)}, u32[]{:S(2)}) collective-permute-start(f32[128,512]{0,1:T(8,128)S(1)} %get-tuple-element.29), channel_id=1, source_target_pairs={{0,6},{2,4},{4,2},{6,0},{1,7},{3,5},{5,3},{7,1},{8,14},{10,12},{12... | collective-permute-start | bytes 786440 | tf_op jit(solution)/shard_map/ppermute | solution.py:172
  304.5 12.4 %collective-permute-start.20 = (f32[4,128,256]{1,2,0:T(8,128)S(1)}, f32[4,128,256]{1,2,0:T(8,128)S(1)}, u32[]{:S(2)}, u32[]{:S(2)}) collective-permute-start(f32[4,128,256]{1,2,0:T(8,128)S(1)} %get-tuple-element.27), channel_id=1, source_target_pairs={{0,1},{1,0},{2,3},{3,2},{4,5},{5,4},{6,7},{7,6},{8,9},{9,8},{10,11... | collective-permute-start | bytes 1572872 | tf_op jit(solution)/shard_map/ppermute | solution.py:174
  (4 other events, 57.3 us)
Sparse Core Ops, SparseCore 0:
  14.9 79.5 all-gather.3
  96.2 56.3 all-gather.5
  154.3 50.2 all-gather.7

commit v2 on v1

v2 whole, which is shorter than its diff:
```python
import jax
import jax.numpy as jnp
import numpy as np
from jax import lax
from jax.experimental import pallas as pl
from jax.experimental.pallas import tpu as pltpu
from jax.sharding import Mesh, PartitionSpec as P

STEPS = 4
Y, CORES = 4, 2
LANES = Y * CORES
CHUNKS = 2
F32, BF16 = jnp.float32, jnp.bfloat16
VMEM_LIMIT = 48 * 2**20


def swap(x, axis, mask):
    return lax.ppermute(x, axis, [(i, i ^ mask) for i in range(lax.axis_size(axis))])


def params():
    return pltpu.CompilerParams(vmem_limit_bytes=VMEM_LIMIT)


def split(x):
    high = x.astype(BF16)
    return high, (x - high.astype(F32)).astype(BF16)


def widen(hidden):
    steps, rows, feats = hidden.shape

    def body(x_ref, o_ref):
        o_ref[...] = x_ref[...].astype(F32)

    spec = pl.BlockSpec((1, rows, feats), lambda s: (s, 0, 0))
    return pl.pallas_call(
        body,
        grid=(steps,),
        in_specs=[spec],
        out_specs=spec,
        out_shape=jax.ShapeDtypeStruct(hidden.shape, F32),
        compiler_params=params(),
    )(hidden)


def narrow(gathered, order):
    if isinstance(gathered, list):
        rows, feats = gathered[0].shape
        arrays, count = gathered, len(gathered)
    else:
        count, rows, feats = gathered.shape
        arrays = [gathered] * count
    some = rows // 4

    def body(order_ref, *refs):
        x_ref, t_ref = refs[count:]
        for k in range(count):
            block = refs[k][...].reshape(some, feats).astype(F32)
            x_ref[:, k * feats : (k + 1) * feats] = block.astype(BF16)
            t_ref[k * feats : (k + 1) * feats, :] = block.T.astype(BF16)

    if isinstance(gathered, list):
        specs = [pl.BlockSpec((some, feats), lambda i, order: (i, 0))] * count
    else:
        specs = [
            pl.BlockSpec((1, some, feats), lambda i, order, k=k: (order[k], i, 0))
            for k in range(count)
        ]
    return pl.pallas_call(
        body,
        grid_spec=pltpu.PrefetchScalarGridSpec(
            num_scalar_prefetch=1,
            grid=(rows // some,),
            in_specs=specs,
            out_specs=[
                pl.BlockSpec((some, count * feats), lambda i, order: (i, 0)),
                pl.BlockSpec((count * feats, some), lambda i, order: (0, i)),
            ],
        ),
        out_shape=[
            jax.ShapeDtypeStruct((rows, count * feats), BF16),
            jax.ShapeDtypeStruct((count * feats, rows), BF16),
        ],
        compiler_params=params(),
    )(order, *arrays)


def begin(near, far, weights):
    rows, feats = near[0].shape
    half = rows // 2
    probes = weights[0].shape[1]
    some = probes // CHUNKS
    slots = (0, 1, 2, 3, 6, 7)

    def body(*refs):
        near_refs, far_refs, w_refs = refs[:6], refs[6:10], refs[10:14]
        x_ref = refs[14]
        state_refs, margin_refs = refs[15 : 15 + CHUNKS], refs[15 + CHUNKS : 15 + 2 * CHUNKS]
        high, low = refs[-2:]

        @pl.when(pl.program_id(0) == 0)
        def _():
            for k in range(Y):
                for j in range(CORES):
                    at = slice((k * CORES + j) * feats, (k * CORES + j + 1) * feats)
                    piece = w_refs[k][j]
                    for c in range(CHUNKS):
                        state_refs[c][:, at] = piece[c * some : (c + 1) * some]
                    high[:, at], low[:, at] = split(piece)
            for j in range(CORES):
                x_ref[:, (4 + j) * feats : (5 + j) * feats] = far_refs[j][...].astype(BF16)

        @pl.when(pl.program_id(0) == 1)
        def _():
            for j in range(CORES):
                x_ref[:, (4 + j) * feats : (5 + j) * feats] = far_refs[2 + j][...].astype(BF16)

        for ref, k in zip(near_refs, slots, strict=True):
            x_ref[:, k * feats : (k + 1) * feats] = ref[...].astype(BF16)
        dims = (((1,), (1,)), ((), ()))
        x = x_ref[...]
        margin = lax.dot_general(high[...], x, dims, preferred_element_type=F32)
        margin += lax.dot_general(low[...], x, dims, preferred_element_type=F32)
        for c in range(CHUNKS):
            margin_refs[c][...] = margin[c * some : (c + 1) * some]

    wide = LANES * feats
    outs = pl.pallas_call(
        body,
        grid=(2,),
        in_specs=[pl.BlockSpec((half, feats), lambda i: (i, 0))] * 6
        + [pl.BlockSpec((half, feats), lambda i: (0, 0))] * 4
        + [pl.BlockSpec((CORES, probes, feats), lambda i: (0, 0, 0))] * 4,
        out_specs=[pl.BlockSpec((half, wide), lambda i: (i, 0))]
        + [pl.BlockSpec((some, wide), lambda i: (0, 0))] * CHUNKS
        + [pl.BlockSpec((some, half), lambda i: (0, i))] * CHUNKS,
        out_shape=[jax.ShapeDtypeStruct((rows, wide), BF16)]
        + [jax.ShapeDtypeStruct((some, wide), F32)] * CHUNKS
        + [jax.ShapeDtypeStruct((some, rows), F32)] * CHUNKS,
        scratch_shapes=[pltpu.VMEM((probes, wide), BF16)] * 2,
        compiler_params=params(),
    )(*near, *far, *weights)
    return outs[0], outs[1 : 1 + CHUNKS], outs[1 + CHUNKS :]


def weights_in(weights, order):
    feats, probes = weights.shape
    width = probes // LANES

    def body(order_ref, w_ref, own_ref, other_ref):
        for k in range(Y):
            for j, o_ref in enumerate((own_ref, other_ref)):
                start = pl.multiple_of(order_ref[k * CORES + j] * width, width)
                o_ref[k] = w_ref[:, pl.ds(start, width)].T

    shape = (Y, width, feats)
    spec = pl.BlockSpec(shape, lambda i, order: (0, 0, 0))
    return pl.pallas_call(
        body,
        grid_spec=pltpu.PrefetchScalarGridSpec(
            num_scalar_prefetch=1,
            grid=(1,),
            in_specs=[pl.BlockSpec((feats, probes), lambda i, order: (0, 0))],
            out_specs=[spec] * 2,
        ),
        out_shape=[jax.ShapeDtypeStruct(shape, F32)] * 2,
        compiler_params=params(),
    )(order, weights)


def weights_out(own, other, order):
    _, width, feats = own.shape

    def body(order_ref, own_ref, other_ref, o_ref):
        for k in range(Y):
            for j, w_ref in enumerate((own_ref, other_ref)):
                start = pl.multiple_of(order_ref[k * CORES + j] * width, width)
                o_ref[:, pl.ds(start, width)] = w_ref[k].T

    spec = pl.BlockSpec(own.shape, lambda i, order: (0, 0, 0))
    out = (feats, LANES * width)
    return pl.pallas_call(
        body,
        grid_spec=pltpu.PrefetchScalarGridSpec(
            num_scalar_prefetch=1,
            grid=(1,),
            in_specs=[spec] * 2,
            out_specs=pl.BlockSpec(out, lambda i, order: (0, 0)),
        ),
        out_shape=jax.ShapeDtypeStruct(out, F32),
        compiler_params=params(),
    )(order, own, other)


def labels_in(labels, order):
    steps, rows, probes = labels.shape
    width = probes // LANES

    def body(order_ref, l_ref, o_ref):
        o_ref[0] = l_ref[0].astype(F32).T

    return pl.pallas_call(
        body,
        grid_spec=pltpu.PrefetchScalarGridSpec(
            num_scalar_prefetch=1,
            grid=(steps,),
            in_specs=[pl.BlockSpec((1, rows, width), lambda s, order: (s, 0, order[0]))],
            out_specs=pl.BlockSpec((1, width, rows), lambda s, order: (s, 0, 0)),
        ),
        out_shape=jax.ShapeDtypeStruct((steps, width, rows), F32),
        compiler_params=params(),
    )(order, labels)


def two_pass(x, y):
    n = x.shape[0]
    high = lax.reduce_precision(x, 8, 7)
    both = jnp.concatenate([high.astype(BF16), (x - high).astype(BF16)])
    out = jnp.dot(both, y, preferred_element_type=F32)
    return out[:n] + out[n:]


def gather(x):
    half = x.shape[0] // 2
    one, three = swap(x, "y", 1), swap(x, "y", 3)
    two = [swap(one[:half], "y", 3), swap(three[half:], "y", 1)]
    return one, three, two


def after(x, *others):
    return lax.optimization_barrier((x, *others))[0]


def local(hidden, labels, weights):
    rows, feats = hidden.shape[1:]
    y, core = lax.axis_index("y"), lax.axis_index("core")
    order = jnp.arange(LANES, dtype=jnp.int32) ^ (y * CORES + core).astype(jnp.int32)

    zero = widen(hidden[:1])[0]
    one, three, two = gather(zero)
    keep, give = weights_in(weights[0], order)
    got = swap(give, "core", 1)
    pieces = jnp.stack([keep, got], axis=1)
    pieces = [pieces[0]] + [swap(pieces[k], "y", k) for k in (1, 2, 3)]

    wide = after(widen(hidden[1:]), one, three)
    later = {1: lax.all_gather(wide[0], ("y", "core"))}
    targets = labels_in(labels, order)

    near = []
    for block in (zero, one, three):
        near += [block, swap(block, "core", 1)]
    near[0] = hidden[0]
    far = []
    for block in two:
        far += [block, swap(block, "core", 1)]
    x, states, margins = begin(near, far, pieces)

    received = [swap(m, "x_hi", 1) for m in margins]
    second = after(wide[1], *received)
    one, three, two = gather(second)
    later[3] = lax.all_gather(after(wide[2], *received), ("y", "core"))

    for step in range(STEPS):
        if step in (1, 3):
            x, xt = narrow(later[step], order)
        elif step == 2:
            two = jnp.concatenate(two)
            blocks = []
            for block in (second, one, two, three):
                blocks += [block, swap(block, "core", 1)]
            blocks[0] = hidden[2]
            x, xt = narrow(blocks, order)
        if step:
            margins = [two_pass(s, xt) for s in states]
            received = [swap(m, "x_hi", 1) for m in margins]
        updates = []
        for c in range(CHUNKS):
            some = margins[c].shape[0]
            residual = jax.nn.sigmoid(margins[c] + received[c]) - targets[step, c * some : (c + 1) * some]
            updates.append(states[c] - 2.0 / rows * two_pass(residual, x))
        bit = step % 3
        partners = [swap(u, "z", bit) if bit else swap(u, "x_lo", 1) for u in updates]
        states = [0.5 * (u + p) for u, p in zip(updates, partners, strict=True)]

    deep = CORES * feats
    parts = []
    for state in states:
        parts.append(
            [state[:, :deep]] + [swap(state[:, k * deep : (k + 1) * deep], "y", k) for k in (1, 2, 3)]
        )
    blocks = jnp.stack([jnp.concatenate([part[k] for part in parts]) for k in range(Y)])
    own, give = blocks[:, :, :feats], blocks[:, :, feats:]
    return weights_out(own, swap(give, "core", 1), order)[None]


def solution(mesh):
    devices = np.asarray(mesh.devices).reshape(4, 2, 2, Y, CORES)
    fine = Mesh(devices, ("z", "x_lo", "x_hi", "y", "core"))
    rep, feat = ("z", "x_lo"), ("x_hi", "y", "core")
    in_specs = (P(None, rep, feat), P(None, rep, None), P(rep, feat, None))
    return jax.shard_map(
        local, mesh=fine, in_specs=in_specs, out_specs=P(rep, feat, None), check_vma=False
    )
```

time: 333 us -> 334 us (level)
  starting transfers between devices: 54.7 us -> 80.3 us
  Pallas kernels: 55.2 us -> 33.1 us
  waiting for transfers between devices: 158 us -> 170 us
  matrix products: 21.6 us -> 14.8 us
  other arithmetic: 15.7 us -> 8.91 us
    ppermute x21 -> x44, starting transfers between devices: 54.6 us -> 80.3 us  [swap(): lax.ppermute(x, axis, [(i, i ^ mask) for i in range(lax.axis_size(axis))])]
    pallas_call x4 -> x3, Pallas kernels: 33.8 us -> 20.9 us  [narrow(): pl.pallas_call(body, grid_spec=pltpu.PrefetchScalarGridSpec(num_scalar_pr...]
    ppermute x21 -> x44, waiting for transfers between devices: 157 us -> 170 us  [swap(): lax.ppermute(x, axis, [(i, i ^ mask) for i in range(lax.axis_size(axis))])]
    another operation x5, other arithmetic: 7.13 us -> 0.14 us  [local(): jnp.stack([jnp.concatenate([part[k] for part in parts]) for k in range(Y)])]
    dot_general x8 -> x14, matrix products: 21.6 us -> 14.8 us  [two_pass(): out = jnp.dot(both, y, preferred_element_type=F32)]
    another operation x4 -> x0, local copies, waits for them, and re-layouts: 5.92 us -> none  [the longest x1 3.83 us: gather_first(): return jnp.stack([own, other], axis=1).reshape((LANES,) + x.shape)]
    pallas_call x0 -> x1, Pallas kernels: none -> 5.58 us  [begin(): pl.pallas_call(body, grid=(2,), in_specs=[pl.BlockSpec((half, feats), lam...]
    pallas_call x1, Pallas kernels: 6.15 us -> 0.88 us  [weights_in(): pl.pallas_call(body, grid_spec=pltpu.PrefetchScalarGridSpec(num_scalar_pr...]
  transfers between devices with their start and end apart: 24 -> 46, of which waited for: 18 -> 26; matrix products, arithmetic and copies ran while one was open for 11% -> 8% of each run, Pallas kernels for 14% -> 9%
where the time goes in v2:
time: 334 us; the launch traced here: 333 us
  waiting for transfers between devices  170 us (51%)
  starting transfers between devices  80.3 us (24%)
  Pallas kernels  33.1 us (10%)
  matrix products  14.8 us (4%)
  between operations  14.2 us (4%)
  local copies, waits for them, and re-layouts  12.2 us (4%)
  other arithmetic  8.91 us (3%)
    ppermute x44, waiting for transfers between devices, swap(): lax.ppermute(x, axis, [(i, i ^ mask) for i in range(lax.axis_size(axis))])  170 us
    ppermute x44, starting transfers between devices, swap(): lax.ppermute(x, axis, [(i, i ^ mask) for i in range(lax.axis_size(axis))])  80.3 us
    pallas_call x3, Pallas kernels, narrow(): pl.pallas_call(body, grid_spec=pltpu.PrefetchScalarGridSpec(num_scalar_pr...  20.9 us
    dot_general x14, matrix products, two_pass(): out = jnp.dot(both, y, preferred_element_type=F32)  14.8 us
  transfers between devices with their start and end apart: 46, of which 26 were waited for; matrix products, arithmetic and copies ran while one was open for 8% of the time, Pallas kernels for 9%

profile of v2, /device:TPU:1, one launch (start us, length us, event | category | flops | bytes accessed | tf_op | source)
XLA Modules:
  0.0 333.1 jit_solution(1523353102287681116)
XLA Ops:
  13.3 20.2 %collective-permute-done.1.refs_2_ = f32[1024,256]{1,0:T(8,128)S(1)} collective-permute-done((f32[1024,256]{1,0:T(8,128)S(1)}, f32[1024,256]{1,0:T(8,128)S(1)}, u32[]{:S(2)}, u32[]{:S(2)}) %collective-permute-start.1) | collective-permute-done | bytes 1048608 | tf_op jit(solution)/shard_map/ppermute | solution.py:18
  50.8 8.4 %collective-permute-done.11.refs_12_ = f32[2,128,256]{2,1,0:T(8,128)S(1)} collective-permute-done((f32[2,128,256]{2,1,0:T(8,128)S(1)}, f32[2,128,256]{2,1,0:T(8,128)S(1)}, u32[]{:S(2)}, u32[]{:S(2)}) %collective-permute-start.11) | collective-permute-done | bytes 262176 | tf_op jit(solution)/shard_map/ppermute | solution.py:18
  62.8 3.7 %collective-permute-start.4 = (f32[1024,256]{1,0:T(8,128)S(1)}, f32[1024,256]{1,0:T(8,128)S(1)}, u32[]{:S(2)}, u32[]{:S(2)}) collective-permute-start(f32[1024,256]{1,0:T(8,128)S(1)} %copy-done.21), channel_id=1, source_target_pairs={{0,1},{1,0},{2,3},{3,2},{4,5},{5,4},{6,7},{7,6},{8,9},{9,8},{10,11... | collective-permute-start | bytes 3145736 | tf_op jit(solution)/shard_map/ppermute | solution.py:18
  66.5 16.4 %collective-permute-done.5.refs_6_ = f32[512,256]{1,0:T(8,128)S(1)} collective-permute-done((f32[512,256]{1,0:T(8,128)S(1)}, f32[512,256]{1,0:T(8,128)S(1)}, u32[]{:S(2)}, u32[]{:S(2)}) %collective-permute-start.5) | collective-permute-done | bytes 524320 | tf_op jit(solution)/shard_map/ppermute | solution.py:18
  82.9 4.6 %collective-permute-start.6 = (f32[512,256]{1,0:T(8,128)S(1)}, f32[512,256]{1,0:T(8,128)S(1)}, u32[]{:S(2)}, u32[]{:S(2)}) collective-permute-start(f32[512,256]{1,0:T(8,128)S(1)} %collective-permute-done.5.refs_6_), channel_id=1, source_target_pairs={{0,1},{1,0},{2,3},{3,2},{4,5},{5,4},{6,7},{7,6},{8,9},{9,8},{10,11... | collective-permute-start | bytes 1572872 | tf_op jit(solution)/shard_map/ppermute | solution.py:18
  91.2 5.6 %shard_map.39 = (bf16[1024,2048]{1,0:T(8,128)(2,1)}, f32[64,2048]{1,0:T(8,128)S(1)}, f32[64,2048]{1,0:T(8,128)S(1)}, f32[64,1024]{1,0:T(8,128)S(1)}, f32[64,1024]{1,0:T(8,128)S(1)}) custom-call(bf16[1024,256]{1,0:T(8,128)(2,1)S(1)} %get-tuple-element.65.refs_0_, f32[1024,256]{1,0:T(8,128)} %copy-done.26, f32[1024,256]{1,0:T(8,128)} %copy-done.18, ...), custom_call_target="tpu_custom_call" | custom-call | tf_op jit(solution)/shard_map/pallas_call | solution.py:129
  101.4 6.1 %collective-permute-done.13 = f32[64,1024]{1,0:T(8,128)S(1)} collective-permute-done((f32[64,1024]{1,0:T(8,128)S(1)}, f32[64,1024]{1,0:T(8,128)S(1)}, u32[]{:S(2)}, u32[]{:S(2)}) %collective-permute-start.13) | collective-permute-done | bytes 262176 | tf_op jit(solution)/shard_map/ppermute | solution.py:18
  107.5 5.6 %collective-permute-done.17 = f32[64,1024]{1,0:T(8,128)S(1)} collective-permute-done((f32[64,1024]{1,0:T(8,128)S(1)}, f32[64,1024]{1,0:T(8,128)S(1)}, u32[]{:S(2)}, u32[]{:S(2)}) %collective-permute-start.17) | collective-permute-done | bytes 262176 | tf_op jit(solution)/shard_map/ppermute | solution.py:18
  124.0 29.8 %collective-permute-done.19.refs_2_ = f32[1024,256]{1,0:T(8,128)S(1)} collective-permute-done((f32[1024,256]{1,0:T(8,128)}, f32[1024,256]{1,0:T(8,128)S(1)}, u32[]{:S(2)}, u32[]{:S(2)}) %collective-permute-start.19) | collective-permute-done | bytes 1048608 | tf_op jit(solution)/shard_map/ppermute | solution.py:18
  158.2 6.6 %collective-permute-start.20 = (f32[1024,256]{1,0:T(8,128)S(1)}, f32[1024,256]{1,0:T(8,128)}, u32[]{:S(2)}, u32[]{:S(2)}) collective-permute-start(f32[1024,256]{1,0:T(8,128)S(1)} %collective-permute-done.19.refs_2_), channel_id=1, source_target_pairs={{0,1},{1,0},{2,3},{3,2},{4,5},{5,4},{6,7},{7,6},{8,9},{9,8},{10,11... | collective-permute-start | bytes 3145736 | tf_op jit(solution)/shard_map/ppermute | solution.py:18
  164.9 14.8 %collective-permute-done.21 = f32[512,256]{1,0:T(8,128)S(1)} collective-permute-done((f32[512,256]{1,0:T(8,128)S(1)}, f32[512,256]{1,0:T(8,128)S(1)}, u32[]{:S(2)}, u32[]{:S(2)}) %collective-permute-start.21) | collective-permute-done | bytes 524320 | tf_op jit(solution)/shard_map/ppermute | solution.py:18
  181.5 6.6 %collective-permute-start.24 = (f32[1024,256]{1,0:T(8,128)}, f32[1024,256]{1,0:T(8,128)}, u32[]{:S(2)}, u32[]{:S(2)}) collective-permute-start(f32[1024,256]{1,0:T(8,128)} %constant_dynamic-update-slice_fusion.refs_4_), channel_id=1, source_target_pairs={{0,1},{1,0},{2,3},{3,2},{4,5},{5,4},{6,7},{7,6},{8,9},{9,8},{10,11... | collective-permute-start | bytes 3145736 | tf_op jit(solution)/shard_map/ppermute | solution.py:18
  188.0 6.9 %shard_map.42 = (bf16[1024,2048]{1,0:T(8,128)(2,1)S(1)}, bf16[2048,1024]{1,0:T(8,128)(2,1)}) custom-call(s32[8]{0:T(128)S(1)} %iota_xor_fusion.order_ref, f32[8,1024,256]{2,1,0:T(8,128)} %all-gather.4.cloned.1.call-done.refs_0_.refs_1_.refs_2_.refs_3_.refs_4_.refs_5_.refs_6_.refs_7_, ...), custom_call_target="tpu_custom_call" | custom-call | tf_op jit(solution)/shard_map/pallas_call | solution.py:70
  202.0 7.2 %shard_map.43 = (bf16[1024,2048]{1,0:T(8,128)(2,1)}, bf16[2048,1024]{1,0:T(8,128)(2,1)}) custom-call(s32[8]{0:T(128)S(1)} %iota_xor_fusion.order_ref, bf16[1024,256]{1,0:T(8,128)(2,1)S(1)} %copy-done, f32[1024,256]{1,0:T(8,128)} %collective-permute-done.18.refs_1_, f32[1024,256]{1,0:T(8,128)S(1)} %collective-permute-done.19.refs_2_, ...), custom_call_target="tpu_custom_call" | custom-call | tf_op jit(solution)/shard_map/pallas_call | solution.py:70
  209.2 4.0 %collective-permute-done.15 = f32[64,1024]{1,0:T(8,128)S(1)} collective-permute-done((f32[64,1024]{1,0:T(8,128)S(1)}, f32[64,1024]{1,0:T(8,128)S(1)}, u32[]{:S(2)}, u32[]{:S(2)}) %collective-permute-start.15) | collective-permute-done | bytes 262176 | tf_op jit(solution)/shard_map/ppermute | solution.py:18
  217.7 10.4 %collective-permute-done.32 = f32[64,2048]{1,0:T(8,128)S(1)} collective-permute-done((f32[64,2048]{1,0:T(8,128)S(1)}, f32[64,2048]{1,0:T(8,128)S(1)}, u32[]{:S(2)}, u32[]{:S(2)}) %collective-permute-start.32) | collective-permute-done | bytes 524320 | tf_op jit(solution)/shard_map/ppermute | solution.py:18
  231.9 7.5 %collective-permute-done.16 = f32[64,2048]{1,0:T(8,128)S(1)} collective-permute-done((f32[64,2048]{1,0:T(8,128)S(1)}, f32[64,2048]{1,0:T(8,128)S(1)}, u32[]{:S(2)}, u32[]{:S(2)}) %collective-permute-start.16) | collective-permute-done | bytes 524320 | tf_op jit(solution)/shard_map/ppermute | solution.py:18
  243.1 5.3 %collective-permute-done.26 = f32[64,1024]{1,0:T(8,128)S(1)} collective-permute-done((f32[64,1024]{1,0:T(8,128)S(1)}, f32[64,1024]{1,0:T(8,128)S(1)}, u32[]{:S(2)}, u32[]{:S(2)}) %collective-permute-start.26) | collective-permute-done | bytes 262176 | tf_op jit(solution)/shard_map/ppermute | solution.py:18
  253.8 6.9 %shard_map.44 = (bf16[1024,2048]{1,0:T(8,128)(2,1)S(1)}, bf16[2048,1024]{1,0:T(8,128)(2,1)}) custom-call(s32[8]{0:T(128)S(1)} %iota_xor_fusion.order_ref, f32[8,1024,256]{2,1,0:T(8,128)} %bitcast.89, f32[8,1024,256]{2,1,0:T(8,128)} %bitcast.90, f32[8,1024,256]{2,1,0:T(8,128)} %bitcast.91, f32[8,1024,256]{2,1,0:T(8,128)} %bitcast.92, ...), custom_call_target="tpu_custom_call" | custom-call | tf_op jit(solution)/shard_map/pallas_call | solution.py:70
  269.6 4.3 %collective-permute-done.27 = f32[64,2048]{1,0:T(8,128)} collective-permute-done((f32[64,2048]{1,0:T(8,128)S(1)}, f32[64,2048]{1,0:T(8,128)}, u32[]{:S(2)}, u32[]{:S(2)}) %collective-permute-start.27) | collective-permute-done | bytes 524320 | tf_op jit(solution)/shard_map/ppermute | solution.py:18
  278.7 4.1 %collective-permute-done.28 = f32[64,1024]{1,0:T(8,128)S(1)} collective-permute-done((f32[64,1024]{1,0:T(8,128)S(1)}, f32[64,1024]{1,0:T(8,128)S(1)}, u32[]{:S(2)}, u32[]{:S(2)}) %collective-permute-start.28) | collective-permute-done | bytes 262176 | tf_op jit(solution)/shard_map/ppermute | solution.py:18
  288.6 5.7 %collective-permute-done.29 = f32[64,2048]{1,0:T(8,128)S(1)} collective-permute-done((f32[64,2048]{1,0:T(8,128)S(1)}, f32[64,2048]{1,0:T(8,128)S(1)}, u32[]{:S(2)}, u32[]{:S(2)}) %collective-permute-start.29) | collective-permute-done | bytes 524320 | tf_op jit(solution)/shard_map/ppermute | solution.py:18
  294.6 10.8 %collective-permute-done.36 = f32[64,2048]{1,0:T(8,128)S(1)} collective-permute-done((f32[64,2048]{1,0:T(8,128)S(1)}, f32[64,2048]{1,0:T(8,128)S(1)}, u32[]{:S(2)}, u32[]{:S(2)}) %collective-permute-start.36) | collective-permute-done | bytes 524320 | tf_op jit(solution)/shard_map/ppermute | solution.py:18
  317.7 5.2 %collective-permute-start.43 = (f32[4,128,256]{2,1,0:T(8,128)S(1)}, f32[4,128,256]{2,1,0:T(8,128)S(1)}, u32[]{:S(2)}, u32[]{:S(2)}) collective-permute-start(f32[4,128,256]{2,1,0:T(8,128)S(1)} %get-tuple-element.67), channel_id=1, source_target_pairs={{0,1},{1,0},{2,3},{3,2},{4,5},{5,4},{6,7},{7,6},{8,9},{9,8},{10,11... | collective-permute-start | bytes 1572872 | tf_op jit(solution)/shard_map/ppermute | solution.py:18
  (218 shorter events, 112.4 us)
Async XLA Ops:
  6.5 181.5 %all-gather.4.cloned.1.call-start = ((), (), s32[]{:S(2)}) async-start(), calls=%async_computation | async-start | bytes 9437184 | tf_op jit(solution)/shard_map/all_gather | solution.py:248
  8.8 24.7 %collective-permute-start.1 = (f32[1024,256]{1,0:T(8,128)S(1)}, f32[1024,256]{1,0:T(8,128)S(1)}, u32[]{:S(2)}, u32[]{:S(2)}) collective-permute-start(f32[1024,256]{1,0:T(8,128)S(1)} %bitcast.84), channel_id=1, source_target_pairs={{0,2},{2,0},{4,6},{6,4},{1,3},{3,1},{5,7},{7,5},{8,10},{10,8},{12,... | collective-permute-start | bytes 3145736 | tf_op jit(solution)/shard_map/ppermute | solution.py:18
  11.1 24.9 %collective-permute-start.3 = (f32[1024,256]{1,0:T(8,128)S(1)}, f32[1024,256]{1,0:T(8,128)S(1)}, u32[]{:S(2)}, u32[]{:S(2)}) collective-permute-start(f32[1024,256]{1,0:T(8,128)S(1)} %bitcast.85), channel_id=1, source_target_pairs={{0,6},{2,4},{4,2},{6,0},{1,7},{3,5},{5,3},{7,1},{8,14},{10,12},{12... | collective-permute-start | bytes 3145736 | tf_op jit(solution)/shard_map/ppermute | solution.py:18
  37.9 215.8 %all-gather.6.cloned.1.call-start = ((), (), s32[]{:S(2)}) async-start(), calls=%async_computation.1 | async-start | bytes 9437184 | tf_op jit(solution)/shard_map/all_gather | solution.py:263
  42.5 16.6 %collective-permute-start.11 = (f32[2,128,256]{2,1,0:T(8,128)S(1)}, f32[2,128,256]{2,1,0:T(8,128)S(1)}, u32[]{:S(2)}, u32[]{:S(2)}) collective-permute-start(f32[2,128,256]{2,1,0:T(8,128)S(1)} %get-tuple-element.84), channel_id=1, source_target_pairs={{0,4},{2,6},{4,0},{6,2},{1,5},{3,7},{5,1},{7,3},{8,12},{10,14},{12... | collective-permute-start | bytes 786440 | tf_op jit(solution)/shard_map/ppermute | solution.py:18
  45.6 17.2 %collective-permute-start.12 = (f32[2,128,256]{2,1,0:T(8,128)S(1)}, f32[2,128,256]{2,1,0:T(8,128)S(1)}, u32[]{:S(2)}, u32[]{:S(2)}) collective-permute-start(f32[2,128,256]{2,1,0:T(8,128)S(1)} %get-tuple-element.81), channel_id=1, source_target_pairs={{0,6},{2,4},{4,2},{6,0},{1,7},{3,5},{5,3},{7,1},{8,14},{10,12},{12... | collective-permute-start | bytes 786440 | tf_op jit(solution)/shard_map/ppermute | solution.py:18
  46.4 41.1 %collective-permute-start = (f32[1024,256]{1,0:T(8,128)S(1)}, f32[1024,256]{1,0:T(8,128)S(1)}, u32[]{:S(2)}, u32[]{:S(2)}) collective-permute-start(f32[1024,256]{1,0:T(8,128)S(1)} %bitcast.86), channel_id=1, source_target_pairs={{0,1},{1,0},{2,3},{3,2},{4,5},{5,4},{6,7},{7,6},{8,9},{9,8},{10,11... | collective-permute-start | bytes 3145736 | tf_op jit(solution)/shard_map/ppermute | solution.py:18
  48.7 34.2 %collective-permute-start.5 = (f32[512,256]{1,0:T(8,128)S(1)}, f32[512,256]{1,0:T(8,128)S(1)}, u32[]{:S(2)}, u32[]{:S(2)}) collective-permute-start(f32[512,256]{1,0:T(8,128)S(1)} %slice.241), channel_id=1, source_target_pairs={{0,6},{2,4},{4,2},{6,0},{1,7},{3,5},{5,3},{7,1},{8,14},{10,12},{12... | collective-permute-start | bytes 1572872 | tf_op jit(solution)/shard_map/ppermute | solution.py:18
  50.7 36.8 %collective-permute-start.7 = (f32[512,256]{1,0:T(8,128)S(1)}, f32[512,256]{1,0:T(8,128)S(1)}, u32[]{:S(2)}, u32[]{:S(2)}) collective-permute-start(f32[512,256]{1,0:T(8,128)S(1)} %slice.242), channel_id=1, source_target_pairs={{0,2},{2,0},{4,6},{6,4},{1,3},{3,1},{5,7},{7,5},{8,10},{10,8},{12,... | collective-permute-start | bytes 1572872 | tf_op jit(solution)/shard_map/ppermute | solution.py:18
  59.2 30.7 %collective-permute-start.2 = (f32[1024,256]{1,0:T(8,128)S(1)}, f32[1024,256]{1,0:T(8,128)S(1)}, u32[]{:S(2)}, u32[]{:S(2)}) collective-permute-start(f32[1024,256]{1,0:T(8,128)S(1)} %copy-done.19), channel_id=1, source_target_pairs={{0,1},{1,0},{2,3},{3,2},{4,5},{5,4},{6,7},{7,6},{8,9},{9,8},{10,11... | collective-permute-start | bytes 3145736 | tf_op jit(solution)/shard_map/ppermute | solution.py:18
  62.8 27.0 %collective-permute-start.4 = (f32[1024,256]{1,0:T(8,128)S(1)}, f32[1024,256]{1,0:T(8,128)S(1)}, u32[]{:S(2)}, u32[]{:S(2)}) collective-permute-start(f32[1024,256]{1,0:T(8,128)S(1)} %copy-done.21), channel_id=1, source_target_pairs={{0,1},{1,0},{2,3},{3,2},{4,5},{5,4},{6,7},{7,6},{8,9},{9,8},{10,11... | collective-permute-start | bytes 3145736 | tf_op jit(solution)/shard_map/ppermute | solution.py:18
  117.4 36.4 %collective-permute-start.19 = (f32[1024,256]{1,0:T(8,128)}, f32[1024,256]{1,0:T(8,128)S(1)}, u32[]{:S(2)}, u32[]{:S(2)}) collective-permute-start(f32[1024,256]{1,0:T(8,128)} %get-tuple-element.30), channel_id=1, source_target_pairs={{0,2},{2,0},{4,6},{6,4},{1,3},{3,1},{5,7},{7,5},{8,10},{10,8},{12,... | collective-permute-start | bytes 3145736 | tf_op jit(solution)/shard_map/ppermute | solution.py:18
  117.5 38.2 %collective-permute-start.22 = (f32[1024,256]{1,0:T(8,128)}, f32[1024,256]{1,0:T(8,128)}, u32[]{:S(2)}, u32[]{:S(2)}) collective-permute-start(f32[1024,256]{1,0:T(8,128)} %get-tuple-element.30), channel_id=1, source_target_pairs={{0,6},{2,4},{4,2},{6,0},{1,7},{3,5},{5,3},{7,1},{8,14},{10,12},{12... | collective-permute-start | bytes 3145736 | tf_op jit(solution)/shard_map/ppermute | solution.py:18
  119.5 34.8 %collective-permute-start.30 = (f32[64,2048]{1,0:T(8,128)S(1)}, f32[64,2048]{1,0:T(8,128)S(1)}, u32[]{:S(2)}, u32[]{:S(2)}) collective-permute-start(f32[64,2048]{1,0:T(8,128)S(1)} %fusion.13), channel_id=1, source_target_pairs={{0,16},{16,0},{1,17},{17,1},{2,18},{18,2},{3,19},{19,3},{4,20},{20... | collective-permute-start | bytes 1572872 | tf_op jit(solution)/shard_map/ppermute | solution.py:18
  121.6 35.6 %collective-permute-start.14 = (f32[64,2048]{1,0:T(8,128)S(1)}, f32[64,2048]{1,0:T(8,128)S(1)}, u32[]{:S(2)}, u32[]{:S(2)}) collective-permute-start(f32[64,2048]{1,0:T(8,128)S(1)} %fusion.21), channel_id=1, source_target_pairs={{0,16},{16,0},{1,17},{17,1},{2,18},{18,2},{3,19},{19,3},{4,20},{20... | collective-permute-start | bytes 1572872 | tf_op jit(solution)/shard_map/ppermute | solution.py:18
  122.0 79.7 %collective-permute-start.18 = (f32[1024,256]{1,0:T(8,128)}, f32[1024,256]{1,0:T(8,128)}, u32[]{:S(2)}, u32[]{:S(2)}) collective-permute-start(f32[1024,256]{1,0:T(8,128)} %get-tuple-element.30), channel_id=1, source_target_pairs={{0,1},{1,0},{2,3},{3,2},{4,5},{5,4},{6,7},{7,6},{8,9},{9,8},{10,11... | collective-permute-start | bytes 3145736 | tf_op jit(solution)/shard_map/ppermute | solution.py:18
  153.8 25.9 %collective-permute-start.21 = (f32[512,256]{1,0:T(8,128)S(1)}, f32[512,256]{1,0:T(8,128)S(1)}, u32[]{:S(2)}, u32[]{:S(2)}) collective-permute-start(f32[512,256]{1,0:T(8,128)S(1)} %slice.257), channel_id=1, source_target_pairs={{0,6},{2,4},{4,2},{6,0},{1,7},{3,5},{5,3},{7,1},{8,14},{10,12},{12... | collective-permute-start | bytes 1572872 | tf_op jit(solution)/shard_map/ppermute | solution.py:18
  156.9 23.8 %collective-permute-start.23 = (f32[512,256]{1,0:T(8,128)S(1)}, f32[512,256]{1,0:T(8,128)S(1)}, u32[]{:S(2)}, u32[]{:S(2)}) collective-permute-start(f32[512,256]{1,0:T(8,128)S(1)} %slice.258), channel_id=1, source_target_pairs={{0,2},{2,0},{4,6},{6,4},{1,3},{3,1},{5,7},{7,5},{8,10},{10,8},{12,... | collective-permute-start | bytes 1572872 | tf_op jit(solution)/shard_map/ppermute | solution.py:18
  158.2 43.8 %collective-permute-start.20 = (f32[1024,256]{1,0:T(8,128)S(1)}, f32[1024,256]{1,0:T(8,128)}, u32[]{:S(2)}, u32[]{:S(2)}) collective-permute-start(f32[1024,256]{1,0:T(8,128)S(1)} %collective-permute-done.19.refs_2_), channel_id=1, source_target_pairs={{0,1},{1,0},{2,3},{3,2},{4,5},{5,4},{6,7},{7,6},{8,9},{9,8},{10,11... | collective-permute-start | bytes 3145736 | tf_op jit(solution)/shard_map/ppermute | solution.py:18
  164.8 37.2 %collective-permute-start.25 = (f32[1024,256]{1,0:T(8,128)}, f32[1024,256]{1,0:T(8,128)}, u32[]{:S(2)}, u32[]{:S(2)}) collective-permute-start(f32[1024,256]{1,0:T(8,128)} %collective-permute-done.22.refs_6_), channel_id=1, source_target_pairs={{0,1},{1,0},{2,3},{3,2},{4,5},{5,4},{6,7},{7,6},{8,9},{9,8},{10,11... | collective-permute-start | bytes 3145736 | tf_op jit(solution)/shard_map/ppermute | solution.py:18
  181.5 20.6 %collective-permute-start.24 = (f32[1024,256]{1,0:T(8,128)}, f32[1024,256]{1,0:T(8,128)}, u32[]{:S(2)}, u32[]{:S(2)}) collective-permute-start(f32[1024,256]{1,0:T(8,128)} %constant_dynamic-update-slice_fusion.refs_4_), channel_id=1, source_target_pairs={{0,1},{1,0},{2,3},{3,2},{4,5},{5,4},{6,7},{7,6},{8,9},{9,8},{10,11... | collective-permute-start | bytes 3145736 | tf_op jit(solution)/shard_map/ppermute | solution.py:18
  217.5 21.9 %collective-permute-start.16 = (f32[64,2048]{1,0:T(8,128)S(1)}, f32[64,2048]{1,0:T(8,128)S(1)}, u32[]{:S(2)}, u32[]{:S(2)}) collective-permute-start(f32[64,2048]{1,0:T(8,128)S(1)} %fusion.19), channel_id=1, source_target_pairs={{0,32},{32,0},{64,96},{96,64},{1,33},{33,1},{65,97},{97,65},{2,34}... | collective-permute-start | bytes 1572872 | tf_op jit(solution)/shard_map/ppermute | solution.py:18
  253.6 20.2 %collective-permute-start.27 = (f32[64,2048]{1,0:T(8,128)S(1)}, f32[64,2048]{1,0:T(8,128)}, u32[]{:S(2)}, u32[]{:S(2)}) collective-permute-start(f32[64,2048]{1,0:T(8,128)S(1)} %fusion.17), channel_id=1, source_target_pairs={{0,64},{32,96},{64,0},{96,32},{1,65},{33,97},{65,1},{97,33},{2,66}... | collective-permute-start | bytes 1572872 | tf_op jit(solution)/shard_map/ppermute | solution.py:18
  288.2 17.3 %collective-permute-start.36 = (f32[64,2048]{1,0:T(8,128)S(1)}, f32[64,2048]{1,0:T(8,128)S(1)}, u32[]{:S(2)}, u32[]{:S(2)}) collective-permute-start(f32[64,2048]{1,0:T(8,128)S(1)} %fusion.7), channel_id=1, source_target_pairs={{0,16},{16,0},{1,17},{17,1},{2,18},{18,2},{3,19},{19,3},{4,20},{20... | collective-permute-start | bytes 1572872 | tf_op jit(solution)/shard_map/ppermute | solution.py:18
  (58 other events, 469.0 us)
Sparse Core Ops, SparseCore 0:
  38.0 69.6 all-gather.3
  113.9 77.1 all-gather.5

commit v3 on v2

v3 whole, which is shorter than its diff:
```python
import jax
import jax.numpy as jnp
import numpy as np
from jax import lax
from jax.experimental import pallas as pl
from jax.experimental.pallas import tpu as pltpu
from jax.sharding import Mesh, PartitionSpec as P

STEPS = 4
Y, CORES = 4, 2
LANES = Y * CORES
F32, BF16 = jnp.float32, jnp.bfloat16
MIB = 2**20


def swap(x, axis, mask):
    return lax.ppermute(x, axis, [(i, i ^ mask) for i in range(lax.axis_size(axis))])


def params(mib):
    return pltpu.CompilerParams(vmem_limit_bytes=mib * MIB)


def cost(bytes_accessed, flops=0):
    return pl.CostEstimate(flops=flops, bytes_accessed=bytes_accessed, transcendentals=0)


def split(x):
    high = x.astype(BF16)
    return high, (x - high.astype(F32)).astype(BF16)


def widen(hidden, step, behind=()):
    _, rows, feats = hidden.shape

    def body(x_ref, *refs):
        refs[-1][...] = x_ref[0].astype(F32)

    return pl.pallas_call(
        body,
        grid=(2,),
        in_specs=[pl.BlockSpec((1, rows // 2, feats), lambda i: (step, i, 0))]
        + [pl.BlockSpec(memory_space=pl.ANY)] * len(behind),
        out_specs=pl.BlockSpec((rows // 2, feats), lambda i: (i, 0)),
        out_shape=jax.ShapeDtypeStruct((rows, feats), F32),
        compiler_params=params(6),
        cost_estimate=cost(6 * rows * feats),
    )(hidden, *behind)


def narrow(near, far):
    rows, feats = near[0].shape
    some, wide = rows // 4, LANES * feats
    slots = (0, 1, 2, 3, 6, 7)

    def body(*refs):
        near_refs, far_refs = refs[:6], refs[6:10]
        x_ref, t_ref = refs[10:]

        def put(k, block):
            at = slice(k * feats, (k + 1) * feats)
            x_ref[:, at] = block.astype(BF16)
            t_ref[at, :] = block.astype(F32).T.astype(BF16)

        for ref, k in zip(near_refs, slots, strict=True):
            put(k, ref[...])
        late = pl.program_id(0) >= 2
        for j in range(CORES):
            put(4 + j, jnp.where(late, far_refs[2 + j][...], far_refs[j][...]))

    return pl.pallas_call(
        body,
        grid=(rows // some,),
        in_specs=[pl.BlockSpec((some, feats), lambda i: (i, 0))] * 6
        + [pl.BlockSpec((some, feats), lambda i: (jnp.minimum(i, 1), 0))] * 2
        + [pl.BlockSpec((some, feats), lambda i: (jnp.maximum(i, 2) - 2, 0))] * 2,
        out_specs=[
            pl.BlockSpec((some, wide), lambda i: (i, 0)),
            pl.BlockSpec((wide, some), lambda i: (0, i)),
        ],
        out_shape=[
            jax.ShapeDtypeStruct((rows, wide), BF16),
            jax.ShapeDtypeStruct((wide, rows), BF16),
        ],
        compiler_params=params(14),
        cost_estimate=cost(8 * rows * wide),
    )(*near, *far)


def narrow_gathered(gathered, order):
    count, rows, feats = gathered.shape
    some = rows // 4

    def body(order_ref, *refs):
        x_ref, t_ref = refs[count:]
        for k in range(count):
            at = slice(k * feats, (k + 1) * feats)
            block = refs[k][0]
            x_ref[:, at] = block.astype(BF16)
            t_ref[at, :] = block.T.astype(BF16)

    return pl.pallas_call(
        body,
        grid_spec=pltpu.PrefetchScalarGridSpec(
            num_scalar_prefetch=1,
            grid=(rows // some,),
            in_specs=[
                pl.BlockSpec((1, some, feats), lambda i, order, k=k: (order[k], i, 0))
                for k in range(count)
            ],
            out_specs=[
                pl.BlockSpec((some, count * feats), lambda i, order: (i, 0)),
                pl.BlockSpec((count * feats, some), lambda i, order: (0, i)),
            ],
        ),
        out_shape=[
            jax.ShapeDtypeStruct((rows, count * feats), BF16),
            jax.ShapeDtypeStruct((count * feats, rows), BF16),
        ],
        compiler_params=params(14),
        cost_estimate=cost(8 * count * rows * feats),
    )(order, *[gathered] * count)


def begin(near, far, weights):
    rows, feats = near[0].shape
    half = rows // 2
    probes = weights[0].shape[1]
    wide = LANES * feats
    slots = (0, 1, 2, 3, 6, 7)

    def body(*refs):
        near_refs, far_refs, w_refs = refs[:6], refs[6:10], refs[10:14]
        x_ref, state_ref, margin_ref, high, low = refs[14:]

        @pl.when(pl.program_id(0) == 0)
        def _():
            for k in range(Y):
                for j in range(CORES):
                    at = slice((k * CORES + j) * feats, (k * CORES + j + 1) * feats)
                    piece = w_refs[k][j]
                    state_ref[:, at] = piece
                    high[:, at], low[:, at] = split(piece)
            for j in range(CORES):
                x_ref[:, (4 + j) * feats : (5 + j) * feats] = far_refs[j][...].astype(BF16)

        @pl.when(pl.program_id(0) == 1)
        def _():
            for j in range(CORES):
                x_ref[:, (4 + j) * feats : (5 + j) * feats] = far_refs[2 + j][...].astype(BF16)

        for ref, k in zip(near_refs, slots, strict=True):
            x_ref[:, k * feats : (k + 1) * feats] = ref[...].astype(BF16)
        dims = (((1,), (1,)), ((), ()))
        x = x_ref[...]
        margin = lax.dot_general(high[...], x, dims, preferred_element_type=F32)
        margin += lax.dot_general(low[...], x, dims, preferred_element_type=F32)
        margin_ref[...] = margin

    return pl.pallas_call(
        body,
        grid=(2,),
        in_specs=[pl.BlockSpec((half, feats), lambda i: (i, 0))] * 6
        + [pl.BlockSpec((half, feats), lambda i: (0, 0))] * 4
        + [pl.BlockSpec((CORES, probes, feats), lambda i: (0, 0, 0))] * 4,
        out_specs=[
            pl.BlockSpec((half, wide), lambda i: (i, 0)),
            pl.BlockSpec((probes, wide), lambda i: (0, 0)),
            pl.BlockSpec((probes, half), lambda i: (0, i)),
        ],
        out_shape=[
            jax.ShapeDtypeStruct((rows, wide), BF16),
            jax.ShapeDtypeStruct((probes, wide), F32),
            jax.ShapeDtypeStruct((probes, rows), F32),
        ],
        scratch_shapes=[pltpu.VMEM((probes, wide), BF16)] * 2,
        compiler_params=params(24),
        cost_estimate=cost(6 * rows * wide, 4 * rows * wide * probes),
    )(*near, *far, *weights)


def weights_in(weights, order):
    feats, probes = weights.shape
    width = probes // LANES

    def body(order_ref, w_ref, own_ref, other_ref):
        for k in range(Y):
            for j, o_ref in enumerate((own_ref, other_ref)):
                start = pl.multiple_of(order_ref[k * CORES + j] * width, width)
                o_ref[k] = w_ref[:, pl.ds(start, width)].T

    shape = (Y, width, feats)
    spec = pl.BlockSpec(shape, lambda i, order: (0, 0, 0))
    return pl.pallas_call(
        body,
        grid_spec=pltpu.PrefetchScalarGridSpec(
            num_scalar_prefetch=1,
            grid=(1,),
            in_specs=[pl.BlockSpec((feats, probes), lambda i, order: (0, 0))],
            out_specs=[spec] * 2,
        ),
        out_shape=[jax.ShapeDtypeStruct(shape, F32)] * 2,
        compiler_params=params(8),
    )(order, weights)


def weights_out(own, other, order):
    _, width, feats = own.shape

    def body(order_ref, own_ref, other_ref, o_ref):
        for k in range(Y):
            for j, w_ref in enumerate((own_ref, other_ref)):
                start = pl.multiple_of(order_ref[k * CORES + j] * width, width)
                o_ref[:, pl.ds(start, width)] = w_ref[k].T

    spec = pl.BlockSpec(own.shape, lambda i, order: (0, 0, 0))
    out = (feats, LANES * width)
    return pl.pallas_call(
        body,
        grid_spec=pltpu.PrefetchScalarGridSpec(
            num_scalar_prefetch=1,
            grid=(1,),
            in_specs=[spec] * 2,
            out_specs=pl.BlockSpec(out, lambda i, order: (0, 0)),
        ),
        out_shape=jax.ShapeDtypeStruct(out, F32),
        compiler_params=params(8),
    )(order, own, other)


def labels_in(labels, order):
    steps, rows, probes = labels.shape
    width = probes // LANES

    def body(order_ref, l_ref, o_ref):
        o_ref[0] = l_ref[0].astype(F32).T

    return pl.pallas_call(
        body,
        grid_spec=pltpu.PrefetchScalarGridSpec(
            num_scalar_prefetch=1,
            grid=(steps,),
            in_specs=[pl.BlockSpec((1, rows, width), lambda s, order: (s, 0, order[0]))],
            out_specs=pl.BlockSpec((1, width, rows), lambda s, order: (s, 0, 0)),
        ),
        out_shape=jax.ShapeDtypeStruct((steps, width, rows), F32),
        compiler_params=params(52),
        cost_estimate=cost(8 * steps * rows * width),
    )(order, labels)


def send_behind(x, token):
    def body(x_ref, token_ref, o_ref):
        o_ref[...] = x_ref[...]

    return pl.pallas_call(
        body,
        in_specs=[pl.BlockSpec(memory_space=pltpu.VMEM), pl.BlockSpec(memory_space=pl.ANY)],
        out_shape=jax.ShapeDtypeStruct(x.shape, x.dtype),
        compiler_params=params(4),
    )(x, token)


def two_pass(x, y):
    n = x.shape[0]
    high = lax.reduce_precision(x, 8, 7)
    both = jnp.concatenate([high.astype(BF16), (x - high).astype(BF16)])
    out = jnp.dot(both, y, preferred_element_type=F32)
    return out[:n] + out[n:]


def first_hop(x):
    return swap(x, "y", 1), swap(x, "y", 3)


def second_hop(one, three):
    half = one.shape[0] // 2
    return swap(one[:half], "y", 3), swap(three[half:], "y", 1)


def land(own, narrow_own, one, three, two):
    near = [narrow_own, swap(own, "core", 1), one, swap(one, "core", 1), three, swap(three, "core", 1)]
    far = [two[0], swap(two[0], "core", 1), two[1], swap(two[1], "core", 1)]
    return near, far


def corners(*arrays):
    return [x[:8, :128] for x in arrays]


def in_turn(x, axis):
    first, second = ([(core, 2 + core), (2 + core, core)] for core in range(CORES))
    early = lax.ppermute(x, (axis, "core"), first)
    token = lax.ppermute(early[:8, :128], "core", [(0, 1)])
    late = lax.ppermute(send_behind(x, token), (axis, "core"), second)
    return early + late


def tie(*arrays):
    return lax.optimization_barrier(arrays)


def local(hidden, labels, weights):
    rows, feats = hidden.shape[1:]
    y, core = lax.axis_index("y"), lax.axis_index("core")
    order = jnp.arange(LANES, dtype=jnp.int32) ^ (y * CORES + core).astype(jnp.int32)

    own = widen(hidden, 0)
    one, three = first_hop(own)
    keep, give = weights_in(weights[0], order)
    pieces = jnp.stack([keep, swap(give, "core", 1)], axis=1)
    pieces = [pieces[0]] + [swap(pieces[k], "y", k) for k in (1, 2, 3)]
    one, three, *pieces = tie(one, three, *pieces)
    near, far = land(own, hidden[0], one, three, second_hop(one, three))

    next_own = widen(hidden, 1)
    next_one, next_three = first_hop(next_own)
    targets = labels_in(labels, order)

    x, state, margin = begin(near, far, pieces)

    for step in range(STEPS):
        if step:
            margin = two_pass(state, xt)
        received = in_turn(margin, "x_hi") if step == 1 else swap(margin, "x_hi", 1)
        if step == 0:
            received, one, three = tie(received, next_one, next_three)
            landed = corners(received, one, three)
            later = {s: lax.all_gather(widen(hidden, s, landed), ("y", "core")) for s in (2, 3)}
        residual = jax.nn.sigmoid(margin + received) - targets[step]
        update = state - 2.0 / rows * two_pass(residual, x)
        if step + 1 == STEPS:
            break
        bit = step % 3
        partner = swap(update, "z", bit) if bit else swap(update, "x_lo", 1)
        if step == 0:
            x, xt = narrow(*land(next_own, hidden[1], one, three, second_hop(one, three)))
        else:
            x, xt = narrow_gathered(later[step + 1], order)
        state = 0.5 * (update + partner)

    deep = CORES * feats
    away, stay = update[:, deep:], update[:, :deep]
    away = 0.5 * (away + swap(away, "x_lo", 1))
    stay, away = tie(stay, away)
    blocks = [0.5 * (stay + swap(stay, "x_lo", 1))]
    blocks += [swap(away[:, (k - 1) * deep : k * deep], "y", k) for k in (1, 2, 3)]
    blocks = jnp.stack(blocks)
    own, give = blocks[:, :, :feats], blocks[:, :, feats:]
    return weights_out(own, swap(give, "core", 1), order)[None]


def solution(mesh):
    devices = np.asarray(mesh.devices).reshape(4, 2, 2, Y, CORES)
    fine = Mesh(devices, ("z", "x_lo", "x_hi", "y", "core"))
    rep, feat = ("z", "x_lo"), ("x_hi", "y", "core")
    in_specs = (P(None, rep, feat), P(None, rep, None), P(rep, feat, None))
    return jax.shard_map(
        local, mesh=fine, in_specs=in_specs, out_specs=P(rep, feat, None), check_vma=False
    )
```

time: 334 us -> 273 us (0.82)
  waiting for transfers between devices: 170 us -> 145 us
  starting transfers between devices: 80.3 us -> 55.7 us
  Pallas kernels: 33.1 us -> 22 us
  local copies, waits for them, and re-layouts: 12.2 us -> 19.4 us
  matrix products: 14.8 us -> 8.76 us
    ppermute x44 -> x34, waiting for transfers between devices: 170 us -> 121 us  [swap(): lax.ppermute(x, axis, [(i, i ^ mask) for i in range(lax.axis_size(axis))])]
    ppermute x44 -> x34, starting transfers between devices: 80.3 us -> 49 us  [swap(): lax.ppermute(x, axis, [(i, i ^ mask) for i in range(lax.axis_size(axis))])]
    ppermute x0 -> x3, waiting for transfers between devices: none -> 20.3 us  [the longest x1 13.6 us: in_turn(): token = lax.ppermute(early[:8, :128], 'core', [(0, 1)])]
    pallas_call x5 -> x8, Pallas kernels: 21.2 us -> 9.81 us  [the longest x2 5.33 us: narrow_gathered(): pl.pallas_call(body, grid_spec=pltpu.PrefetchScalarGridSpec(num_scalar_pr...]
    unnamed x73 -> x38, local copies, waits for them, and re-layouts: 4.82 us -> 16 us
    ppermute x0 -> x3, starting transfers between devices: none -> 6.63 us  [the longest x1 4.64 us: in_turn(): late = lax.ppermute(send_behind(x, token), (axis, 'core'), second)]
    dot_general x14 -> x7, matrix products: 14.8 us -> 8.76 us  [two_pass(): out = jnp.dot(both, y, preferred_element_type=F32)]
  transfers between devices with their start and end apart: 46 -> 39, of which waited for: 26 -> 23; matrix products, arithmetic and copies ran while one was open for 8% -> 5% of each run, Pallas kernels for 9% -> 7%
where the time goes in v3:
time: 273 us; the launch traced here: 272 us
  waiting for transfers between devices  145 us (53%)
  starting transfers between devices  55.7 us (20%)
  Pallas kernels  22 us (8%)
  local copies, waits for them, and re-layouts  19.4 us (7%)
  between operations  14 us (5%)
  matrix products  8.76 us (3%)
  other arithmetic  7.43 us (3%)
    ppermute x34, waiting for transfers between devices, swap(): lax.ppermute(x, axis, [(i, i ^ mask) for i in range(lax.axis_size(axis))])  121 us
    ppermute x34, starting transfers between devices, swap(): lax.ppermute(x, axis, [(i, i ^ mask) for i in range(lax.axis_size(axis))])  49 us
    unnamed x38, local copies, waits for them, and re-layouts  16 us
    ppermute x1, waiting for transfers between devices, in_turn(): token = lax.ppermute(early[:8, :128], 'core', [(0, 1)])  13.6 us
    dot_general x7, matrix products, two_pass(): out = jnp.dot(both, y, preferred_element_type=F32)  8.76 us
    ppermute x1, waiting for transfers between devices, in_turn(): late = lax.ppermute(send_behind(x, token), (axis, 'core'), second)  6.78 us
    convert_element_type x11, other arithmetic, two_pass(): both = jnp.concatenate([high.astype(BF16), (x - high).astype(BF16)])  5.8 us
  transfers between devices with their start and end apart: 39, of which 23 were waited for; matrix products, arithmetic and copies ran while one was open for 5% of the time, Pallas kernels for 7%

profile of v3, /device:TPU:1, one launch (start us, length us, event | category | flops | bytes accessed | tf_op | source)
XLA Modules:
  0.0 271.9 jit_solution(15762517286217631310)
XLA Ops:
  21.3 17.2 %collective-permute-done.4.refs_11_ = f32[2,128,256]{2,1,0:T(8,128)S(1)} collective-permute-done((f32[2,128,256]{2,1,0:T(8,128)S(1)}, f32[2,128,256]{2,1,0:T(8,128)S(1)}, u32[]{:S(2)}, u32[]{:S(2)}) %collective-permute-start.4) | collective-permute-done | bytes 262176 | tf_op jit(solution)/shard_map/ppermute | solution.py:17
  38.5 2.9 %collective-permute-start = (f32[1024,256]{1,0:T(8,128)S(1)}, f32[1024,256]{1,0:T(8,128)S(1)}, u32[]{:S(2)}, u32[]{:S(2)}) collective-permute-start(f32[1024,256]{1,0:T(8,128)S(1)} %shard_map.37), channel_id=1, source_target_pairs={{0,1},{1,0},{2,3},{3,2},{4,5},{5,4},{6,7},{7,6},{8,9},{9,8},{10,11... | collective-permute-start | bytes 3145736 | tf_op jit(solution)/shard_map/ppermute | solution.py:17
  41.4 5.4 %collective-permute-done.5.refs_12_ = f32[2,128,256]{2,1,0:T(8,128)S(1)} collective-permute-done((f32[2,128,256]{2,1,0:T(8,128)S(1)}, f32[2,128,256]{2,1,0:T(8,128)S(1)}, u32[]{:S(2)}, u32[]{:S(2)}) %collective-permute-start.5) | collective-permute-done | bytes 262176 | tf_op jit(solution)/shard_map/ppermute | solution.py:17
  53.2 7.9 %collective-permute-done.9.refs_6_ = f32[512,256]{1,0:T(8,128)S(1)} collective-permute-done((f32[512,256]{1,0:T(8,128)S(1)}, f32[512,256]{1,0:T(8,128)S(1)}, u32[]{:S(2)}, u32[]{:S(2)}) %collective-permute-start.9) | collective-permute-done | bytes 524320 | tf_op jit(solution)/shard_map/ppermute | solution.py:17
  67.6 4.7 %shard_map.39 = (bf16[1024,2048]{1,0:T(8,128)(2,1)S(1)}, f32[128,2048]{1,0:T(8,128)S(1)}, f32[128,1024]{1,0:T(8,128)S(1)}) custom-call(bf16[1024,256]{1,0:T(8,128)(2,1)S(1)} %get-tuple-element.64.refs_0_, f32[1024,256]{1,0:T(8,128)S(1)} %collective-permute-done.refs_1_, f32[1024,256]{1,0:T(8,128)} %collective-permute-done.1.refs_2_, ...), custom_call_target="tpu_custom_call" | custom-call | flops 1073741824 | bytes 12582912 | tf_op jit(solution)/shard_map/pallas_call | solution.py:160
  75.3 2.7 %collective-permute-start.13 = (f32[128,1024]{1,0:T(8,128)S(1)}, f32[128,1024]{1,0:T(8,128)S(1)}, u32[]{:S(2)}, u32[]{:S(2)}) collective-permute-start(f32[128,1024]{1,0:T(8,128)S(1)} %get-tuple-element.36), channel_id=1, source_target_pairs={{0,8},{8,0},{1,9},{9,1},{2,10},{10,2},{3,11},{11,3},{4,12},{12,4},... | collective-permute-start | bytes 1572872 | tf_op jit(solution)/shard_map/ppermute | solution.py:17
  78.1 12.1 %collective-permute-done.14.refs_2_ = f32[1024,256]{1,0:T(8,128)S(1)} collective-permute-done((f32[1024,256]{1,0:T(8,128)S(1)}, f32[1024,256]{1,0:T(8,128)S(1)}, u32[]{:S(2)}, u32[]{:S(2)}) %collective-permute-start.14) | collective-permute-done | bytes 1048608 | tf_op jit(solution)/shard_map/ppermute | solution.py:17
  95.8 4.7 %shard_map.41 = f32[4,128,1024]{2,1,0:T(8,128)} custom-call(s32[8]{0:T(128)S(1)} %iota_xor_fusion.order_ref, s32[4,1024,1024]{2,1,0:T(8,128)} %l_ref.1), custom_call_target="tpu_custom_call" | custom-call | bytes 4194304 | tf_op jit(solution)/shard_map/pallas_call | solution.py:238
  107.4 15.0 %collective-permute-done.20.refs_6_ = f32[512,256]{1,0:T(8,128)S(1)} collective-permute-done((f32[512,256]{1,0:T(8,128)S(1)}, f32[512,256]{1,0:T(8,128)S(1)}, u32[]{:S(2)}, u32[]{:S(2)}) %collective-permute-start.20) | collective-permute-done | bytes 524320 | tf_op jit(solution)/shard_map/ppermute | solution.py:17
  134.3 13.6 %collective-permute-done.25.token_ref = f32[8,128]{1,0:T(8,128)S(1)} collective-permute-done((f32[8,128]{1,0:T(8,128)S(1)}, f32[8,128]{1,0:T(8,128)S(1)}, u32[]{:S(2)}, u32[]{:S(2)}) %collective-permute-start.25) | collective-permute-done | bytes 4128 | tf_op jit(solution)/shard_map/ppermute | solution.py:294
  147.9 4.6 %collective-permute-start.26 = (f32[128,1024]{1,0:T(8,128)S(1)}, f32[128,1024]{1,0:T(8,128)S(1)}, u32[]{:S(2)}, u32[]{:S(2)}) collective-permute-start(f32[128,1024]{1,0:T(8,128)S(1)} %shard_map.43), channel_id=1, source_target_pairs={{1,9},{9,1},{3,11},{11,3},{5,13},{13,5},{7,15},{15,7},{17,25},{25,... | collective-permute-start | bytes 1572872 | tf_op jit(solution)/shard_map/ppermute | solution.py:295
  152.6 6.8 %collective-permute-done.26 = f32[128,1024]{1,0:T(8,128)S(1)} collective-permute-done((f32[128,1024]{1,0:T(8,128)S(1)}, f32[128,1024]{1,0:T(8,128)S(1)}, u32[]{:S(2)}, u32[]{:S(2)}) %collective-permute-start.26) | collective-permute-done | bytes 524320 | tf_op jit(solution)/shard_map/ppermute | solution.py:295
  164.0 13.5 %collective-permute-done.27 = f32[128,2048]{1,0:T(8,128)S(1)} collective-permute-done((f32[128,2048]{1,0:T(8,128)S(1)}, f32[128,2048]{1,0:T(8,128)S(1)}, u32[]{:S(2)}, u32[]{:S(2)}) %collective-permute-start.27) | collective-permute-done | bytes 1048608 | tf_op jit(solution)/shard_map/ppermute | solution.py:17
  177.8 3.5 %copy-done.1 = f32[8192,256]{1,0:T(8,128)S(1)} copy-done((f32[8192,256]{1,0:T(8,128)S(1)}, f32[8192,256]{1,0:T(8,128)}, u32[]{:S(2)}) %copy-start.1) | copy-done | bytes 8388632
  185.3 2.8 %collective-permute-start.28 = (f32[128,1024]{1,0:T(8,128)S(1)}, f32[128,1024]{1,0:T(8,128)S(1)}, u32[]{:S(2)}, u32[]{:S(2)}) collective-permute-start(f32[128,1024]{1,0:T(8,128)S(1)} %slice_add_fusion.5), channel_id=1, source_target_pairs={{0,8},{8,0},{1,9},{9,1},{2,10},{10,2},{3,11},{11,3},{4,12},{12,4},... | collective-permute-start | bytes 1572872 | tf_op jit(solution)/shard_map/ppermute | solution.py:17
  188.1 7.1 %collective-permute-done.28 = f32[128,1024]{1,0:T(8,128)S(1)} collective-permute-done((f32[128,1024]{1,0:T(8,128)S(1)}, f32[128,1024]{1,0:T(8,128)S(1)}, u32[]{:S(2)}, u32[]{:S(2)}) %collective-permute-start.28) | collective-permute-done | bytes 524320 | tf_op jit(solution)/shard_map/ppermute | solution.py:17
  198.1 3.5 %collective-permute-start.29 = (f32[128,2048]{1,0:T(8,128)S(1)}, f32[128,2048]{1,0:T(8,128)S(1)}, u32[]{:S(2)}, u32[]{:S(2)}) collective-permute-start(f32[128,2048]{1,0:T(8,128)S(1)} %fusion.6), channel_id=1, source_target_pairs={{0,64},{32,96},{64,0},{96,32},{1,65},{33,97},{65,1},{97,33},{2,66}... | collective-permute-start | bytes 3145736 | tf_op jit(solution)/shard_map/ppermute | solution.py:17
  201.6 2.8 %all-gather.7.cloned.1.call-done = f32[8192,256]{1,0:T(8,128)} async-done(((f32[1024,256]{1,0:T(8,128)}), f32[8192,256]{1,0:T(8,128)}) %all-gather.7.cloned.1.call-update) | async-done | bytes 8388624 | tf_op jit(solution)/shard_map/all_gather | solution.py:329
  204.4 3.4 %copy-done = f32[8192,256]{1,0:T(8,128)S(1)} copy-done((f32[8192,256]{1,0:T(8,128)S(1)}, f32[8192,256]{1,0:T(8,128)}, u32[]{:S(2)}) %copy-start) | copy-done | bytes 8388632
  210.5 5.8 %collective-permute-done.29 = f32[128,2048]{1,0:T(8,128)S(1)} collective-permute-done((f32[128,2048]{1,0:T(8,128)S(1)}, f32[128,2048]{1,0:T(8,128)S(1)}, u32[]{:S(2)}, u32[]{:S(2)}) %collective-permute-start.29) | collective-permute-done | bytes 1048608 | tf_op jit(solution)/shard_map/ppermute | solution.py:17
  217.9 2.8 %collective-permute-start.30 = (f32[128,1024]{1,0:T(8,128)S(1)}, f32[128,1024]{1,0:T(8,128)S(1)}, u32[]{:S(2)}, u32[]{:S(2)}) collective-permute-start(f32[128,1024]{1,0:T(8,128)S(1)} %slice_add_fusion.4), channel_id=1, source_target_pairs={{0,8},{8,0},{1,9},{9,1},{2,10},{10,2},{3,11},{11,3},{4,12},{12,4},... | collective-permute-start | bytes 1572872 | tf_op jit(solution)/shard_map/ppermute | solution.py:17
  220.7 7.3 %collective-permute-done.30 = f32[128,1024]{1,0:T(8,128)S(1)} collective-permute-done((f32[128,1024]{1,0:T(8,128)S(1)}, f32[128,1024]{1,0:T(8,128)S(1)}, u32[]{:S(2)}, u32[]{:S(2)}) %collective-permute-start.30) | collective-permute-done | bytes 524320 | tf_op jit(solution)/shard_map/ppermute | solution.py:17
  232.2 14.6 %collective-permute-done.31 = f32[128,1536]{1,0:T(8,128)S(1)} collective-permute-done((f32[128,1536]{1,0:T(8,128)S(1)}, f32[128,1536]{1,0:T(8,128)S(1)}, u32[]{:S(2)}, u32[]{:S(2)}) %collective-permute-start.31) | collective-permute-done | bytes 786464 | tf_op jit(solution)/shard_map/ppermute | solution.py:17
  252.6 3.6 %collective-permute-done.33 = f32[128,512]{1,0:T(8,128)S(1)} collective-permute-done((f32[128,512]{1,0:T(8,128)S(1)}, f32[128,512]{1,0:T(8,128)S(1)}, u32[]{:S(2)}, u32[]{:S(2)}) %collective-permute-start.33) | collective-permute-done | bytes 262176 | tf_op jit(solution)/shard_map/ppermute | solution.py:17
  (149 shorter events, 89.5 us)
Async XLA Ops:
  6.5 171.3 %all-gather.5.cloned.1.call-start = ((), (), s32[]{:S(2)}) async-start(), calls=%async_computation | async-start | bytes 9437184 | tf_op jit(solution)/shard_map/all_gather | solution.py:329
  8.2 38.6 %collective-permute-start.1 = (f32[1024,256]{1,0:T(8,128)S(1)}, f32[1024,256]{1,0:T(8,128)}, u32[]{:S(2)}, u32[]{:S(2)}) collective-permute-start(f32[1024,256]{1,0:T(8,128)S(1)} %shard_map.37), channel_id=1, source_target_pairs={{0,2},{2,0},{4,6},{6,4},{1,3},{3,1},{5,7},{7,5},{8,10},{10,8},{12,... | collective-permute-start | bytes 3145736 | tf_op jit(solution)/shard_map/ppermute | solution.py:17
  10.4 36.4 %collective-permute-start.2 = (f32[1024,256]{1,0:T(8,128)S(1)}, f32[1024,256]{1,0:T(8,128)}, u32[]{:S(2)}, u32[]{:S(2)}) collective-permute-start(f32[1024,256]{1,0:T(8,128)S(1)} %shard_map.37), channel_id=1, source_target_pairs={{0,6},{2,4},{4,2},{6,0},{1,7},{3,5},{5,3},{7,1},{8,14},{10,12},{12... | collective-permute-start | bytes 3145736 | tf_op jit(solution)/shard_map/ppermute | solution.py:17
  17.4 21.2 %collective-permute-start.4 = (f32[2,128,256]{2,1,0:T(8,128)S(1)}, f32[2,128,256]{2,1,0:T(8,128)S(1)}, u32[]{:S(2)}, u32[]{:S(2)}) collective-permute-start(f32[2,128,256]{2,1,0:T(8,128)S(1)} %get-tuple-element.69), channel_id=1, source_target_pairs={{0,2},{2,0},{4,6},{6,4},{1,3},{3,1},{5,7},{7,5},{8,10},{10,8},{12,... | collective-permute-start | bytes 786440 | tf_op jit(solution)/shard_map/ppermute | solution.py:17
  17.9 29.0 %collective-permute-start.5 = (f32[2,128,256]{2,1,0:T(8,128)S(1)}, f32[2,128,256]{2,1,0:T(8,128)S(1)}, u32[]{:S(2)}, u32[]{:S(2)}) collective-permute-start(f32[2,128,256]{2,1,0:T(8,128)S(1)} %get-tuple-element.70), channel_id=1, source_target_pairs={{0,4},{2,6},{4,0},{6,2},{1,5},{3,7},{5,1},{7,3},{8,12},{10,14},{12... | collective-permute-start | bytes 786440 | tf_op jit(solution)/shard_map/ppermute | solution.py:17
  19.4 27.4 %collective-permute-start.6 = (f32[2,128,256]{2,1,0:T(8,128)S(1)}, f32[2,128,256]{2,1,0:T(8,128)S(1)}, u32[]{:S(2)}, u32[]{:S(2)}) collective-permute-start(f32[2,128,256]{2,1,0:T(8,128)S(1)} %get-tuple-element.67), channel_id=1, source_target_pairs={{0,6},{2,4},{4,2},{6,0},{1,7},{3,5},{5,3},{7,1},{8,14},{10,12},{12... | collective-permute-start | bytes 786440 | tf_op jit(solution)/shard_map/ppermute | solution.py:17
  38.5 26.7 %collective-permute-start = (f32[1024,256]{1,0:T(8,128)S(1)}, f32[1024,256]{1,0:T(8,128)S(1)}, u32[]{:S(2)}, u32[]{:S(2)}) collective-permute-start(f32[1024,256]{1,0:T(8,128)S(1)} %shard_map.37), channel_id=1, source_target_pairs={{0,1},{1,0},{2,3},{3,2},{4,5},{5,4},{6,7},{7,6},{8,9},{9,8},{10,11... | collective-permute-start | bytes 3145736 | tf_op jit(solution)/shard_map/ppermute | solution.py:17
  48.0 13.1 %collective-permute-start.9 = (f32[512,256]{1,0:T(8,128)S(1)}, f32[512,256]{1,0:T(8,128)S(1)}, u32[]{:S(2)}, u32[]{:S(2)}) collective-permute-start(f32[512,256]{1,0:T(8,128)S(1)} %slice.122), channel_id=1, source_target_pairs={{0,6},{2,4},{4,2},{6,0},{1,7},{3,5},{5,3},{7,1},{8,14},{10,12},{12... | collective-permute-start | bytes 1572872 | tf_op jit(solution)/shard_map/ppermute | solution.py:17
  50.7 12.8 %collective-permute-start.11 = (f32[512,256]{1,0:T(8,128)S(1)}, f32[512,256]{1,0:T(8,128)S(1)}, u32[]{:S(2)}, u32[]{:S(2)}) collective-permute-start(f32[512,256]{1,0:T(8,128)S(1)} %slice.123), channel_id=1, source_target_pairs={{0,2},{2,0},{4,6},{6,4},{1,3},{3,1},{5,7},{7,5},{8,10},{10,8},{12,... | collective-permute-start | bytes 1572872 | tf_op jit(solution)/shard_map/ppermute | solution.py:17
  50.8 16.8 %collective-permute-start.7 = (f32[1024,256]{1,0:T(8,128)}, f32[1024,256]{1,0:T(8,128)S(1)}, u32[]{:S(2)}, u32[]{:S(2)}) collective-permute-start(f32[1024,256]{1,0:T(8,128)} %collective-permute-done.1.refs_2_), channel_id=1, source_target_pairs={{0,1},{1,0},{2,3},{3,2},{4,5},{5,4},{6,7},{7,6},{8,9},{9,8},{10,11... | collective-permute-start | bytes 3145736 | tf_op jit(solution)/shard_map/ppermute | solution.py:17
  53.1 14.6 %collective-permute-start.8 = (f32[1024,256]{1,0:T(8,128)}, f32[1024,256]{1,0:T(8,128)S(1)}, u32[]{:S(2)}, u32[]{:S(2)}) collective-permute-start(f32[1024,256]{1,0:T(8,128)} %collective-permute-done.2.refs_4_), channel_id=1, source_target_pairs={{0,1},{1,0},{2,3},{3,2},{4,5},{5,4},{6,7},{7,6},{8,9},{9,8},{10,11... | collective-permute-start | bytes 3145736 | tf_op jit(solution)/shard_map/ppermute | solution.py:17
  65.3 24.9 %collective-permute-start.14 = (f32[1024,256]{1,0:T(8,128)S(1)}, f32[1024,256]{1,0:T(8,128)S(1)}, u32[]{:S(2)}, u32[]{:S(2)}) collective-permute-start(f32[1024,256]{1,0:T(8,128)S(1)} %shard_map.40), channel_id=1, source_target_pairs={{0,2},{2,0},{4,6},{6,4},{1,3},{3,1},{5,7},{7,5},{8,10},{10,8},{12,... | collective-permute-start | bytes 3145736 | tf_op jit(solution)/shard_map/ppermute | solution.py:17
  65.4 25.9 %collective-permute-start.15 = (f32[1024,256]{1,0:T(8,128)S(1)}, f32[1024,256]{1,0:T(8,128)S(1)}, u32[]{:S(2)}, u32[]{:S(2)}) collective-permute-start(f32[1024,256]{1,0:T(8,128)S(1)} %shard_map.40), channel_id=1, source_target_pairs={{0,6},{2,4},{4,2},{6,0},{1,7},{3,5},{5,3},{7,1},{8,14},{10,12},{12... | collective-permute-start | bytes 3145736 | tf_op jit(solution)/shard_map/ppermute | solution.py:17
  75.3 15.9 %collective-permute-start.13 = (f32[128,1024]{1,0:T(8,128)S(1)}, f32[128,1024]{1,0:T(8,128)S(1)}, u32[]{:S(2)}, u32[]{:S(2)}) collective-permute-start(f32[128,1024]{1,0:T(8,128)S(1)} %get-tuple-element.36), channel_id=1, source_target_pairs={{0,8},{8,0},{1,9},{9,1},{2,10},{10,2},{3,11},{11,3},{4,12},{12,4},... | collective-permute-start | bytes 1572872 | tf_op jit(solution)/shard_map/ppermute | solution.py:17
  93.5 110.9 %all-gather.7.cloned.1.call-start = ((), (), s32[]{:S(2)}) async-start(), calls=%async_computation.1 | async-start | bytes 9437184 | tf_op jit(solution)/shard_map/all_gather | solution.py:329
  100.5 26.5 %collective-permute-start.18 = (f32[1024,256]{1,0:T(8,128)S(1)}, f32[1024,256]{1,0:T(8,128)S(1)}, u32[]{:S(2)}, u32[]{:S(2)}) collective-permute-start(f32[1024,256]{1,0:T(8,128)S(1)} %collective-permute-done.14.refs_2_), channel_id=1, source_target_pairs={{0,1},{1,0},{2,3},{3,2},{4,5},{5,4},{6,7},{7,6},{8,9},{9,8},{10,11... | collective-permute-start | bytes 3145736 | tf_op jit(solution)/shard_map/ppermute | solution.py:17
  100.6 26.4 %collective-permute-start.19 = (f32[1024,256]{1,0:T(8,128)S(1)}, f32[1024,256]{1,0:T(8,128)S(1)}, u32[]{:S(2)}, u32[]{:S(2)}) collective-permute-start(f32[1024,256]{1,0:T(8,128)S(1)} %copy-done.5), channel_id=1, source_target_pairs={{0,1},{1,0},{2,3},{3,2},{4,5},{5,4},{6,7},{7,6},{8,9},{9,8},{10,11... | collective-permute-start | bytes 3145736 | tf_op jit(solution)/shard_map/ppermute | solution.py:17
  101.1 21.3 %collective-permute-start.20 = (f32[512,256]{1,0:T(8,128)S(1)}, f32[512,256]{1,0:T(8,128)S(1)}, u32[]{:S(2)}, u32[]{:S(2)}) collective-permute-start(f32[512,256]{1,0:T(8,128)S(1)} %slice.128), channel_id=1, source_target_pairs={{0,6},{2,4},{4,2},{6,0},{1,7},{3,5},{5,3},{7,1},{8,14},{10,12},{12... | collective-permute-start | bytes 1572872 | tf_op jit(solution)/shard_map/ppermute | solution.py:17
  102.4 21.7 %collective-permute-start.22 = (f32[512,256]{1,0:T(8,128)S(1)}, f32[512,256]{1,0:T(8,128)S(1)}, u32[]{:S(2)}, u32[]{:S(2)}) collective-permute-start(f32[512,256]{1,0:T(8,128)S(1)} %slice.129), channel_id=1, source_target_pairs={{0,2},{2,0},{4,6},{6,4},{1,3},{3,1},{5,7},{7,5},{8,10},{10,8},{12,... | collective-permute-start | bytes 1572872 | tf_op jit(solution)/shard_map/ppermute | solution.py:17
  106.2 24.5 %collective-permute-start.16 = (f32[128,2048]{1,0:T(8,128)S(1)}, f32[128,2048]{1,0:T(8,128)S(1)}, u32[]{:S(2)}, u32[]{:S(2)}) collective-permute-start(f32[128,2048]{1,0:T(8,128)S(1)} %fusion.10), channel_id=1, source_target_pairs={{0,16},{16,0},{1,17},{17,1},{2,18},{18,2},{3,19},{19,3},{4,20},{20... | collective-permute-start | bytes 3145736 | tf_op jit(solution)/shard_map/ppermute | solution.py:17
  133.0 14.9 %collective-permute-start.25 = (f32[8,128]{1,0:T(8,128)S(1)}, f32[8,128]{1,0:T(8,128)S(1)}, u32[]{:S(2)}, u32[]{:S(2)}) collective-permute-start(f32[8,128]{1,0:T(8,128)S(1)} %slice.167), channel_id=1, source_target_pairs={{0,1},{2,3},{4,5},{6,7},{8,9},{10,11},{12,13},{14,15},{16,17},{18,... | collective-permute-start | bytes 12296 | tf_op jit(solution)/shard_map/ppermute | solution.py:294
  162.3 15.3 %collective-permute-start.27 = (f32[128,2048]{1,0:T(8,128)S(1)}, f32[128,2048]{1,0:T(8,128)S(1)}, u32[]{:S(2)}, u32[]{:S(2)}) collective-permute-start(f32[128,2048]{1,0:T(8,128)S(1)} %fusion.8), channel_id=1, source_target_pairs={{0,32},{32,0},{64,96},{96,64},{1,33},{33,1},{65,97},{97,65},{2,34}... | collective-permute-start | bytes 3145736 | tf_op jit(solution)/shard_map/ppermute | solution.py:17
  198.1 18.2 %collective-permute-start.29 = (f32[128,2048]{1,0:T(8,128)S(1)}, f32[128,2048]{1,0:T(8,128)S(1)}, u32[]{:S(2)}, u32[]{:S(2)}) collective-permute-start(f32[128,2048]{1,0:T(8,128)S(1)} %fusion.6), channel_id=1, source_target_pairs={{0,64},{32,96},{64,0},{96,32},{1,65},{33,97},{65,1},{97,33},{2,66}... | collective-permute-start | bytes 3145736 | tf_op jit(solution)/shard_map/ppermute | solution.py:17
  230.9 15.9 %collective-permute-start.31 = (f32[128,1536]{1,0:T(8,128)S(1)}, f32[128,1536]{1,0:T(8,128)S(1)}, u32[]{:S(2)}, u32[]{:S(2)}) collective-permute-start(f32[128,1536]{1,0:T(8,128)S(1)} %slice.182), channel_id=1, source_target_pairs={{0,16},{16,0},{1,17},{17,1},{2,18},{18,2},{3,19},{19,3},{4,20},{20... | collective-permute-start | bytes 2359304 | tf_op jit(solution)/shard_map/ppermute | solution.py:17
  (34 other events, 242.3 us)
Sparse Core Ops, SparseCore 0:
  93.7 58.2 all-gather.4
  153.7 50.6 all-gather.6

commit v4 on v3

--- a/solution.py
+++ b/solution.py
@@ -17,6 +17,10 @@
     return lax.ppermute(x, axis, [(i, i ^ mask) for i in range(lax.axis_size(axis))])
 
 
+def swap_both(x, mask):
+    return lax.ppermute(x, ("x_lo", "y"), [(i, i ^ (Y + mask)) for i in range(2 * Y)])
+
+
 def params(mib):
     return pltpu.CompilerParams(vmem_limit_bytes=mib * MIB)
 
@@ -30,22 +34,21 @@
     return high, (x - high.astype(F32)).astype(BF16)
 
 
-def widen(hidden, step, behind=()):
+def widen(hidden, step):
     _, rows, feats = hidden.shape
 
-    def body(x_ref, *refs):
-        refs[-1][...] = x_ref[0].astype(F32)
+    def body(x_ref, o_ref):
+        o_ref[...] = x_ref[0].astype(F32)
 
     return pl.pallas_call(
         body,
         grid=(2,),
-        in_specs=[pl.BlockSpec((1, rows // 2, feats), lambda i: (step, i, 0))]
-        + [pl.BlockSpec(memory_space=pl.ANY)] * len(behind),
+        in_specs=[pl.BlockSpec((1, rows // 2, feats), lambda i: (step, i, 0))],
         out_specs=pl.BlockSpec((rows // 2, feats), lambda i: (i, 0)),
         out_shape=jax.ShapeDtypeStruct((rows, feats), F32),
         compiler_params=params(6),
         cost_estimate=cost(6 * rows * feats),
-    )(hidden, *behind)
+    )(hidden)
 
 
 def narrow(near, far):
@@ -122,16 +125,49 @@
     )(order, *[gathered] * count)
 
 
+SLOTS = (0, 1, 2, 3, 6, 7)
+
+
+def place(near_refs, far_refs, x_ref):
+    feats = near_refs[0].shape[1]
+    for ref, k in zip(near_refs, SLOTS, strict=True):
+        x_ref[:, k * feats : (k + 1) * feats] = ref[...].astype(BF16)
+    for half in range(2):
+
+        @pl.when(pl.program_id(0) == half)
+        def _(half=half):
+            for j in range(CORES):
+                at = slice((4 + j) * feats, (5 + j) * feats)
+                x_ref[:, at] = far_refs[2 * half + j][...].astype(BF16)
+
+
+def collect(near, far):
+    rows, feats = near[0].shape
+    half, wide = rows // 2, LANES * feats
+
+    def body(*refs):
+        place(refs[:6], refs[6:10], refs[10])
+
+    return pl.pallas_call(
+        body,
+        grid=(2,),
+        in_specs=[pl.BlockSpec((half, feats), lambda i: (i, 0))] * 6
+        + [pl.BlockSpec((half, feats), lambda i: (0, 0))] * 4,
+        out_specs=pl.BlockSpec((half, wide), lambda i: (i, 0)),
+        out_shape=jax.ShapeDtypeStruct((rows, wide), BF16),
+        compiler_params=params(16),
+    )(*near, *far)
+
+
 def begin(near, far, weights):
     rows, feats = near[0].shape
     half = rows // 2
     probes = weights[0].shape[1]
     wide = LANES * feats
-    slots = (0, 1, 2, 3, 6, 7)
 
     def body(*refs):
         near_refs, far_refs, w_refs = refs[:6], refs[6:10], refs[10:14]
-        x_ref, state_ref, margin_ref, high, low = refs[14:]
+        state_ref, margin_ref, x_ref, high, low = refs[14:]
 
         @pl.when(pl.program_id(0) == 0)
         def _():
@@ -141,16 +177,8 @@
                     piece = w_refs[k][j]
                     state_ref[:, at] = piece
                     high[:, at], low[:, at] = split(piece)
-            for j in range(CORES):
-                x_ref[:, (4 + j) * feats : (5 + j) * feats] = far_refs[j][...].astype(BF16)
-
-        @pl.when(pl.program_id(0) == 1)
-        def _():
-            for j in range(CORES):
-                x_ref[:, (4 + j) * feats : (5 + j) * feats] = far_refs[2 + j][...].astype(BF16)
-
-        for ref, k in zip(near_refs, slots, strict=True):
-            x_ref[:, k * feats : (k + 1) * feats] = ref[...].astype(BF16)
+
+        place(near_refs, far_refs, x_ref)
         dims = (((1,), (1,)), ((), ()))
         x = x_ref[...]
         margin = lax.dot_general(high[...], x, dims, preferred_element_type=F32)
@@ -164,18 +192,15 @@
         + [pl.BlockSpec((half, feats), lambda i: (0, 0))] * 4
         + [pl.BlockSpec((CORES, probes, feats), lambda i: (0, 0, 0))] * 4,
         out_specs=[
-            pl.BlockSpec((half, wide), lambda i: (i, 0)),
             pl.BlockSpec((probes, wide), lambda i: (0, 0)),
             pl.BlockSpec((probes, half), lambda i: (0, i)),
         ],
         out_shape=[
-            jax.ShapeDtypeStruct((rows, wide), BF16),
             jax.ShapeDtypeStruct((probes, wide), F32),
             jax.ShapeDtypeStruct((probes, rows), F32),
         ],
-        scratch_shapes=[pltpu.VMEM((probes, wide), BF16)] * 2,
-        compiler_params=params(24),
-        cost_estimate=cost(6 * rows * wide, 4 * rows * wide * probes),
+        scratch_shapes=[pltpu.VMEM((half, wide), BF16)] + [pltpu.VMEM((probes, wide), BF16)] * 2,
+        compiler_params=params(20),
     )(*near, *far, *weights)
 
 
@@ -284,10 +309,6 @@
     return near, far
 
 
-def corners(*arrays):
-    return [x[:8, :128] for x in arrays]
-
-
 def in_turn(x, axis):
     first, second = ([(core, 2 + core), (2 + core, core)] for core in range(CORES))
     early = lax.ppermute(x, (axis, "core"), first)
@@ -310,23 +331,24 @@
     keep, give = weights_in(weights[0], order)
     pieces = jnp.stack([keep, swap(give, "core", 1)], axis=1)
     pieces = [pieces[0]] + [swap(pieces[k], "y", k) for k in (1, 2, 3)]
-    one, three, *pieces = tie(one, three, *pieces)
+    targets = labels_in(labels, order)
+    one, three, targets, *pieces = tie(one, three, targets, *pieces)
     near, far = land(own, hidden[0], one, three, second_hop(one, three))
 
     next_own = widen(hidden, 1)
     next_one, next_three = first_hop(next_own)
-    targets = labels_in(labels, order)
-
-    x, state, margin = begin(near, far, pieces)
+    wides = [widen(hidden, s) for s in (2, 3)]
+
+    state, margin = begin(near, far, pieces)
+    x = collect(near, far)
 
     for step in range(STEPS):
         if step:
             margin = two_pass(state, xt)
         received = in_turn(margin, "x_hi") if step == 1 else swap(margin, "x_hi", 1)
         if step == 0:
-            received, one, three = tie(received, next_one, next_three)
-            landed = corners(received, one, three)
-            later = {s: lax.all_gather(widen(hidden, s, landed), ("y", "core")) for s in (2, 3)}
+            received, x, one, three, *wides = tie(received, x, next_one, next_three, *wides)
+            later = {s: lax.all_gather(wide, ("y", "core")) for s, wide in zip((2, 3), wides, strict=True)}
         residual = jax.nn.sigmoid(margin + received) - targets[step]
         update = state - 2.0 / rows * two_pass(residual, x)
         if step + 1 == STEPS:
@@ -337,15 +359,15 @@
             x, xt = narrow(*land(next_own, hidden[1], one, three, second_hop(one, three)))
         else:
             x, xt = narrow_gathered(later[step + 1], order)
+            partner, x, xt = tie(partner, x, xt)
         state = 0.5 * (update + partner)
 
     deep = CORES * feats
-    away, stay = update[:, deep:], update[:, :deep]
-    away = 0.5 * (away + swap(away, "x_lo", 1))
-    stay, away = tie(stay, away)
-    blocks = [0.5 * (stay + swap(stay, "x_lo", 1))]
-    blocks += [swap(away[:, (k - 1) * deep : k * deep], "y", k) for k in (1, 2, 3)]
-    blocks = jnp.stack(blocks)
+    pieces = [update[:, k * deep : (k + 1) * deep] for k in range(Y)]
+    landed = tie(*[swap_both(pieces[k], k) for k in (2, 1, 3, 0)], *[swap(pieces[k], "y", k) for k in (2, 1, 3)])
+    mine = (*landed[4:], pieces[0])
+    two, one, three, zero = (0.5 * (a + b) for a, b in zip(mine, landed[:4], strict=True))
+    blocks = jnp.stack([zero, one, two, three])
     own, give = blocks[:, :, :feats], blocks[:, :, feats:]
     return weights_out(own, swap(give, "core", 1), order)[None]
 

time: 273 us -> 270 us (0.989)
  waiting for transfers between devices: 145 us -> 126 us
  local copies, waits for them, and re-layouts: 19.4 us -> 27.3 us
  Pallas kernels: 22 us -> 28.4 us
    ppermute x34 -> x32, waiting for transfers between devices: 121 us -> 77.2 us  [swap(): lax.ppermute(x, axis, [(i, i ^ mask) for i in range(lax.axis_size(axis))])]
    ppermute x0 -> x4, waiting for transfers between devices: none -> 16.8 us  [swap_both(): lax.ppermute(x, ('x_lo', 'y'), [(i, i ^ Y + mask) for i in range(2 * Y)])]
    all_gather x2, waiting for transfers between devices: 2.82 us -> 9.69 us  [local(): lax.all_gather(wide, ('y', 'core'))]
    unnamed x38 -> x54, local copies, waits for them, and re-layouts: 16 us -> 22.6 us
    ppermute x0 -> x4, starting transfers between devices: none -> 5.29 us  [swap_both(): lax.ppermute(x, ('x_lo', 'y'), [(i, i ^ Y + mask) for i in range(2 * Y)])]
    ppermute x34 -> x32, starting transfers between devices: 49 us -> 46.4 us  [swap(): lax.ppermute(x, axis, [(i, i ^ mask) for i in range(lax.axis_size(axis))])]
  transfers between devices with their start and end apart: 39 -> 41, of which waited for: 23 -> 20; matrix products, arithmetic and copies ran while one was open for 5% -> 6% of each run, Pallas kernels for 7% -> 10%
where the time goes in v4:
time: 270 us; the launch traced here: 269 us
  waiting for transfers between devices  126 us (47%)
  starting transfers between devices  57.1 us (21%)
  Pallas kernels  28.4 us (11%)
  local copies, waits for them, and re-layouts  27.3 us (10%)
  between operations  14 us (5%)
  matrix products  8.93 us (3%)
  other arithmetic  6.64 us (2%)
    ppermute x32, waiting for transfers between devices, swap(): lax.ppermute(x, axis, [(i, i ^ mask) for i in range(lax.axis_size(axis))])  77.2 us
    ppermute x32, starting transfers between devices, swap(): lax.ppermute(x, axis, [(i, i ^ mask) for i in range(lax.axis_size(axis))])  46.4 us
    unnamed x54, local copies, waits for them, and re-layouts  22.6 us
    ppermute x4, waiting for transfers between devices, swap_both(): lax.ppermute(x, ('x_lo', 'y'), [(i, i ^ Y + mask) for i in range(2 * Y)])  16.8 us
    ppermute x1, waiting for transfers between devices, in_turn(): token = lax.ppermute(early[:8, :128], 'core', [(0, 1)])  13.9 us
    all_gather x2, waiting for transfers between devices, local(): lax.all_gather(wide, ('y', 'core'))  9.69 us
    dot_general x7, matrix products, two_pass(): out = jnp.dot(both, y, preferred_element_type=F32)  8.93 us
    ppermute x1, waiting for transfers between devices, in_turn(): late = lax.ppermute(send_behind(x, token), (axis, 'core'), second)  8.03 us
  transfers between devices with their start and end apart: 41, of which 20 were waited for; matrix products, arithmetic and copies ran while one was open for 6% of the time, Pallas kernels for 10%

profile of v4, /device:TPU:1, one launch (start us, length us, event | category | flops | bytes accessed | tf_op | source)
XLA Modules:
  0.0 268.7 jit_solution(12201410331981820593)
XLA Ops:
  22.1 4.7 %shard_map.38 = f32[4,128,1024]{2,1,0:T(8,128)} custom-call(s32[8]{0:T(128)S(1)} %iota_xor_fusion.order_ref, s32[4,1024,1024]{2,1,0:T(8,128)} %l_ref.1), custom_call_target="tpu_custom_call" | custom-call | bytes 4194304 | tf_op jit(solution)/shard_map/pallas_call | solution.py:263
  26.8 12.7 %collective-permute-done.4.refs_11_ = f32[2,128,256]{2,1,0:T(8,128)S(1)} collective-permute-done((f32[2,128,256]{2,1,0:T(8,128)S(1)}, f32[2,128,256]{2,1,0:T(8,128)S(1)}, u32[]{:S(2)}, u32[]{:S(2)}) %collective-permute-start.4) | collective-permute-done | bytes 262176 | tf_op jit(solution)/shard_map/ppermute | solution.py:17
  39.6 2.9 %collective-permute-start = (f32[1024,256]{1,0:T(8,128)}, f32[1024,256]{1,0:T(8,128)S(1)}, u32[]{:S(2)}, u32[]{:S(2)}) collective-permute-start(f32[1024,256]{1,0:T(8,128)} %shard_map.37), channel_id=1, source_target_pairs={{0,1},{1,0},{2,3},{3,2},{4,5},{5,4},{6,7},{7,6},{8,9},{9,8},{10,11... | collective-permute-start | bytes 3145736 | tf_op jit(solution)/shard_map/ppermute | solution.py:17
  42.4 5.4 %collective-permute-done.5.refs_12_ = f32[2,128,256]{2,1,0:T(8,128)S(1)} collective-permute-done((f32[2,128,256]{2,1,0:T(8,128)S(1)}, f32[2,128,256]{2,1,0:T(8,128)S(1)}, u32[]{:S(2)}, u32[]{:S(2)}) %collective-permute-start.5) | collective-permute-done | bytes 262176 | tf_op jit(solution)/shard_map/ppermute | solution.py:17
  53.1 7.9 %collective-permute-done.9.refs_6_ = f32[512,256]{1,0:T(8,128)S(1)} collective-permute-done((f32[512,256]{1,0:T(8,128)S(1)}, f32[512,256]{1,0:T(8,128)S(1)}, u32[]{:S(2)}, u32[]{:S(2)}) %collective-permute-start.9) | collective-permute-done | bytes 524320 | tf_op jit(solution)/shard_map/ppermute | solution.py:17
  68.4 6.1 %shard_map.40 = (f32[128,2048]{1,0:T(8,128)S(1)}, f32[128,1024]{1,0:T(8,128)}) custom-call(bf16[1024,256]{1,0:T(8,128)(2,1)S(1)} %get-tuple-element.91.refs_0_, f32[1024,256]{1,0:T(8,128)S(1)} %collective-permute-done.refs_1_, f32[1024,256]{1,0:T(8,128)S(1)} %collective-permute-done.1.refs_2_, f32[1024,256]{1,0:T(8,128)S(1)} %collective-permute-done.7.refs_3_, ...), custom_call_target="tpu_custom_call" | custom-call | tf_op jit(solution)/shard_map/pallas_call | solution.py:188
  75.5 2.7 %collective-permute-start.13 = (f32[128,1024]{1,0:T(8,128)}, f32[128,1024]{1,0:T(8,128)}, u32[]{:S(2)}, u32[]{:S(2)}) collective-permute-start(f32[128,1024]{1,0:T(8,128)} %get-tuple-element.50), channel_id=1, source_target_pairs={{0,8},{8,0},{1,9},{9,1},{2,10},{10,2},{3,11},{11,3},{4,12},{12,4},... | collective-permute-start | bytes 1572872 | tf_op jit(solution)/shard_map/ppermute | solution.py:17
  102.9 13.9 %collective-permute-done.20.refs_6_ = f32[512,256]{1,0:T(8,128)S(1)} collective-permute-done((f32[512,256]{1,0:T(8,128)S(1)}, f32[512,256]{1,0:T(8,128)S(1)}, u32[]{:S(2)}, u32[]{:S(2)}) %collective-permute-start.20) | collective-permute-done | bytes 524320 | tf_op jit(solution)/shard_map/ppermute | solution.py:17
  121.9 3.7 %shard_map.45 = (bf16[1024,2048]{1,0:T(8,128)(2,1)S(1)}, bf16[2048,1024]{1,0:T(8,128)(2,1)S(1)}) custom-call(bf16[1024,256]{1,0:T(8,128)(2,1)S(1)} %copy-done.22, f32[1024,256]{1,0:T(8,128)S(1)} %collective-permute-done.17.refs_1_, f32[1024,256]{1,0:T(8,128)} %collective-permute-done.14.refs_2_, f32[1024,256]{1,0:T(8,128)S(1)} %collective-permute-done.18.refs_3_, ...), custom_call_target="tpu_custom_call" | custom-call | bytes 16777216 | tf_op jit(solution)/shard_map/pallas_call | solution.py:74
  130.4 13.9 %collective-permute-done.25.token_ref = f32[8,128]{1,0:T(8,128)S(1)} collective-permute-done((f32[8,128]{1,0:T(8,128)S(1)}, f32[8,128]{1,0:T(8,128)S(1)}, u32[]{:S(2)}, u32[]{:S(2)}) %collective-permute-start.25) | collective-permute-done | bytes 4128 | tf_op jit(solution)/shard_map/ppermute | solution.py:315
  144.3 3.4 %collective-permute-start.26 = (f32[128,1024]{1,0:T(8,128)S(1)}, f32[128,1024]{1,0:T(8,128)S(1)}, u32[]{:S(2)}, u32[]{:S(2)}) collective-permute-start(f32[128,1024]{1,0:T(8,128)S(1)} %shard_map.46), channel_id=1, source_target_pairs={{1,9},{9,1},{3,11},{11,3},{5,13},{13,5},{7,15},{15,7},{17,25},{25,... | collective-permute-start | bytes 1572872 | tf_op jit(solution)/shard_map/ppermute | solution.py:316
  147.7 8.0 %collective-permute-done.26 = f32[128,1024]{1,0:T(8,128)S(1)} collective-permute-done((f32[128,1024]{1,0:T(8,128)S(1)}, f32[128,1024]{1,0:T(8,128)S(1)}, u32[]{:S(2)}, u32[]{:S(2)}) %collective-permute-start.26) | collective-permute-done | bytes 524320 | tf_op jit(solution)/shard_map/ppermute | solution.py:316
  159.4 4.5 %copy-done.1 = f32[8192,256]{1,0:T(8,128)S(1)} copy-done((f32[8192,256]{1,0:T(8,128)S(1)}, f32[8192,256]{1,0:T(8,128)}, u32[]{:S(2)}) %copy-start.1) | copy-done | bytes 8388632
  166.6 6.4 %collective-permute-done.27 = f32[128,2048]{1,0:T(8,128)S(1)} collective-permute-done((f32[128,2048]{1,0:T(8,128)S(1)}, f32[128,2048]{1,0:T(8,128)S(1)}, u32[]{:S(2)}, u32[]{:S(2)}) %collective-permute-start.27) | collective-permute-done | bytes 1048608 | tf_op jit(solution)/shard_map/ppermute | solution.py:17
  176.1 8.3 %collective-permute-done.28 = f32[128,1024]{1,0:T(8,128)S(1)} collective-permute-done((f32[128,1024]{1,0:T(8,128)S(1)}, f32[128,1024]{1,0:T(8,128)S(1)}, u32[]{:S(2)}, u32[]{:S(2)}) %collective-permute-start.28) | collective-permute-done | bytes 524320 | tf_op jit(solution)/shard_map/ppermute | solution.py:17
  187.4 3.4 %collective-permute-start.29 = (f32[128,2048]{1,0:T(8,128)S(1)}, f32[128,2048]{1,0:T(8,128)S(1)}, u32[]{:S(2)}, u32[]{:S(2)}) collective-permute-start(f32[128,2048]{1,0:T(8,128)S(1)} %fusion.6), channel_id=1, source_target_pairs={{0,64},{32,96},{64,0},{96,32},{1,65},{33,97},{65,1},{97,33},{2,66}... | collective-permute-start | bytes 3145736 | tf_op jit(solution)/shard_map/ppermute | solution.py:17
  190.8 9.7 %all-gather.7.cloned.1.call-done = f32[8192,256]{1,0:T(8,128)} async-done(((f32[1024,256]{1,0:T(8,128)}), f32[8192,256]{1,0:T(8,128)}) %all-gather.7.cloned.1.call-update) | async-done | bytes 8388624 | tf_op jit(solution)/shard_map/all_gather | solution.py:351
  200.5 3.4 %copy-done = f32[8192,256]{1,0:T(8,128)S(1)} copy-done((f32[8192,256]{1,0:T(8,128)S(1)}, f32[8192,256]{1,0:T(8,128)}, u32[]{:S(2)}) %copy-start) | copy-done | bytes 8388632
  208.2 2.8 %collective-permute-start.30 = (f32[128,1024]{1,0:T(8,128)S(1)}, f32[128,1024]{1,0:T(8,128)S(1)}, u32[]{:S(2)}, u32[]{:S(2)}) collective-permute-start(f32[128,1024]{1,0:T(8,128)S(1)} %slice_add_fusion.4), channel_id=1, source_target_pairs={{0,8},{8,0},{1,9},{9,1},{2,10},{10,2},{3,11},{11,3},{4,12},{12,4},... | collective-permute-start | bytes 1572872 | tf_op jit(solution)/shard_map/ppermute | solution.py:17
  211.0 12.1 %collective-permute-done.30 = f32[128,1024]{1,0:T(8,128)S(1)} collective-permute-done((f32[128,1024]{1,0:T(8,128)S(1)}, f32[128,1024]{1,0:T(8,128)S(1)}, u32[]{:S(2)}, u32[]{:S(2)}) %collective-permute-start.30) | collective-permute-done | bytes 524320 | tf_op jit(solution)/shard_map/ppermute | solution.py:17
  235.6 3.5 %collective-permute-done.32 = f32[128,512]{1,0:T(8,128)S(1)} collective-permute-done((f32[128,512]{1,0:T(8,128)S(1)}, f32[128,512]{1,0:T(8,128)S(1)}, u32[]{:S(2)}, u32[]{:S(2)}) %collective-permute-start.32) | collective-permute-done | bytes 262176 | tf_op jit(solution)/shard_map/ppermute | solution.py:21
  241.2 7.2 %collective-permute-done.33 = f32[128,512]{1,0:T(8,128)S(1)} collective-permute-done((f32[128,512]{1,0:T(8,128)S(1)}, f32[128,512]{1,0:T(8,128)S(1)}, u32[]{:S(2)}, u32[]{:S(2)}) %collective-permute-start.33) | collective-permute-done | bytes 262176 | tf_op jit(solution)/shard_map/ppermute | solution.py:21
  248.4 4.5 %collective-permute-done.34 = f32[128,512]{1,0:T(8,128)S(1)} collective-permute-done((f32[128,512]{1,0:T(8,128)S(1)}, f32[128,512]{1,0:T(8,128)S(1)}, u32[]{:S(2)}, u32[]{:S(2)}) %collective-permute-start.34) | collective-permute-done | bytes 262176 | tf_op jit(solution)/shard_map/ppermute | solution.py:21
  254.7 2.8 %collective-permute-done.37 = f32[128,512]{1,0:T(8,128)S(1)} collective-permute-done((f32[128,512]{1,0:T(8,128)S(1)}, f32[128,512]{1,0:T(8,128)S(1)}, u32[]{:S(2)}, u32[]{:S(2)}) %collective-permute-start.37) | collective-permute-done | bytes 262176 | tf_op jit(solution)/shard_map/ppermute | solution.py:17
  (165 shorter events, 100.8 us)
Async XLA Ops:
  6.5 152.9 %all-gather.5.cloned.1.call-start = ((), (), s32[]{:S(2)}) async-start(), calls=%async_computation | async-start | bytes 9437184 | tf_op jit(solution)/shard_map/all_gather | solution.py:351
  9.1 38.8 %collective-permute-start.1 = (f32[1024,256]{1,0:T(8,128)}, f32[1024,256]{1,0:T(8,128)S(1)}, u32[]{:S(2)}, u32[]{:S(2)}) collective-permute-start(f32[1024,256]{1,0:T(8,128)} %shard_map.37), channel_id=1, source_target_pairs={{0,2},{2,0},{4,6},{6,4},{1,3},{3,1},{5,7},{7,5},{8,10},{10,8},{12,... | collective-permute-start | bytes 3145736 | tf_op jit(solution)/shard_map/ppermute | solution.py:17
  11.3 36.6 %collective-permute-start.2 = (f32[1024,256]{1,0:T(8,128)}, f32[1024,256]{1,0:T(8,128)}, u32[]{:S(2)}, u32[]{:S(2)}) collective-permute-start(f32[1024,256]{1,0:T(8,128)} %shard_map.37), channel_id=1, source_target_pairs={{0,6},{2,4},{4,2},{6,0},{1,7},{3,5},{5,3},{7,1},{8,14},{10,12},{12... | collective-permute-start | bytes 3145736 | tf_op jit(solution)/shard_map/ppermute | solution.py:17
  18.2 21.4 %collective-permute-start.4 = (f32[2,128,256]{2,1,0:T(8,128)S(1)}, f32[2,128,256]{2,1,0:T(8,128)S(1)}, u32[]{:S(2)}, u32[]{:S(2)}) collective-permute-start(f32[2,128,256]{2,1,0:T(8,128)S(1)} %get-tuple-element.101), channel_id=1, source_target_pairs={{0,2},{2,0},{4,6},{6,4},{1,3},{3,1},{5,7},{7,5},{8,10},{10,8},{12,... | collective-permute-start | bytes 786440 | tf_op jit(solution)/shard_map/ppermute | solution.py:17
  18.7 29.2 %collective-permute-start.5 = (f32[2,128,256]{2,1,0:T(8,128)S(1)}, f32[2,128,256]{2,1,0:T(8,128)S(1)}, u32[]{:S(2)}, u32[]{:S(2)}) collective-permute-start(f32[2,128,256]{2,1,0:T(8,128)S(1)} %get-tuple-element.102), channel_id=1, source_target_pairs={{0,4},{2,6},{4,0},{6,2},{1,5},{3,7},{5,1},{7,3},{8,12},{10,14},{12... | collective-permute-start | bytes 786440 | tf_op jit(solution)/shard_map/ppermute | solution.py:17
  20.2 27.7 %collective-permute-start.6 = (f32[2,128,256]{2,1,0:T(8,128)S(1)}, f32[2,128,256]{2,1,0:T(8,128)S(1)}, u32[]{:S(2)}, u32[]{:S(2)}) collective-permute-start(f32[2,128,256]{2,1,0:T(8,128)S(1)} %get-tuple-element.99), channel_id=1, source_target_pairs={{0,6},{2,4},{4,2},{6,0},{1,7},{3,5},{5,3},{7,1},{8,14},{10,12},{12... | collective-permute-start | bytes 786440 | tf_op jit(solution)/shard_map/ppermute | solution.py:17
  39.6 26.7 %collective-permute-start = (f32[1024,256]{1,0:T(8,128)}, f32[1024,256]{1,0:T(8,128)S(1)}, u32[]{:S(2)}, u32[]{:S(2)}) collective-permute-start(f32[1024,256]{1,0:T(8,128)} %shard_map.37), channel_id=1, source_target_pairs={{0,1},{1,0},{2,3},{3,2},{4,5},{5,4},{6,7},{7,6},{8,9},{9,8},{10,11... | collective-permute-start | bytes 3145736 | tf_op jit(solution)/shard_map/ppermute | solution.py:17
  50.8 17.5 %collective-permute-start.7 = (f32[1024,256]{1,0:T(8,128)S(1)}, f32[1024,256]{1,0:T(8,128)S(1)}, u32[]{:S(2)}, u32[]{:S(2)}) collective-permute-start(f32[1024,256]{1,0:T(8,128)S(1)} %collective-permute-done.1.refs_2_), channel_id=1, source_target_pairs={{0,1},{1,0},{2,3},{3,2},{4,5},{5,4},{6,7},{7,6},{8,9},{9,8},{10,11... | collective-permute-start | bytes 3145736 | tf_op jit(solution)/shard_map/ppermute | solution.py:17
  53.0 15.3 %collective-permute-start.8 = (f32[1024,256]{1,0:T(8,128)}, f32[1024,256]{1,0:T(8,128)S(1)}, u32[]{:S(2)}, u32[]{:S(2)}) collective-permute-start(f32[1024,256]{1,0:T(8,128)} %collective-permute-done.2.refs_4_), channel_id=1, source_target_pairs={{0,1},{1,0},{2,3},{3,2},{4,5},{5,4},{6,7},{7,6},{8,9},{9,8},{10,11... | collective-permute-start | bytes 3145736 | tf_op jit(solution)/shard_map/ppermute | solution.py:17
  66.3 26.6 %collective-permute-start.14 = (f32[1024,256]{1,0:T(8,128)}, f32[1024,256]{1,0:T(8,128)}, u32[]{:S(2)}, u32[]{:S(2)}) collective-permute-start(f32[1024,256]{1,0:T(8,128)} %shard_map.42), channel_id=1, source_target_pairs={{0,2},{2,0},{4,6},{6,4},{1,3},{3,1},{5,7},{7,5},{8,10},{10,8},{12,... | collective-permute-start | bytes 3145736 | tf_op jit(solution)/shard_map/ppermute | solution.py:17
  66.3 26.6 %collective-permute-start.15 = (f32[1024,256]{1,0:T(8,128)}, f32[1024,256]{1,0:T(8,128)}, u32[]{:S(2)}, u32[]{:S(2)}) collective-permute-start(f32[1024,256]{1,0:T(8,128)} %shard_map.42), channel_id=1, source_target_pairs={{0,6},{2,4},{4,2},{6,0},{1,7},{3,5},{5,3},{7,1},{8,14},{10,12},{12... | collective-permute-start | bytes 3145736 | tf_op jit(solution)/shard_map/ppermute | solution.py:17
  75.5 17.4 %collective-permute-start.13 = (f32[128,1024]{1,0:T(8,128)}, f32[128,1024]{1,0:T(8,128)}, u32[]{:S(2)}, u32[]{:S(2)}) collective-permute-start(f32[128,1024]{1,0:T(8,128)} %get-tuple-element.50), channel_id=1, source_target_pairs={{0,8},{8,0},{1,9},{9,1},{2,10},{10,2},{3,11},{11,3},{4,12},{12,4},... | collective-permute-start | bytes 1572872 | tf_op jit(solution)/shard_map/ppermute | solution.py:17
  92.9 107.6 %all-gather.7.cloned.1.call-start = ((), (), s32[]{:S(2)}) async-start(), calls=%async_computation.1 | async-start | bytes 9437184 | tf_op jit(solution)/shard_map/all_gather | solution.py:351
  96.0 25.9 %collective-permute-start.18 = (f32[1024,256]{1,0:T(8,128)}, f32[1024,256]{1,0:T(8,128)S(1)}, u32[]{:S(2)}, u32[]{:S(2)}) collective-permute-start(f32[1024,256]{1,0:T(8,128)} %collective-permute-done.14.refs_2_), channel_id=1, source_target_pairs={{0,1},{1,0},{2,3},{3,2},{4,5},{5,4},{6,7},{7,6},{8,9},{9,8},{10,11... | collective-permute-start | bytes 3145736 | tf_op jit(solution)/shard_map/ppermute | solution.py:17
  97.2 24.8 %collective-permute-start.19 = (f32[1024,256]{1,0:T(8,128)}, f32[1024,256]{1,0:T(8,128)S(1)}, u32[]{:S(2)}, u32[]{:S(2)}) collective-permute-start(f32[1024,256]{1,0:T(8,128)} %collective-permute-done.15.refs_4_), channel_id=1, source_target_pairs={{0,1},{1,0},{2,3},{3,2},{4,5},{5,4},{6,7},{7,6},{8,9},{9,8},{10,11... | collective-permute-start | bytes 3145736 | tf_op jit(solution)/shard_map/ppermute | solution.py:17
  97.7 19.1 %collective-permute-start.20 = (f32[512,256]{1,0:T(8,128)S(1)}, f32[512,256]{1,0:T(8,128)S(1)}, u32[]{:S(2)}, u32[]{:S(2)}) collective-permute-start(f32[512,256]{1,0:T(8,128)S(1)} %slice.116), channel_id=1, source_target_pairs={{0,6},{2,4},{4,2},{6,0},{1,7},{3,5},{5,3},{7,1},{8,14},{10,12},{12... | collective-permute-start | bytes 1572872 | tf_op jit(solution)/shard_map/ppermute | solution.py:17
  99.4 19.2 %collective-permute-start.22 = (f32[512,256]{1,0:T(8,128)S(1)}, f32[512,256]{1,0:T(8,128)S(1)}, u32[]{:S(2)}, u32[]{:S(2)}) collective-permute-start(f32[512,256]{1,0:T(8,128)S(1)} %slice.117), channel_id=1, source_target_pairs={{0,2},{2,0},{4,6},{6,4},{1,3},{3,1},{5,7},{7,5},{8,10},{10,8},{12,... | collective-permute-start | bytes 1572872 | tf_op jit(solution)/shard_map/ppermute | solution.py:17
  102.5 24.3 %collective-permute-start.16 = (f32[128,2048]{1,0:T(8,128)S(1)}, f32[128,2048]{1,0:T(8,128)S(1)}, u32[]{:S(2)}, u32[]{:S(2)}) collective-permute-start(f32[128,2048]{1,0:T(8,128)S(1)} %fusion.10), channel_id=1, source_target_pairs={{0,16},{16,0},{1,17},{17,1},{2,18},{18,2},{3,19},{19,3},{4,20},{20... | collective-permute-start | bytes 3145736 | tf_op jit(solution)/shard_map/ppermute | solution.py:17
  187.4 19.2 %collective-permute-start.29 = (f32[128,2048]{1,0:T(8,128)S(1)}, f32[128,2048]{1,0:T(8,128)S(1)}, u32[]{:S(2)}, u32[]{:S(2)}) collective-permute-start(f32[128,2048]{1,0:T(8,128)S(1)} %fusion.6), channel_id=1, source_target_pairs={{0,64},{32,96},{64,0},{96,32},{1,65},{33,97},{65,1},{97,33},{2,66}... | collective-permute-start | bytes 3145736 | tf_op jit(solution)/shard_map/ppermute | solution.py:17
  228.6 24.3 %collective-permute-start.35 = (f32[128,512]{1,0:T(8,128)S(1)}, f32[128,512]{1,0:T(8,128)S(1)}, u32[]{:S(2)}, u32[]{:S(2)}) collective-permute-start(f32[128,512]{1,0:T(8,128)S(1)} %get-tuple-element.98), channel_id=1, source_target_pairs={{0,4},{2,6},{4,0},{6,2},{1,5},{3,7},{5,1},{7,3},{8,12},{10,14},{12... | collective-permute-start | bytes 786440 | tf_op jit(solution)/shard_map/ppermute | solution.py:17
  231.0 17.4 %collective-permute-start.33 = (f32[128,512]{1,0:T(8,128)S(1)}, f32[128,512]{1,0:T(8,128)S(1)}, u32[]{:S(2)}, u32[]{:S(2)}) collective-permute-start(f32[128,512]{1,0:T(8,128)S(1)} %get-tuple-element.96), channel_id=1, source_target_pairs={{0,22},{2,20},{4,18},{6,16},{16,6},{18,4},{20,2},{22,0},{1,23},{3,... | collective-permute-start | bytes 786440 | tf_op jit(solution)/shard_map/ppermute | solution.py:21
  233.4 19.5 %collective-permute-start.34 = (f32[128,512]{1,0:T(8,128)S(1)}, f32[128,512]{1,0:T(8,128)S(1)}, u32[]{:S(2)}, u32[]{:S(2)}) collective-permute-start(f32[128,512]{1,0:T(8,128)S(1)} %get-tuple-element.95), channel_id=1, source_target_pairs={{0,16},{2,18},{4,20},{6,22},{16,0},{18,2},{20,4},{22,6},{1,17},{3,... | collective-permute-start | bytes 786440 | tf_op jit(solution)/shard_map/ppermute | solution.py:21
  235.3 19.4 %collective-permute-start.36 = (f32[128,512]{1,0:T(8,128)S(1)}, f32[128,512]{1,0:T(8,128)S(1)}, u32[]{:S(2)}, u32[]{:S(2)}) collective-permute-start(f32[128,512]{1,0:T(8,128)S(1)} %get-tuple-element.97), channel_id=1, source_target_pairs={{0,2},{2,0},{4,6},{6,4},{1,3},{3,1},{5,7},{7,5},{8,10},{10,8},{12,... | collective-permute-start | bytes 786440 | tf_op jit(solution)/shard_map/ppermute | solution.py:17
  239.1 18.4 %collective-permute-start.37 = (f32[128,512]{1,0:T(8,128)S(1)}, f32[128,512]{1,0:T(8,128)S(1)}, u32[]{:S(2)}, u32[]{:S(2)}) collective-permute-start(f32[128,512]{1,0:T(8,128)S(1)} %get-tuple-element.96), channel_id=1, source_target_pairs={{0,6},{2,4},{4,2},{6,0},{1,7},{3,5},{5,3},{7,1},{8,14},{10,12},{12... | collective-permute-start | bytes 786440 | tf_op jit(solution)/shard_map/ppermute | solution.py:17
  (44 other events, 312.5 us)
Sparse Core Ops, SparseCore 0:
  93.1 55.7 all-gather.4
  150.5 49.9 all-gather.6

commit v5 on v3

--- a/solution.py
+++ b/solution.py
@@ -17,12 +17,12 @@
     return lax.ppermute(x, axis, [(i, i ^ mask) for i in range(lax.axis_size(axis))])
 
 
+def swap_both(x, mask):
+    return lax.ppermute(x, ("x_lo", "y"), [(i, i ^ (Y + mask)) for i in range(2 * Y)])
+
+
 def params(mib):
     return pltpu.CompilerParams(vmem_limit_bytes=mib * MIB)
-
-
-def cost(bytes_accessed, flops=0):
-    return pl.CostEstimate(flops=flops, bytes_accessed=bytes_accessed, transcendentals=0)
 
 
 def split(x):
@@ -30,22 +30,20 @@
     return high, (x - high.astype(F32)).astype(BF16)
 
 
-def widen(hidden, step, behind=()):
+def widen(hidden, step):
     _, rows, feats = hidden.shape
 
-    def body(x_ref, *refs):
-        refs[-1][...] = x_ref[0].astype(F32)
+    def body(x_ref, o_ref):
+        o_ref[...] = x_ref[0].astype(F32)
 
     return pl.pallas_call(
         body,
         grid=(2,),
-        in_specs=[pl.BlockSpec((1, rows // 2, feats), lambda i: (step, i, 0))]
-        + [pl.BlockSpec(memory_space=pl.ANY)] * len(behind),
+        in_specs=[pl.BlockSpec((1, rows // 2, feats), lambda i: (step, i, 0))],
         out_specs=pl.BlockSpec((rows // 2, feats), lambda i: (i, 0)),
         out_shape=jax.ShapeDtypeStruct((rows, feats), F32),
         compiler_params=params(6),
-        cost_estimate=cost(6 * rows * feats),
-    )(hidden, *behind)
+    )(hidden)
 
 
 def narrow(near, far):
@@ -83,7 +81,6 @@
             jax.ShapeDtypeStruct((wide, rows), BF16),
         ],
         compiler_params=params(14),
-        cost_estimate=cost(8 * rows * wide),
     )(*near, *far)
 
 
@@ -118,7 +115,6 @@
             jax.ShapeDtypeStruct((count * feats, rows), BF16),
         ],
         compiler_params=params(14),
-        cost_estimate=cost(8 * count * rows * feats),
     )(order, *[gathered] * count)
 
 
@@ -175,7 +171,6 @@
         ],
         scratch_shapes=[pltpu.VMEM((probes, wide), BF16)] * 2,
         compiler_params=params(24),
-        cost_estimate=cost(6 * rows * wide, 4 * rows * wide * probes),
     )(*near, *far, *weights)
 
 
@@ -245,7 +240,6 @@
         ),
         out_shape=jax.ShapeDtypeStruct((steps, width, rows), F32),
         compiler_params=params(52),
-        cost_estimate=cost(8 * steps * rows * width),
     )(order, labels)
 
 
@@ -273,19 +267,19 @@
     return swap(x, "y", 1), swap(x, "y", 3)
 
 
-def second_hop(one, three):
+def to_pass_on(one, three):
     half = one.shape[0] // 2
-    return swap(one[:half], "y", 3), swap(three[half:], "y", 1)
+    return one[:half], three[half:]
+
+
+def second_hop(upper, lower):
+    return swap(upper, "y", 3), swap(lower, "y", 1)
 
 
 def land(own, narrow_own, one, three, two):
     near = [narrow_own, swap(own, "core", 1), one, swap(one, "core", 1), three, swap(three, "core", 1)]
     far = [two[0], swap(two[0], "core", 1), two[1], swap(two[1], "core", 1)]
     return near, far
-
-
-def corners(*arrays):
-    return [x[:8, :128] for x in arrays]
 
 
 def in_turn(x, axis):
@@ -310,12 +304,12 @@
     keep, give = weights_in(weights[0], order)
     pieces = jnp.stack([keep, swap(give, "core", 1)], axis=1)
     pieces = [pieces[0]] + [swap(pieces[k], "y", k) for k in (1, 2, 3)]
-    one, three, *pieces = tie(one, three, *pieces)
-    near, far = land(own, hidden[0], one, three, second_hop(one, three))
-
-    next_own = widen(hidden, 1)
+    targets = labels_in(labels, order)
+    next_own, upper, lower, targets, *pieces = tie(widen(hidden, 1), *to_pass_on(one, three), targets, *pieces)
+    near, far = land(own, hidden[0], one, three, second_hop(upper, lower))
+
     next_one, next_three = first_hop(next_own)
-    targets = labels_in(labels, order)
+    wides = [widen(hidden, s) for s in (2, 3)]
 
     x, state, margin = begin(near, far, pieces)
 
@@ -324,9 +318,8 @@
             margin = two_pass(state, xt)
         received = in_turn(margin, "x_hi") if step == 1 else swap(margin, "x_hi", 1)
         if step == 0:
-            received, one, three = tie(received, next_one, next_three)
-            landed = corners(received, one, three)
-            later = {s: lax.all_gather(widen(hidden, s, landed), ("y", "core")) for s in (2, 3)}
+            received, one, three, *wides = tie(received, next_one, next_three, *wides)
+            later = {s: lax.all_gather(wide, ("y", "core")) for s, wide in zip((2, 3), wides, strict=True)}
         residual = jax.nn.sigmoid(margin + received) - targets[step]
         update = state - 2.0 / rows * two_pass(residual, x)
         if step + 1 == STEPS:
@@ -334,18 +327,18 @@
         bit = step % 3
         partner = swap(update, "z", bit) if bit else swap(update, "x_lo", 1)
         if step == 0:
-            x, xt = narrow(*land(next_own, hidden[1], one, three, second_hop(one, three)))
+            x, xt = narrow(*land(next_own, hidden[1], one, three, second_hop(*to_pass_on(one, three))))
         else:
             x, xt = narrow_gathered(later[step + 1], order)
+            partner, x, xt = tie(partner, x, xt)
         state = 0.5 * (update + partner)
 
     deep = CORES * feats
-    away, stay = update[:, deep:], update[:, :deep]
-    away = 0.5 * (away + swap(away, "x_lo", 1))
-    stay, away = tie(stay, away)
-    blocks = [0.5 * (stay + swap(stay, "x_lo", 1))]
-    blocks += [swap(away[:, (k - 1) * deep : k * deep], "y", k) for k in (1, 2, 3)]
-    blocks = jnp.stack(blocks)
+    pieces = [update[:, k * deep : (k + 1) * deep] for k in range(Y)]
+    landed = tie(*[swap_both(pieces[k], k) for k in (2, 1, 3, 0)], *[swap(pieces[k], "y", k) for k in (2, 1, 3)])
+    mine = (*landed[4:], pieces[0])
+    two, one, three, zero = (0.5 * (a + b) for a, b in zip(mine, landed[:4], strict=True))
+    blocks = jnp.stack([zero, one, two, three])
     own, give = blocks[:, :, :feats], blocks[:, :, feats:]
     return weights_out(own, swap(give, "core", 1), order)[None]
 

time: 273 us -> 266 us (0.974)
  waiting for transfers between devices: 145 us -> 133 us
  starting transfers between devices: 55.7 us -> 60.2 us
  Pallas kernels: 22 us -> 25 us
    ppermute x34 -> x32, waiting for transfers between devices: 121 us -> 85 us  [swap(): lax.ppermute(x, axis, [(i, i ^ mask) for i in range(lax.axis_size(axis))])]
    ppermute x0 -> x4, waiting for transfers between devices: none -> 16.8 us  [swap_both(): lax.ppermute(x, ('x_lo', 'y'), [(i, i ^ Y + mask) for i in range(2 * Y)])]
    all_gather x2, waiting for transfers between devices: 2.82 us -> 10.4 us  [local(): lax.all_gather(wide, ('y', 'core'))]
    ppermute x0 -> x4, starting transfers between devices: none -> 5.29 us  [swap_both(): lax.ppermute(x, ('x_lo', 'y'), [(i, i ^ Y + mask) for i in range(2 * Y)])]
    unnamed x38 -> x22, local copies, waits for them, and re-layouts: 16 us -> 13.4 us
    ppermute x34 -> x32, starting transfers between devices: 49 us -> 48.2 us  [swap(): lax.ppermute(x, axis, [(i, i ^ mask) for i in range(lax.axis_size(axis))])]
  transfers between devices with their start and end apart: 39 -> 41, of which waited for: 23 -> 24; matrix products, arithmetic and copies ran while one was open for 5% -> 6% of each run, Pallas kernels for 7% -> 9%
where the time goes in v5:
time: 266 us
  waiting for transfers between devices  133 us (50%)
  starting transfers between devices  60.2 us (23%)
  Pallas kernels  25 us (9%)
  local copies, waits for them, and re-layouts  17.7 us (7%)
  between operations  13.8 us (5%)
  matrix products  8.91 us (3%)
  other arithmetic  6.62 us (2%)
    ppermute x32, waiting for transfers between devices, swap(): lax.ppermute(x, axis, [(i, i ^ mask) for i in range(lax.axis_size(axis))])  85 us
    ppermute x32, starting transfers between devices, swap(): lax.ppermute(x, axis, [(i, i ^ mask) for i in range(lax.axis_size(axis))])  48.2 us
    ppermute x4, waiting for transfers between devices, swap_both(): lax.ppermute(x, ('x_lo', 'y'), [(i, i ^ Y + mask) for i in range(2 * Y)])  16.8 us
    ppermute x1, waiting for transfers between devices, in_turn(): token = lax.ppermute(early[:8, :128], 'core', [(0, 1)])  13.6 us
    unnamed x22, local copies, waits for them, and re-layouts  13.4 us
    all_gather x2, waiting for transfers between devices, local(): lax.all_gather(wide, ('y', 'core'))  10.4 us
    dot_general x7, matrix products, two_pass(): out = jnp.dot(both, y, preferred_element_type=F32)  8.91 us
    ppermute x1, waiting for transfers between devices, in_turn(): late = lax.ppermute(send_behind(x, token), (axis, 'core'), second)  6.77 us
  transfers between devices with their start and end apart: 41, of which 24 were waited for; matrix products, arithmetic and copies ran while one was open for 6% of the time, Pallas kernels for 9%

profile of v5, /device:TPU:1, one launch (start us, length us, event | category | flops | bytes accessed | tf_op | source)
XLA Modules:
  0.0 265.5 jit_solution(17042472654310812148)
XLA Ops:
  22.4 4.7 %shard_map.39 = f32[4,128,1024]{2,1,0:T(8,128)} custom-call(s32[8]{0:T(128)S(1)} %iota_xor_fusion.order_ref, s32[4,1024,1024]{2,1,0:T(8,128)} %l_ref.1), custom_call_target="tpu_custom_call" | custom-call | tf_op jit(solution)/shard_map/pallas_call | solution.py:233
  27.1 6.0 %collective-permute-done.1.refs_2_ = f32[1024,256]{1,0:T(8,128)} collective-permute-done((f32[1024,256]{1,0:T(8,128)S(1)}, f32[1024,256]{1,0:T(8,128)}, u32[]{:S(2)}, u32[]{:S(2)}) %collective-permute-start.1) | collective-permute-done | bytes 1048608 | tf_op jit(solution)/shard_map/ppermute | solution.py:17
  33.0 2.9 %collective-permute-start = (f32[1024,256]{1,0:T(8,128)S(1)}, f32[1024,256]{1,0:T(8,128)S(1)}, u32[]{:S(2)}, u32[]{:S(2)}) collective-permute-start(f32[1024,256]{1,0:T(8,128)S(1)} %shard_map.37), channel_id=1, source_target_pairs={{0,1},{1,0},{2,3},{3,2},{4,5},{5,4},{6,7},{7,6},{8,9},{9,8},{10,11... | collective-permute-start | bytes 3145736 | tf_op jit(solution)/shard_map/ppermute | solution.py:17
  38.5 8.3 %collective-permute-done.7.refs_12_ = f32[2,128,256]{2,1,0:T(8,128)S(1)} collective-permute-done((f32[2,128,256]{2,1,0:T(8,128)S(1)}, f32[2,128,256]{2,1,0:T(8,128)S(1)}, u32[]{:S(2)}, u32[]{:S(2)}) %collective-permute-start.7) | collective-permute-done | bytes 262176 | tf_op jit(solution)/shard_map/ppermute | solution.py:17
  50.6 9.2 %collective-permute-done.9.refs_6_ = f32[512,256]{1,0:T(8,128)S(1)} collective-permute-done((f32[512,256]{1,0:T(8,128)S(1)}, f32[512,256]{1,0:T(8,128)S(1)}, u32[]{:S(2)}, u32[]{:S(2)}) %collective-permute-start.9) | collective-permute-done | bytes 524320 | tf_op jit(solution)/shard_map/ppermute | solution.py:17
  66.5 5.4 %shard_map.41 = (bf16[1024,2048]{1,0:T(8,128)(2,1)S(1)}, f32[128,2048]{1,0:T(8,128)S(1)}, f32[128,1024]{1,0:T(8,128)}) custom-call(bf16[1024,256]{1,0:T(8,128)(2,1)S(1)} %get-tuple-element.93.refs_0_, f32[1024,256]{1,0:T(8,128)S(1)} %collective-permute-done.refs_1_, f32[1024,256]{1,0:T(8,128)} %collective-permute-done.1.refs_2_, ...), custom_call_target="tpu_custom_call" | custom-call | tf_op jit(solution)/shard_map/pallas_call | solution.py:156
  79.6 8.3 %collective-permute-done.14.refs_2_ = f32[1024,256]{1,0:T(8,128)S(1)} collective-permute-done((f32[1024,256]{1,0:T(8,128)}, f32[1024,256]{1,0:T(8,128)S(1)}, u32[]{:S(2)}, u32[]{:S(2)}) %collective-permute-start.14) | collective-permute-done | bytes 1048608 | tf_op jit(solution)/shard_map/ppermute | solution.py:17
  100.0 11.4 %collective-permute-done.20.refs_6_ = f32[512,256]{1,0:T(8,128)S(1)} collective-permute-done((f32[512,256]{1,0:T(8,128)S(1)}, f32[512,256]{1,0:T(8,128)S(1)}, u32[]{:S(2)}, u32[]{:S(2)}) %collective-permute-start.20) | collective-permute-done | bytes 524320 | tf_op jit(solution)/shard_map/ppermute | solution.py:17
  116.4 3.6 %shard_map.44 = (bf16[1024,2048]{1,0:T(8,128)(2,1)S(1)}, bf16[2048,1024]{1,0:T(8,128)(2,1)S(1)}) custom-call(bf16[1024,256]{1,0:T(8,128)(2,1)S(1)} %copy-done.4, f32[1024,256]{1,0:T(8,128)S(1)} %collective-permute-done.17.refs_1_, f32[1024,256]{1,0:T(8,128)S(1)} %collective-permute-done.14.refs_2_, f32[1024,256]{1,0:T(8,128)S(1)} %collective-permute-done.18.refs_3_, ...), custom_call_target="tpu_custom_call" | custom-call | tf_op jit(solution)/shard_map/pallas_call | solution.py:69
  120.0 3.2 %collective-permute-done.16 = f32[128,2048]{1,0:T(8,128)S(1)} collective-permute-done((f32[128,2048]{1,0:T(8,128)S(1)}, f32[128,2048]{1,0:T(8,128)S(1)}, u32[]{:S(2)}, u32[]{:S(2)}) %collective-permute-start.16) | collective-permute-done | bytes 1048608 | tf_op jit(solution)/shard_map/ppermute | solution.py:17
  126.8 13.6 %collective-permute-done.25.token_ref = f32[8,128]{1,0:T(8,128)S(1)} collective-permute-done((f32[8,128]{1,0:T(8,128)S(1)}, f32[8,128]{1,0:T(8,128)S(1)}, u32[]{:S(2)}, u32[]{:S(2)}) %collective-permute-start.25) | collective-permute-done | bytes 4128 | tf_op jit(solution)/shard_map/ppermute | solution.py:288
  140.4 4.7 %collective-permute-start.26 = (f32[128,1024]{1,0:T(8,128)S(1)}, f32[128,1024]{1,0:T(8,128)S(1)}, u32[]{:S(2)}, u32[]{:S(2)}) collective-permute-start(f32[128,1024]{1,0:T(8,128)S(1)} %shard_map.45), channel_id=1, source_target_pairs={{1,9},{9,1},{3,11},{11,3},{5,13},{13,5},{7,15},{15,7},{17,25},{25,... | collective-permute-start | bytes 1572872 | tf_op jit(solution)/shard_map/ppermute | solution.py:289
  145.1 6.8 %collective-permute-done.26 = f32[128,1024]{1,0:T(8,128)S(1)} collective-permute-done((f32[128,1024]{1,0:T(8,128)S(1)}, f32[128,1024]{1,0:T(8,128)S(1)}, u32[]{:S(2)}, u32[]{:S(2)}) %collective-permute-start.26) | collective-permute-done | bytes 524320 | tf_op jit(solution)/shard_map/ppermute | solution.py:289
  155.5 4.3 %copy-done.1 = f32[8192,256]{1,0:T(8,128)S(1)} copy-done((f32[8192,256]{1,0:T(8,128)S(1)}, f32[8192,256]{1,0:T(8,128)}, u32[]{:S(2)}) %copy-start.1) | copy-done | bytes 8388632
  162.5 6.6 %collective-permute-done.27 = f32[128,2048]{1,0:T(8,128)S(1)} collective-permute-done((f32[128,2048]{1,0:T(8,128)S(1)}, f32[128,2048]{1,0:T(8,128)S(1)}, u32[]{:S(2)}, u32[]{:S(2)}) %collective-permute-start.27) | collective-permute-done | bytes 1048608 | tf_op jit(solution)/shard_map/ppermute | solution.py:17
  170.7 2.8 %collective-permute-start.28 = (f32[128,1024]{1,0:T(8,128)S(1)}, f32[128,1024]{1,0:T(8,128)S(1)}, u32[]{:S(2)}, u32[]{:S(2)}) collective-permute-start(f32[128,1024]{1,0:T(8,128)S(1)} %slice_add_fusion.5), channel_id=1, source_target_pairs={{0,8},{8,0},{1,9},{9,1},{2,10},{10,2},{3,11},{11,3},{4,12},{12,4},... | collective-permute-start | bytes 1572872 | tf_op jit(solution)/shard_map/ppermute | solution.py:17
  173.5 7.1 %collective-permute-done.28 = f32[128,1024]{1,0:T(8,128)S(1)} collective-permute-done((f32[128,1024]{1,0:T(8,128)S(1)}, f32[128,1024]{1,0:T(8,128)S(1)}, u32[]{:S(2)}, u32[]{:S(2)}) %collective-permute-start.28) | collective-permute-done | bytes 524320 | tf_op jit(solution)/shard_map/ppermute | solution.py:17
  183.5 3.4 %collective-permute-start.29 = (f32[128,2048]{1,0:T(8,128)S(1)}, f32[128,2048]{1,0:T(8,128)S(1)}, u32[]{:S(2)}, u32[]{:S(2)}) collective-permute-start(f32[128,2048]{1,0:T(8,128)S(1)} %fusion.6), channel_id=1, source_target_pairs={{0,64},{32,96},{64,0},{96,32},{1,65},{33,97},{65,1},{97,33},{2,66}... | collective-permute-start | bytes 3145736 | tf_op jit(solution)/shard_map/ppermute | solution.py:17
  186.9 10.4 %all-gather.7.cloned.1.call-done = f32[8192,256]{1,0:T(8,128)} async-done(((f32[1024,256]{1,0:T(8,128)}), f32[8192,256]{1,0:T(8,128)}) %all-gather.7.cloned.1.call-update) | async-done | bytes 8388624 | tf_op jit(solution)/shard_map/all_gather | solution.py:322
  197.3 3.4 %copy-done = f32[8192,256]{1,0:T(8,128)S(1)} copy-done((f32[8192,256]{1,0:T(8,128)S(1)}, f32[8192,256]{1,0:T(8,128)}, u32[]{:S(2)}) %copy-start) | copy-done | bytes 8388632
  207.8 12.1 %collective-permute-done.30 = f32[128,1024]{1,0:T(8,128)S(1)} collective-permute-done((f32[128,1024]{1,0:T(8,128)S(1)}, f32[128,1024]{1,0:T(8,128)S(1)}, u32[]{:S(2)}, u32[]{:S(2)}) %collective-permute-start.30) | collective-permute-done | bytes 524320 | tf_op jit(solution)/shard_map/ppermute | solution.py:17
  232.4 3.5 %collective-permute-done.32 = f32[128,512]{1,0:T(8,128)S(1)} collective-permute-done((f32[128,512]{1,0:T(8,128)S(1)}, f32[128,512]{1,0:T(8,128)S(1)}, u32[]{:S(2)}, u32[]{:S(2)}) %collective-permute-start.32) | collective-permute-done | bytes 262176 | tf_op jit(solution)/shard_map/ppermute | solution.py:21
  238.0 7.2 %collective-permute-done.33 = f32[128,512]{1,0:T(8,128)S(1)} collective-permute-done((f32[128,512]{1,0:T(8,128)S(1)}, f32[128,512]{1,0:T(8,128)S(1)}, u32[]{:S(2)}, u32[]{:S(2)}) %collective-permute-start.33) | collective-permute-done | bytes 262176 | tf_op jit(solution)/shard_map/ppermute | solution.py:21
  245.2 4.5 %collective-permute-done.34 = f32[128,512]{1,0:T(8,128)S(1)} collective-permute-done((f32[128,512]{1,0:T(8,128)S(1)}, f32[128,512]{1,0:T(8,128)S(1)}, u32[]{:S(2)}, u32[]{:S(2)}) %collective-permute-start.34) | collective-permute-done | bytes 262176 | tf_op jit(solution)/shard_map/ppermute | solution.py:21
  (132 shorter events, 98.4 us)
Async XLA Ops:
  6.5 149.0 %all-gather.5.cloned.1.call-start = ((), (), s32[]{:S(2)}) async-start(), calls=%async_computation | async-start | bytes 9437184 | tf_op jit(solution)/shard_map/all_gather | solution.py:322
  8.2 24.8 %collective-permute-start.1 = (f32[1024,256]{1,0:T(8,128)S(1)}, f32[1024,256]{1,0:T(8,128)}, u32[]{:S(2)}, u32[]{:S(2)}) collective-permute-start(f32[1024,256]{1,0:T(8,128)S(1)} %shard_map.37), channel_id=1, source_target_pairs={{0,2},{2,0},{4,6},{6,4},{1,3},{3,1},{5,7},{7,5},{8,10},{10,8},{12,... | collective-permute-start | bytes 3145736 | tf_op jit(solution)/shard_map/ppermute | solution.py:17
  10.4 26.5 %collective-permute-start.3 = (f32[1024,256]{1,0:T(8,128)S(1)}, f32[1024,256]{1,0:T(8,128)}, u32[]{:S(2)}, u32[]{:S(2)}) collective-permute-start(f32[1024,256]{1,0:T(8,128)S(1)} %shard_map.37), channel_id=1, source_target_pairs={{0,6},{2,4},{4,2},{6,0},{1,7},{3,5},{5,3},{7,1},{8,14},{10,12},{12... | collective-permute-start | bytes 3145736 | tf_op jit(solution)/shard_map/ppermute | solution.py:17
  17.4 21.2 %collective-permute-start.6 = (f32[2,128,256]{2,1,0:T(8,128)S(1)}, f32[2,128,256]{2,1,0:T(8,128)S(1)}, u32[]{:S(2)}, u32[]{:S(2)}) collective-permute-start(f32[2,128,256]{2,1,0:T(8,128)S(1)} %get-tuple-element.103), channel_id=1, source_target_pairs={{0,2},{2,0},{4,6},{6,4},{1,3},{3,1},{5,7},{7,5},{8,10},{10,8},{12,... | collective-permute-start | bytes 786440 | tf_op jit(solution)/shard_map/ppermute | solution.py:17
  17.9 29.0 %collective-permute-start.7 = (f32[2,128,256]{2,1,0:T(8,128)S(1)}, f32[2,128,256]{2,1,0:T(8,128)S(1)}, u32[]{:S(2)}, u32[]{:S(2)}) collective-permute-start(f32[2,128,256]{2,1,0:T(8,128)S(1)} %get-tuple-element.104), channel_id=1, source_target_pairs={{0,4},{2,6},{4,0},{6,2},{1,5},{3,7},{5,1},{7,3},{8,12},{10,14},{12... | collective-permute-start | bytes 786440 | tf_op jit(solution)/shard_map/ppermute | solution.py:17
  19.4 27.4 %collective-permute-start.8 = (f32[2,128,256]{2,1,0:T(8,128)S(1)}, f32[2,128,256]{2,1,0:T(8,128)S(1)}, u32[]{:S(2)}, u32[]{:S(2)}) collective-permute-start(f32[2,128,256]{2,1,0:T(8,128)S(1)} %get-tuple-element.101), channel_id=1, source_target_pairs={{0,6},{2,4},{4,2},{6,0},{1,7},{3,5},{5,3},{7,1},{8,14},{10,12},{12... | collective-permute-start | bytes 786440 | tf_op jit(solution)/shard_map/ppermute | solution.py:17
  33.0 29.8 %collective-permute-start = (f32[1024,256]{1,0:T(8,128)S(1)}, f32[1024,256]{1,0:T(8,128)S(1)}, u32[]{:S(2)}, u32[]{:S(2)}) collective-permute-start(f32[1024,256]{1,0:T(8,128)S(1)} %shard_map.37), channel_id=1, source_target_pairs={{0,1},{1,0},{2,3},{3,2},{4,5},{5,4},{6,7},{7,6},{8,9},{9,8},{10,11... | collective-permute-start | bytes 3145736 | tf_op jit(solution)/shard_map/ppermute | solution.py:17
  48.5 17.9 %collective-permute-start.2 = (f32[1024,256]{1,0:T(8,128)}, f32[1024,256]{1,0:T(8,128)S(1)}, u32[]{:S(2)}, u32[]{:S(2)}) collective-permute-start(f32[1024,256]{1,0:T(8,128)} %collective-permute-done.1.refs_2_), channel_id=1, source_target_pairs={{0,1},{1,0},{2,3},{3,2},{4,5},{5,4},{6,7},{7,6},{8,9},{9,8},{10,11... | collective-permute-start | bytes 3145736 | tf_op jit(solution)/shard_map/ppermute | solution.py:17
  50.6 15.8 %collective-permute-start.4 = (f32[1024,256]{1,0:T(8,128)}, f32[1024,256]{1,0:T(8,128)S(1)}, u32[]{:S(2)}, u32[]{:S(2)}) collective-permute-start(f32[1024,256]{1,0:T(8,128)} %collective-permute-done.3.refs_4_), channel_id=1, source_target_pairs={{0,1},{1,0},{2,3},{3,2},{4,5},{5,4},{6,7},{7,6},{8,9},{9,8},{10,11... | collective-permute-start | bytes 3145736 | tf_op jit(solution)/shard_map/ppermute | solution.py:17
  62.8 25.0 %collective-permute-start.14 = (f32[1024,256]{1,0:T(8,128)}, f32[1024,256]{1,0:T(8,128)S(1)}, u32[]{:S(2)}, u32[]{:S(2)}) collective-permute-start(f32[1024,256]{1,0:T(8,128)} %shard_map.38), channel_id=1, source_target_pairs={{0,2},{2,0},{4,6},{6,4},{1,3},{3,1},{5,7},{7,5},{8,10},{10,8},{12,... | collective-permute-start | bytes 3145736 | tf_op jit(solution)/shard_map/ppermute | solution.py:17
  63.9 25.9 %collective-permute-start.15 = (f32[1024,256]{1,0:T(8,128)}, f32[1024,256]{1,0:T(8,128)}, u32[]{:S(2)}, u32[]{:S(2)}) collective-permute-start(f32[1024,256]{1,0:T(8,128)} %shard_map.38), channel_id=1, source_target_pairs={{0,6},{2,4},{4,2},{6,0},{1,7},{3,5},{5,3},{7,1},{8,14},{10,12},{12... | collective-permute-start | bytes 3145736 | tf_op jit(solution)/shard_map/ppermute | solution.py:17
  89.9 107.5 %all-gather.7.cloned.1.call-start = ((), (), s32[]{:S(2)}) async-start(), calls=%async_computation.1 | async-start | bytes 9437184 | tf_op jit(solution)/shard_map/all_gather | solution.py:322
  92.0 24.5 %collective-permute-start.18 = (f32[1024,256]{1,0:T(8,128)S(1)}, f32[1024,256]{1,0:T(8,128)S(1)}, u32[]{:S(2)}, u32[]{:S(2)}) collective-permute-start(f32[1024,256]{1,0:T(8,128)S(1)} %collective-permute-done.14.refs_2_), channel_id=1, source_target_pairs={{0,1},{1,0},{2,3},{3,2},{4,5},{5,4},{6,7},{7,6},{8,9},{9,8},{10,11... | collective-permute-start | bytes 3145736 | tf_op jit(solution)/shard_map/ppermute | solution.py:17
  93.1 23.3 %collective-permute-start.19 = (f32[1024,256]{1,0:T(8,128)}, f32[1024,256]{1,0:T(8,128)S(1)}, u32[]{:S(2)}, u32[]{:S(2)}) collective-permute-start(f32[1024,256]{1,0:T(8,128)} %collective-permute-done.15.refs_4_), channel_id=1, source_target_pairs={{0,1},{1,0},{2,3},{3,2},{4,5},{5,4},{6,7},{7,6},{8,9},{9,8},{10,11... | collective-permute-start | bytes 3145736 | tf_op jit(solution)/shard_map/ppermute | solution.py:17
  94.1 17.3 %collective-permute-start.20 = (f32[512,256]{1,0:T(8,128)S(1)}, f32[512,256]{1,0:T(8,128)S(1)}, u32[]{:S(2)}, u32[]{:S(2)}) collective-permute-start(f32[512,256]{1,0:T(8,128)S(1)} %slice.116), channel_id=1, source_target_pairs={{0,6},{2,4},{4,2},{6,0},{1,7},{3,5},{5,3},{7,1},{8,14},{10,12},{12... | collective-permute-start | bytes 1572872 | tf_op jit(solution)/shard_map/ppermute | solution.py:17
  95.7 17.4 %collective-permute-start.22 = (f32[512,256]{1,0:T(8,128)S(1)}, f32[512,256]{1,0:T(8,128)S(1)}, u32[]{:S(2)}, u32[]{:S(2)}) collective-permute-start(f32[512,256]{1,0:T(8,128)S(1)} %slice.117), channel_id=1, source_target_pairs={{0,2},{2,0},{4,6},{6,4},{1,3},{3,1},{5,7},{7,5},{8,10},{10,8},{12,... | collective-permute-start | bytes 1572872 | tf_op jit(solution)/shard_map/ppermute | solution.py:17
  98.7 24.6 %collective-permute-start.16 = (f32[128,2048]{1,0:T(8,128)S(1)}, f32[128,2048]{1,0:T(8,128)S(1)}, u32[]{:S(2)}, u32[]{:S(2)}) collective-permute-start(f32[128,2048]{1,0:T(8,128)S(1)} %fusion.10), channel_id=1, source_target_pairs={{0,16},{16,0},{1,17},{17,1},{2,18},{18,2},{3,19},{19,3},{4,20},{20... | collective-permute-start | bytes 3145736 | tf_op jit(solution)/shard_map/ppermute | solution.py:17
  153.8 15.3 %collective-permute-start.27 = (f32[128,2048]{1,0:T(8,128)S(1)}, f32[128,2048]{1,0:T(8,128)S(1)}, u32[]{:S(2)}, u32[]{:S(2)}) collective-permute-start(f32[128,2048]{1,0:T(8,128)S(1)} %fusion.8), channel_id=1, source_target_pairs={{0,32},{32,0},{64,96},{96,64},{1,33},{33,1},{65,97},{97,65},{2,34}... | collective-permute-start | bytes 3145736 | tf_op jit(solution)/shard_map/ppermute | solution.py:17
  183.5 19.9 %collective-permute-start.29 = (f32[128,2048]{1,0:T(8,128)S(1)}, f32[128,2048]{1,0:T(8,128)S(1)}, u32[]{:S(2)}, u32[]{:S(2)}) collective-permute-start(f32[128,2048]{1,0:T(8,128)S(1)} %fusion.6), channel_id=1, source_target_pairs={{0,64},{32,96},{64,0},{96,32},{1,65},{33,97},{65,1},{97,33},{2,66}... | collective-permute-start | bytes 3145736 | tf_op jit(solution)/shard_map/ppermute | solution.py:17
  225.5 24.3 %collective-permute-start.35 = (f32[128,512]{1,0:T(8,128)S(1)}, f32[128,512]{1,0:T(8,128)S(1)}, u32[]{:S(2)}, u32[]{:S(2)}) collective-permute-start(f32[128,512]{1,0:T(8,128)S(1)} %get-tuple-element.100), channel_id=1, source_target_pairs={{0,4},{2,6},{4,0},{6,2},{1,5},{3,7},{5,1},{7,3},{8,12},{10,14},{12... | collective-permute-start | bytes 786440 | tf_op jit(solution)/shard_map/ppermute | solution.py:17
  227.8 17.4 %collective-permute-start.33 = (f32[128,512]{1,0:T(8,128)S(1)}, f32[128,512]{1,0:T(8,128)S(1)}, u32[]{:S(2)}, u32[]{:S(2)}) collective-permute-start(f32[128,512]{1,0:T(8,128)S(1)} %get-tuple-element.98), channel_id=1, source_target_pairs={{0,22},{2,20},{4,18},{6,16},{16,6},{18,4},{20,2},{22,0},{1,23},{3,... | collective-permute-start | bytes 786440 | tf_op jit(solution)/shard_map/ppermute | solution.py:21
  230.2 19.5 %collective-permute-start.34 = (f32[128,512]{1,0:T(8,128)S(1)}, f32[128,512]{1,0:T(8,128)S(1)}, u32[]{:S(2)}, u32[]{:S(2)}) collective-permute-start(f32[128,512]{1,0:T(8,128)S(1)} %get-tuple-element.97), channel_id=1, source_target_pairs={{0,16},{2,18},{4,20},{6,22},{16,0},{18,2},{20,4},{22,6},{1,17},{3,... | collective-permute-start | bytes 786440 | tf_op jit(solution)/shard_map/ppermute | solution.py:21
  232.1 19.4 %collective-permute-start.36 = (f32[128,512]{1,0:T(8,128)S(1)}, f32[128,512]{1,0:T(8,128)S(1)}, u32[]{:S(2)}, u32[]{:S(2)}) collective-permute-start(f32[128,512]{1,0:T(8,128)S(1)} %get-tuple-element.99), channel_id=1, source_target_pairs={{0,2},{2,0},{4,6},{6,4},{1,3},{3,1},{5,7},{7,5},{8,10},{10,8},{12,... | collective-permute-start | bytes 786440 | tf_op jit(solution)/shard_map/ppermute | solution.py:17
  235.9 18.4 %collective-permute-start.37 = (f32[128,512]{1,0:T(8,128)S(1)}, f32[128,512]{1,0:T(8,128)S(1)}, u32[]{:S(2)}, u32[]{:S(2)}) collective-permute-start(f32[128,512]{1,0:T(8,128)S(1)} %get-tuple-element.98), channel_id=1, source_target_pairs={{0,6},{2,4},{4,2},{6,0},{1,7},{3,5},{5,3},{7,1},{8,14},{10,12},{12... | collective-permute-start | bytes 786440 | tf_op jit(solution)/shard_map/ppermute | solution.py:17
  (28 other events, 211.3 us)
Sparse Core Ops, SparseCore 0:
  90.0 55.1 all-gather.4
  146.9 50.4 all-gather.6

commit v6 on v5

--- a/solution.py
+++ b/solution.py
@@ -84,9 +84,9 @@
     )(*near, *far)
 
 
-def narrow_gathered(gathered, order):
+def narrow_gathered(gathered, order, blocks, mib):
     count, rows, feats = gathered.shape
-    some = rows // 4
+    some = rows // blocks
 
     def body(order_ref, *refs):
         x_ref, t_ref = refs[count:]
@@ -114,7 +114,7 @@
             jax.ShapeDtypeStruct((rows, count * feats), BF16),
             jax.ShapeDtypeStruct((count * feats, rows), BF16),
         ],
-        compiler_params=params(14),
+        compiler_params=params(mib),
     )(order, *[gathered] * count)
 
 
@@ -329,15 +329,21 @@
         if step == 0:
             x, xt = narrow(*land(next_own, hidden[1], one, three, second_hop(*to_pass_on(one, three))))
         else:
-            x, xt = narrow_gathered(later[step + 1], order)
+            x, xt = narrow_gathered(later[step + 1], order, 4 if step == 1 else 2, 14 if step == 1 else 44)
             partner, x, xt = tie(partner, x, xt)
         state = 0.5 * (update + partner)
 
     deep = CORES * feats
     pieces = [update[:, k * deep : (k + 1) * deep] for k in range(Y)]
-    landed = tie(*[swap_both(pieces[k], k) for k in (2, 1, 3, 0)], *[swap(pieces[k], "y", k) for k in (2, 1, 3)])
-    mine = (*landed[4:], pieces[0])
-    two, one, three, zero = (0.5 * (a + b) for a, b in zip(mine, landed[:4], strict=True))
+    far = swap(pieces[2], "y", 2)
+    landed = tie(
+        *[swap_both(pieces[k], k) for k in (1, 3, 0)],
+        *[swap(pieces[k], "y", k) for k in (1, 3)],
+        swap(far, "x_lo", 1),
+    )
+    one, three, zero, two = (
+        0.5 * (a + b) for a, b in zip((*landed[3:5], pieces[0], far), (*landed[:3], landed[5]), strict=True)
+    )
     blocks = jnp.stack([zero, one, two, three])
     own, give = blocks[:, :, :feats], blocks[:, :, feats:]
     return weights_out(own, swap(give, "core", 1), order)[None]

time: 266 us -> 262 us (0.985)
  waiting for transfers between devices: 133 us -> 126 us
  starting transfers between devices: 60.2 us -> 63.8 us
  local copies, waits for them, and re-layouts: 17.7 us -> 14.4 us
    ppermute x4 -> x3, waiting for transfers between devices: 16.8 us -> 2.52 us  [swap_both(): lax.ppermute(x, ('x_lo', 'y'), [(i, i ^ Y + mask) for i in range(2 * Y)])]
    ppermute x32 -> x33, waiting for transfers between devices: 85 us -> 92.2 us  [swap(): lax.ppermute(x, axis, [(i, i ^ mask) for i in range(lax.axis_size(axis))])]
    ppermute x32 -> x33, starting transfers between devices: 48.2 us -> 53.4 us  [swap(): lax.ppermute(x, axis, [(i, i ^ mask) for i in range(lax.axis_size(axis))])]
    unnamed x22 -> x20, local copies, waits for them, and re-layouts: 13.4 us -> 10.1 us
  transfers between devices with their start and end apart: 41 -> 41, of which waited for: 24 -> 22; matrix products, arithmetic and copies ran while one was open for 6% -> 6% of each run, Pallas kernels for 9% -> 10%
where the time goes in v6:
time: 262 us; the launch traced here: 261 us
  waiting for transfers between devices  126 us (48%)
  starting transfers between devices  63.8 us (24%)
  Pallas kernels  27.2 us (10%)
  local copies, waits for them, and re-layouts  14.4 us (5%)
  between operations  13.8 us (5%)
  matrix products  8.84 us (3%)
  other arithmetic  6.62 us (3%)
    ppermute x33, waiting for transfers between devices, swap(): lax.ppermute(x, axis, [(i, i ^ mask) for i in range(lax.axis_size(axis))])  92.2 us
    ppermute x33, starting transfers between devices, swap(): lax.ppermute(x, axis, [(i, i ^ mask) for i in range(lax.axis_size(axis))])  53.4 us
    ppermute x1, waiting for transfers between devices, in_turn(): token = lax.ppermute(early[:8, :128], 'core', [(0, 1)])  13.6 us
    all_gather x2, waiting for transfers between devices, local(): lax.all_gather(wide, ('y', 'core'))  10.4 us
    unnamed x20, local copies, waits for them, and re-layouts  10.1 us
    dot_general x7, matrix products, two_pass(): out = jnp.dot(both, y, preferred_element_type=F32)  8.84 us
    pallas_call x2, Pallas kernels, narrow_gathered(): pl.pallas_call(body, grid_spec=pltpu.PrefetchScalarGridSpec(num_scalar_pr...  7.61 us
    ppermute x1, waiting for transfers between devices, in_turn(): late = lax.ppermute(send_behind(x, token), (axis, 'core'), second)  6.77 us
  transfers between devices with their start and end apart: 41, of which 22 were waited for; matrix products, arithmetic and copies ran while one was open for 6% of the time, Pallas kernels for 10%

profile of v6, /device:TPU:1, one launch (start us, length us, event | category | flops | bytes accessed | tf_op | source)
XLA Modules:
  0.0 260.9 jit_solution(6764091660943268959)
XLA Ops:
  22.4 4.7 %shard_map.39 = f32[4,128,1024]{2,1,0:T(8,128)} custom-call(s32[8]{0:T(128)S(1)} %iota_xor_fusion.order_ref, s32[4,1024,1024]{2,1,0:T(8,128)} %l_ref.1), custom_call_target="tpu_custom_call" | custom-call | tf_op jit(solution)/shard_map/pallas_call | solution.py:233
  27.1 5.9 %collective-permute-done.1.refs_2_ = f32[1024,256]{1,0:T(8,128)} collective-permute-done((f32[1024,256]{1,0:T(8,128)S(1)}, f32[1024,256]{1,0:T(8,128)}, u32[]{:S(2)}, u32[]{:S(2)}) %collective-permute-start.1) | collective-permute-done | bytes 1048608 | tf_op jit(solution)/shard_map/ppermute | solution.py:17
  33.0 2.9 %collective-permute-start = (f32[1024,256]{1,0:T(8,128)S(1)}, f32[1024,256]{1,0:T(8,128)S(1)}, u32[]{:S(2)}, u32[]{:S(2)}) collective-permute-start(f32[1024,256]{1,0:T(8,128)S(1)} %shard_map.37), channel_id=1, source_target_pairs={{0,1},{1,0},{2,3},{3,2},{4,5},{5,4},{6,7},{7,6},{8,9},{9,8},{10,11... | collective-permute-start | bytes 3145736 | tf_op jit(solution)/shard_map/ppermute | solution.py:17
  38.5 8.3 %collective-permute-done.7.refs_12_ = f32[2,128,256]{2,1,0:T(8,128)S(1)} collective-permute-done((f32[2,128,256]{2,1,0:T(8,128)S(1)}, f32[2,128,256]{2,1,0:T(8,128)S(1)}, u32[]{:S(2)}, u32[]{:S(2)}) %collective-permute-start.7) | collective-permute-done | bytes 262176 | tf_op jit(solution)/shard_map/ppermute | solution.py:17
  50.6 9.2 %collective-permute-done.9.refs_6_ = f32[512,256]{1,0:T(8,128)S(1)} collective-permute-done((f32[512,256]{1,0:T(8,128)S(1)}, f32[512,256]{1,0:T(8,128)S(1)}, u32[]{:S(2)}, u32[]{:S(2)}) %collective-permute-start.9) | collective-permute-done | bytes 524320 | tf_op jit(solution)/shard_map/ppermute | solution.py:17
  66.5 5.4 %shard_map.41 = (bf16[1024,2048]{1,0:T(8,128)(2,1)S(1)}, f32[128,2048]{1,0:T(8,128)S(1)}, f32[128,1024]{1,0:T(8,128)}) custom-call(bf16[1024,256]{1,0:T(8,128)(2,1)S(1)} %get-tuple-element.91.refs_0_, f32[1024,256]{1,0:T(8,128)S(1)} %collective-permute-done.refs_1_, f32[1024,256]{1,0:T(8,128)} %collective-permute-done.1.refs_2_, ...), custom_call_target="tpu_custom_call" | custom-call | tf_op jit(solution)/shard_map/pallas_call | solution.py:156
  79.6 8.3 %collective-permute-done.14.refs_2_ = f32[1024,256]{1,0:T(8,128)S(1)} collective-permute-done((f32[1024,256]{1,0:T(8,128)}, f32[1024,256]{1,0:T(8,128)S(1)}, u32[]{:S(2)}, u32[]{:S(2)}) %collective-permute-start.14) | collective-permute-done | bytes 1048608 | tf_op jit(solution)/shard_map/ppermute | solution.py:17
  100.0 11.4 %collective-permute-done.20.refs_6_ = f32[512,256]{1,0:T(8,128)S(1)} collective-permute-done((f32[512,256]{1,0:T(8,128)S(1)}, f32[512,256]{1,0:T(8,128)S(1)}, u32[]{:S(2)}, u32[]{:S(2)}) %collective-permute-start.20) | collective-permute-done | bytes 524320 | tf_op jit(solution)/shard_map/ppermute | solution.py:17
  116.4 3.6 %shard_map.44 = (bf16[1024,2048]{1,0:T(8,128)(2,1)S(1)}, bf16[2048,1024]{1,0:T(8,128)(2,1)S(1)}) custom-call(bf16[1024,256]{1,0:T(8,128)(2,1)S(1)} %copy-done.3, f32[1024,256]{1,0:T(8,128)S(1)} %collective-permute-done.17.refs_1_, f32[1024,256]{1,0:T(8,128)S(1)} %collective-permute-done.14.refs_2_, f32[1024,256]{1,0:T(8,128)S(1)} %collective-permute-done.18.refs_3_, ...), custom_call_target="tpu_custom_call" | custom-call | tf_op jit(solution)/shard_map/pallas_call | solution.py:69
  120.0 3.2 %collective-permute-done.16 = f32[128,2048]{1,0:T(8,128)S(1)} collective-permute-done((f32[128,2048]{1,0:T(8,128)S(1)}, f32[128,2048]{1,0:T(8,128)S(1)}, u32[]{:S(2)}, u32[]{:S(2)}) %collective-permute-start.16) | collective-permute-done | bytes 1048608 | tf_op jit(solution)/shard_map/ppermute | solution.py:17
  126.8 13.6 %collective-permute-done.25.token_ref = f32[8,128]{1,0:T(8,128)S(1)} collective-permute-done((f32[8,128]{1,0:T(8,128)S(1)}, f32[8,128]{1,0:T(8,128)S(1)}, u32[]{:S(2)}, u32[]{:S(2)}) %collective-permute-start.25) | collective-permute-done | bytes 4128 | tf_op jit(solution)/shard_map/ppermute | solution.py:288
  140.4 4.7 %collective-permute-start.26 = (f32[128,1024]{1,0:T(8,128)S(1)}, f32[128,1024]{1,0:T(8,128)S(1)}, u32[]{:S(2)}, u32[]{:S(2)}) collective-permute-start(f32[128,1024]{1,0:T(8,128)S(1)} %shard_map.45), channel_id=1, source_target_pairs={{1,9},{9,1},{3,11},{11,3},{5,13},{13,5},{7,15},{15,7},{17,25},{25,... | collective-permute-start | bytes 1572872 | tf_op jit(solution)/shard_map/ppermute | solution.py:289
  145.1 6.8 %collective-permute-done.26 = f32[128,1024]{1,0:T(8,128)S(1)} collective-permute-done((f32[128,1024]{1,0:T(8,128)S(1)}, f32[128,1024]{1,0:T(8,128)S(1)}, u32[]{:S(2)}, u32[]{:S(2)}) %collective-permute-start.26) | collective-permute-done | bytes 524320 | tf_op jit(solution)/shard_map/ppermute | solution.py:289
  155.5 4.3 %copy-done = f32[8192,256]{1,0:T(8,128)S(1)} copy-done((f32[8192,256]{1,0:T(8,128)S(1)}, f32[8192,256]{1,0:T(8,128)}, u32[]{:S(2)}) %copy-start) | copy-done | bytes 8388632
  162.5 6.6 %collective-permute-done.27 = f32[128,2048]{1,0:T(8,128)S(1)} collective-permute-done((f32[128,2048]{1,0:T(8,128)S(1)}, f32[128,2048]{1,0:T(8,128)S(1)}, u32[]{:S(2)}, u32[]{:S(2)}) %collective-permute-start.27) | collective-permute-done | bytes 1048608 | tf_op jit(solution)/shard_map/ppermute | solution.py:17
  170.7 2.8 %collective-permute-start.28 = (f32[128,1024]{1,0:T(8,128)S(1)}, f32[128,1024]{1,0:T(8,128)S(1)}, u32[]{:S(2)}, u32[]{:S(2)}) collective-permute-start(f32[128,1024]{1,0:T(8,128)S(1)} %slice_add_fusion.5), channel_id=1, source_target_pairs={{0,8},{8,0},{1,9},{9,1},{2,10},{10,2},{3,11},{11,3},{4,12},{12,4},... | collective-permute-start | bytes 1572872 | tf_op jit(solution)/shard_map/ppermute | solution.py:17
  173.5 7.1 %collective-permute-done.28 = f32[128,1024]{1,0:T(8,128)S(1)} collective-permute-done((f32[128,1024]{1,0:T(8,128)S(1)}, f32[128,1024]{1,0:T(8,128)S(1)}, u32[]{:S(2)}, u32[]{:S(2)}) %collective-permute-start.28) | collective-permute-done | bytes 524320 | tf_op jit(solution)/shard_map/ppermute | solution.py:17
  183.5 3.4 %collective-permute-start.29 = (f32[128,2048]{1,0:T(8,128)S(1)}, f32[128,2048]{1,0:T(8,128)S(1)}, u32[]{:S(2)}, u32[]{:S(2)}) collective-permute-start(f32[128,2048]{1,0:T(8,128)S(1)} %fusion.6), channel_id=1, source_target_pairs={{0,64},{32,96},{64,0},{96,32},{1,65},{33,97},{65,1},{97,33},{2,66}... | collective-permute-start | bytes 3145736 | tf_op jit(solution)/shard_map/ppermute | solution.py:17
  186.9 10.4 %all-gather.7.cloned.1.call-done = f32[8192,256]{1,0:T(8,128)} async-done(((f32[1024,256]{1,0:T(8,128)}), f32[8192,256]{1,0:T(8,128)}) %all-gather.7.cloned.1.call-update) | async-done | bytes 8388624 | tf_op jit(solution)/shard_map/all_gather | solution.py:322
  197.3 4.9 %shard_map.47 = (bf16[1024,2048]{1,0:T(8,128)(2,1)S(1)}, bf16[2048,1024]{1,0:T(8,128)(2,1)S(1)}) custom-call(s32[8]{0:T(128)S(1)} %iota_xor_fusion.order_ref, f32[8,1024,256]{2,1,0:T(8,128)} %bitcast.55, f32[8,1024,256]{2,1,0:T(8,128)} %bitcast.56, f32[8,1024,256]{2,1,0:T(8,128)} %bitcast.57, f32[8,1024,256]{2,1,0:T(8,128)} %bitcast.58, ...), custom_call_target="tpu_custom_call" | custom-call | tf_op jit(solution)/shard_map/pallas_call | solution.py:99
  203.8 2.8 %collective-permute-start.30 = (f32[128,1024]{1,0:T(8,128)S(1)}, f32[128,1024]{1,0:T(8,128)S(1)}, u32[]{:S(2)}, u32[]{:S(2)}) collective-permute-start(f32[128,1024]{1,0:T(8,128)S(1)} %slice_add_fusion.4), channel_id=1, source_target_pairs={{0,8},{8,0},{1,9},{9,1},{2,10},{10,2},{3,11},{11,3},{4,12},{12,4},... | collective-permute-start | bytes 1572872 | tf_op jit(solution)/shard_map/ppermute | solution.py:17
  206.6 12.1 %collective-permute-done.30 = f32[128,1024]{1,0:T(8,128)S(1)} collective-permute-done((f32[128,1024]{1,0:T(8,128)S(1)}, f32[128,1024]{1,0:T(8,128)S(1)}, u32[]{:S(2)}, u32[]{:S(2)}) %collective-permute-start.30) | collective-permute-done | bytes 524320 | tf_op jit(solution)/shard_map/ppermute | solution.py:17
  229.2 6.2 %collective-permute-done.36 = f32[128,512]{1,0:T(8,128)S(1)} collective-permute-done((f32[128,512]{1,0:T(8,128)S(1)}, f32[128,512]{1,0:T(8,128)S(1)}, u32[]{:S(2)}, u32[]{:S(2)}) %collective-permute-start.36) | collective-permute-done | bytes 262176 | tf_op jit(solution)/shard_map/ppermute | solution.py:17
  243.5 5.0 %collective-permute-done.37 = f32[128,512]{1,0:T(8,128)S(1)} collective-permute-done((f32[128,512]{1,0:T(8,128)S(1)}, f32[128,512]{1,0:T(8,128)S(1)}, u32[]{:S(2)}, u32[]{:S(2)}) %collective-permute-start.37) | collective-permute-done | bytes 262176 | tf_op jit(solution)/shard_map/ppermute | solution.py:17
  (130 shorter events, 93.5 us)
Async XLA Ops:
  6.5 149.0 %all-gather.5.cloned.1.call-start = ((), (), s32[]{:S(2)}) async-start(), calls=%async_computation | async-start | bytes 9437184 | tf_op jit(solution)/shard_map/all_gather | solution.py:322
  8.2 24.8 %collective-permute-start.1 = (f32[1024,256]{1,0:T(8,128)S(1)}, f32[1024,256]{1,0:T(8,128)}, u32[]{:S(2)}, u32[]{:S(2)}) collective-permute-start(f32[1024,256]{1,0:T(8,128)S(1)} %shard_map.37), channel_id=1, source_target_pairs={{0,2},{2,0},{4,6},{6,4},{1,3},{3,1},{5,7},{7,5},{8,10},{10,8},{12,... | collective-permute-start | bytes 3145736 | tf_op jit(solution)/shard_map/ppermute | solution.py:17
  10.4 26.5 %collective-permute-start.3 = (f32[1024,256]{1,0:T(8,128)S(1)}, f32[1024,256]{1,0:T(8,128)}, u32[]{:S(2)}, u32[]{:S(2)}) collective-permute-start(f32[1024,256]{1,0:T(8,128)S(1)} %shard_map.37), channel_id=1, source_target_pairs={{0,6},{2,4},{4,2},{6,0},{1,7},{3,5},{5,3},{7,1},{8,14},{10,12},{12... | collective-permute-start | bytes 3145736 | tf_op jit(solution)/shard_map/ppermute | solution.py:17
  17.4 21.2 %collective-permute-start.6 = (f32[2,128,256]{2,1,0:T(8,128)S(1)}, f32[2,128,256]{2,1,0:T(8,128)S(1)}, u32[]{:S(2)}, u32[]{:S(2)}) collective-permute-start(f32[2,128,256]{2,1,0:T(8,128)S(1)} %get-tuple-element.101), channel_id=1, source_target_pairs={{0,2},{2,0},{4,6},{6,4},{1,3},{3,1},{5,7},{7,5},{8,10},{10,8},{12,... | collective-permute-start | bytes 786440 | tf_op jit(solution)/shard_map/ppermute | solution.py:17
  17.9 29.0 %collective-permute-start.7 = (f32[2,128,256]{2,1,0:T(8,128)S(1)}, f32[2,128,256]{2,1,0:T(8,128)S(1)}, u32[]{:S(2)}, u32[]{:S(2)}) collective-permute-start(f32[2,128,256]{2,1,0:T(8,128)S(1)} %get-tuple-element.102), channel_id=1, source_target_pairs={{0,4},{2,6},{4,0},{6,2},{1,5},{3,7},{5,1},{7,3},{8,12},{10,14},{12... | collective-permute-start | bytes 786440 | tf_op jit(solution)/shard_map/ppermute | solution.py:17
  19.4 27.4 %collective-permute-start.8 = (f32[2,128,256]{2,1,0:T(8,128)S(1)}, f32[2,128,256]{2,1,0:T(8,128)S(1)}, u32[]{:S(2)}, u32[]{:S(2)}) collective-permute-start(f32[2,128,256]{2,1,0:T(8,128)S(1)} %get-tuple-element.99), channel_id=1, source_target_pairs={{0,6},{2,4},{4,2},{6,0},{1,7},{3,5},{5,3},{7,1},{8,14},{10,12},{12... | collective-permute-start | bytes 786440 | tf_op jit(solution)/shard_map/ppermute | solution.py:17
  33.0 29.8 %collective-permute-start = (f32[1024,256]{1,0:T(8,128)S(1)}, f32[1024,256]{1,0:T(8,128)S(1)}, u32[]{:S(2)}, u32[]{:S(2)}) collective-permute-start(f32[1024,256]{1,0:T(8,128)S(1)} %shard_map.37), channel_id=1, source_target_pairs={{0,1},{1,0},{2,3},{3,2},{4,5},{5,4},{6,7},{7,6},{8,9},{9,8},{10,11... | collective-permute-start | bytes 3145736 | tf_op jit(solution)/shard_map/ppermute | solution.py:17
  48.5 18.0 %collective-permute-start.2 = (f32[1024,256]{1,0:T(8,128)}, f32[1024,256]{1,0:T(8,128)S(1)}, u32[]{:S(2)}, u32[]{:S(2)}) collective-permute-start(f32[1024,256]{1,0:T(8,128)} %collective-permute-done.1.refs_2_), channel_id=1, source_target_pairs={{0,1},{1,0},{2,3},{3,2},{4,5},{5,4},{6,7},{7,6},{8,9},{9,8},{10,11... | collective-permute-start | bytes 3145736 | tf_op jit(solution)/shard_map/ppermute | solution.py:17
  50.6 15.8 %collective-permute-start.4 = (f32[1024,256]{1,0:T(8,128)}, f32[1024,256]{1,0:T(8,128)S(1)}, u32[]{:S(2)}, u32[]{:S(2)}) collective-permute-start(f32[1024,256]{1,0:T(8,128)} %collective-permute-done.3.refs_4_), channel_id=1, source_target_pairs={{0,1},{1,0},{2,3},{3,2},{4,5},{5,4},{6,7},{7,6},{8,9},{9,8},{10,11... | collective-permute-start | bytes 3145736 | tf_op jit(solution)/shard_map/ppermute | solution.py:17
  62.8 25.0 %collective-permute-start.14 = (f32[1024,256]{1,0:T(8,128)}, f32[1024,256]{1,0:T(8,128)S(1)}, u32[]{:S(2)}, u32[]{:S(2)}) collective-permute-start(f32[1024,256]{1,0:T(8,128)} %shard_map.38), channel_id=1, source_target_pairs={{0,2},{2,0},{4,6},{6,4},{1,3},{3,1},{5,7},{7,5},{8,10},{10,8},{12,... | collective-permute-start | bytes 3145736 | tf_op jit(solution)/shard_map/ppermute | solution.py:17
  63.9 25.9 %collective-permute-start.15 = (f32[1024,256]{1,0:T(8,128)}, f32[1024,256]{1,0:T(8,128)}, u32[]{:S(2)}, u32[]{:S(2)}) collective-permute-start(f32[1024,256]{1,0:T(8,128)} %shard_map.38), channel_id=1, source_target_pairs={{0,6},{2,4},{4,2},{6,0},{1,7},{3,5},{5,3},{7,1},{8,14},{10,12},{12... | collective-permute-start | bytes 3145736 | tf_op jit(solution)/shard_map/ppermute | solution.py:17
  74.9 15.0 %collective-permute-start.13 = (f32[128,1024]{1,0:T(8,128)}, f32[128,1024]{1,0:T(8,128)}, u32[]{:S(2)}, u32[]{:S(2)}) collective-permute-start(f32[128,1024]{1,0:T(8,128)} %get-tuple-element.50), channel_id=1, source_target_pairs={{0,8},{8,0},{1,9},{9,1},{2,10},{10,2},{3,11},{11,3},{4,12},{12,4},... | collective-permute-start | bytes 1572872 | tf_op jit(solution)/shard_map/ppermute | solution.py:17
  89.9 107.5 %all-gather.7.cloned.1.call-start = ((), (), s32[]{:S(2)}) async-start(), calls=%async_computation.1 | async-start | bytes 9437184 | tf_op jit(solution)/shard_map/all_gather | solution.py:322
  92.0 24.5 %collective-permute-start.18 = (f32[1024,256]{1,0:T(8,128)S(1)}, f32[1024,256]{1,0:T(8,128)S(1)}, u32[]{:S(2)}, u32[]{:S(2)}) collective-permute-start(f32[1024,256]{1,0:T(8,128)S(1)} %collective-permute-done.14.refs_2_), channel_id=1, source_target_pairs={{0,1},{1,0},{2,3},{3,2},{4,5},{5,4},{6,7},{7,6},{8,9},{9,8},{10,11... | collective-permute-start | bytes 3145736 | tf_op jit(solution)/shard_map/ppermute | solution.py:17
  93.1 23.3 %collective-permute-start.19 = (f32[1024,256]{1,0:T(8,128)}, f32[1024,256]{1,0:T(8,128)S(1)}, u32[]{:S(2)}, u32[]{:S(2)}) collective-permute-start(f32[1024,256]{1,0:T(8,128)} %collective-permute-done.15.refs_4_), channel_id=1, source_target_pairs={{0,1},{1,0},{2,3},{3,2},{4,5},{5,4},{6,7},{7,6},{8,9},{9,8},{10,11... | collective-permute-start | bytes 3145736 | tf_op jit(solution)/shard_map/ppermute | solution.py:17
  94.1 17.3 %collective-permute-start.20 = (f32[512,256]{1,0:T(8,128)S(1)}, f32[512,256]{1,0:T(8,128)S(1)}, u32[]{:S(2)}, u32[]{:S(2)}) collective-permute-start(f32[512,256]{1,0:T(8,128)S(1)} %slice.116), channel_id=1, source_target_pairs={{0,6},{2,4},{4,2},{6,0},{1,7},{3,5},{5,3},{7,1},{8,14},{10,12},{12... | collective-permute-start | bytes 1572872 | tf_op jit(solution)/shard_map/ppermute | solution.py:17
  95.7 17.4 %collective-permute-start.22 = (f32[512,256]{1,0:T(8,128)S(1)}, f32[512,256]{1,0:T(8,128)S(1)}, u32[]{:S(2)}, u32[]{:S(2)}) collective-permute-start(f32[512,256]{1,0:T(8,128)S(1)} %slice.117), channel_id=1, source_target_pairs={{0,2},{2,0},{4,6},{6,4},{1,3},{3,1},{5,7},{7,5},{8,10},{10,8},{12,... | collective-permute-start | bytes 1572872 | tf_op jit(solution)/shard_map/ppermute | solution.py:17
  98.7 24.6 %collective-permute-start.16 = (f32[128,2048]{1,0:T(8,128)S(1)}, f32[128,2048]{1,0:T(8,128)S(1)}, u32[]{:S(2)}, u32[]{:S(2)}) collective-permute-start(f32[128,2048]{1,0:T(8,128)S(1)} %fusion.10), channel_id=1, source_target_pairs={{0,16},{16,0},{1,17},{17,1},{2,18},{18,2},{3,19},{19,3},{4,20},{20... | collective-permute-start | bytes 3145736 | tf_op jit(solution)/shard_map/ppermute | solution.py:17
  125.5 14.9 %collective-permute-start.25 = (f32[8,128]{1,0:T(8,128)S(1)}, f32[8,128]{1,0:T(8,128)S(1)}, u32[]{:S(2)}, u32[]{:S(2)}) collective-permute-start(f32[8,128]{1,0:T(8,128)S(1)} %slice.152), channel_id=1, source_target_pairs={{0,1},{2,3},{4,5},{6,7},{8,9},{10,11},{12,13},{14,15},{16,17},{18,... | collective-permute-start | bytes 12296 | tf_op jit(solution)/shard_map/ppermute | solution.py:288
  153.8 15.3 %collective-permute-start.27 = (f32[128,2048]{1,0:T(8,128)S(1)}, f32[128,2048]{1,0:T(8,128)S(1)}, u32[]{:S(2)}, u32[]{:S(2)}) collective-permute-start(f32[128,2048]{1,0:T(8,128)S(1)} %fusion.8), channel_id=1, source_target_pairs={{0,32},{32,0},{64,96},{96,64},{1,33},{33,1},{65,97},{97,65},{2,34}... | collective-permute-start | bytes 3145736 | tf_op jit(solution)/shard_map/ppermute | solution.py:17
  183.5 18.8 %collective-permute-start.29 = (f32[128,2048]{1,0:T(8,128)S(1)}, f32[128,2048]{1,0:T(8,128)S(1)}, u32[]{:S(2)}, u32[]{:S(2)}) collective-permute-start(f32[128,2048]{1,0:T(8,128)S(1)} %fusion.6), channel_id=1, source_target_pairs={{0,64},{32,96},{64,0},{96,32},{1,65},{33,97},{65,1},{97,33},{2,66}... | collective-permute-start | bytes 3145736 | tf_op jit(solution)/shard_map/ppermute | solution.py:17
  203.8 14.9 %collective-permute-start.30 = (f32[128,1024]{1,0:T(8,128)S(1)}, f32[128,1024]{1,0:T(8,128)S(1)}, u32[]{:S(2)}, u32[]{:S(2)}) collective-permute-start(f32[128,1024]{1,0:T(8,128)S(1)} %slice_add_fusion.4), channel_id=1, source_target_pairs={{0,8},{8,0},{1,9},{9,1},{2,10},{10,2},{3,11},{11,3},{4,12},{12,4},... | collective-permute-start | bytes 1572872 | tf_op jit(solution)/shard_map/ppermute | solution.py:17
  224.2 18.6 %collective-permute-start.34 = (f32[128,512]{1,0:T(8,128)S(1)}, f32[128,512]{1,0:T(8,128)S(1)}, u32[]{:S(2)}, u32[]{:S(2)}) collective-permute-start(f32[128,512]{1,0:T(8,128)S(1)} %get-tuple-element.97), channel_id=1, source_target_pairs={{0,2},{2,0},{4,6},{6,4},{1,3},{3,1},{5,7},{7,5},{8,10},{10,8},{12,... | collective-permute-start | bytes 786440 | tf_op jit(solution)/shard_map/ppermute | solution.py:17
  228.0 14.9 %collective-permute-start.33 = (f32[128,512]{1,0:T(8,128)S(1)}, f32[128,512]{1,0:T(8,128)S(1)}, u32[]{:S(2)}, u32[]{:S(2)}) collective-permute-start(f32[128,512]{1,0:T(8,128)S(1)} %get-tuple-element.98), channel_id=1, source_target_pairs={{0,16},{2,18},{4,20},{6,22},{16,0},{18,2},{20,4},{22,6},{1,17},{3,... | collective-permute-start | bytes 786440 | tf_op jit(solution)/shard_map/ppermute | solution.py:21
  (27 other events, 205.7 us)
Sparse Core Ops, SparseCore 0:
  90.0 55.1 all-gather.4
  146.9 50.4 all-gather.6

commit v7 on v6

--- a/solution.py
+++ b/solution.py
@@ -208,15 +208,15 @@
                 start = pl.multiple_of(order_ref[k * CORES + j] * width, width)
                 o_ref[:, pl.ds(start, width)] = w_ref[k].T
 
-    spec = pl.BlockSpec(own.shape, lambda i, order: (0, 0, 0))
+    spec = pl.BlockSpec((Y, width, feats // 2), lambda i, order: (0, 0, i))
     out = (feats, LANES * width)
     return pl.pallas_call(
         body,
         grid_spec=pltpu.PrefetchScalarGridSpec(
             num_scalar_prefetch=1,
-            grid=(1,),
+            grid=(2,),
             in_specs=[spec] * 2,
-            out_specs=pl.BlockSpec(out, lambda i, order: (0, 0)),
+            out_specs=pl.BlockSpec((feats // 2, LANES * width), lambda i, order: (i, 0)),
         ),
         out_shape=jax.ShapeDtypeStruct(out, F32),
         compiler_params=params(8),

time: 262 us -> 262 us (level)
  no operation moved by 1% of the time
where the time goes in v7:
time: 262 us; the launch traced here: 261 us
  waiting for transfers between devices  126 us (48%)
  starting transfers between devices  63.8 us (24%)
  Pallas kernels  27.2 us (10%)
  local copies, waits for them, and re-layouts  14.4 us (5%)
  between operations  13.8 us (5%)
  matrix products  8.84 us (3%)
  other arithmetic  6.62 us (3%)
    ppermute x33, waiting for transfers between devices, swap(): lax.ppermute(x, axis, [(i, i ^ mask) for i in range(lax.axis_size(axis))])  92.2 us
    ppermute x33, starting transfers between devices, swap(): lax.ppermute(x, axis, [(i, i ^ mask) for i in range(lax.axis_size(axis))])  53.4 us
    ppermute x1, waiting for transfers between devices, in_turn(): token = lax.ppermute(early[:8, :128], 'core', [(0, 1)])  13.6 us
    all_gather x2, waiting for transfers between devices, local(): lax.all_gather(wide, ('y', 'core'))  10.4 us
    unnamed x20, local copies, waits for them, and re-layouts  10.1 us
    dot_general x7, matrix products, two_pass(): out = jnp.dot(both, y, preferred_element_type=F32)  8.84 us
    pallas_call x2, Pallas kernels, narrow_gathered(): pl.pallas_call(body, grid_spec=pltpu.PrefetchScalarGridSpec(num_scalar_pr...  7.61 us
    ppermute x1, waiting for transfers between devices, in_turn(): late = lax.ppermute(send_behind(x, token), (axis, 'core'), second)  6.77 us
  transfers between devices with their start and end apart: 41, of which 22 were waited for; matrix products, arithmetic and copies ran while one was open for 6% of the time, Pallas kernels for 10%

profile of v7, /device:TPU:1, one launch (start us, length us, event | category | flops | bytes accessed | tf_op | source)
XLA Modules:
  0.0 260.9 jit_solution(3873244473945797822)
XLA Ops:
  22.4 4.7 %shard_map.39 = f32[4,128,1024]{2,1,0:T(8,128)} custom-call(s32[8]{0:T(128)S(1)} %iota_xor_fusion.order_ref, s32[4,1024,1024]{2,1,0:T(8,128)} %l_ref.1), custom_call_target="tpu_custom_call" | custom-call | tf_op jit(solution)/shard_map/pallas_call | solution.py:233
  27.1 5.9 %collective-permute-done.1.refs_2_ = f32[1024,256]{1,0:T(8,128)} collective-permute-done((f32[1024,256]{1,0:T(8,128)S(1)}, f32[1024,256]{1,0:T(8,128)}, u32[]{:S(2)}, u32[]{:S(2)}) %collective-permute-start.1) | collective-permute-done | bytes 1048608 | tf_op jit(solution)/shard_map/ppermute | solution.py:17
  33.0 2.9 %collective-permute-start = (f32[1024,256]{1,0:T(8,128)S(1)}, f32[1024,256]{1,0:T(8,128)S(1)}, u32[]{:S(2)}, u32[]{:S(2)}) collective-permute-start(f32[1024,256]{1,0:T(8,128)S(1)} %shard_map.37), channel_id=1, source_target_pairs={{0,1},{1,0},{2,3},{3,2},{4,5},{5,4},{6,7},{7,6},{8,9},{9,8},{10,11... | collective-permute-start | bytes 3145736 | tf_op jit(solution)/shard_map/ppermute | solution.py:17
  38.5 8.3 %collective-permute-done.7.refs_12_ = f32[2,128,256]{2,1,0:T(8,128)S(1)} collective-permute-done((f32[2,128,256]{2,1,0:T(8,128)S(1)}, f32[2,128,256]{2,1,0:T(8,128)S(1)}, u32[]{:S(2)}, u32[]{:S(2)}) %collective-permute-start.7) | collective-permute-done | bytes 262176 | tf_op jit(solution)/shard_map/ppermute | solution.py:17
  50.6 9.2 %collective-permute-done.9.refs_6_ = f32[512,256]{1,0:T(8,128)S(1)} collective-permute-done((f32[512,256]{1,0:T(8,128)S(1)}, f32[512,256]{1,0:T(8,128)S(1)}, u32[]{:S(2)}, u32[]{:S(2)}) %collective-permute-start.9) | collective-permute-done | bytes 524320 | tf_op jit(solution)/shard_map/ppermute | solution.py:17
  66.5 5.4 %shard_map.41 = (bf16[1024,2048]{1,0:T(8,128)(2,1)S(1)}, f32[128,2048]{1,0:T(8,128)S(1)}, f32[128,1024]{1,0:T(8,128)}) custom-call(bf16[1024,256]{1,0:T(8,128)(2,1)S(1)} %get-tuple-element.91.refs_0_, f32[1024,256]{1,0:T(8,128)S(1)} %collective-permute-done.refs_1_, f32[1024,256]{1,0:T(8,128)} %collective-permute-done.1.refs_2_, ...), custom_call_target="tpu_custom_call" | custom-call | tf_op jit(solution)/shard_map/pallas_call | solution.py:156
  79.6 8.3 %collective-permute-done.14.refs_2_ = f32[1024,256]{1,0:T(8,128)S(1)} collective-permute-done((f32[1024,256]{1,0:T(8,128)}, f32[1024,256]{1,0:T(8,128)S(1)}, u32[]{:S(2)}, u32[]{:S(2)}) %collective-permute-start.14) | collective-permute-done | bytes 1048608 | tf_op jit(solution)/shard_map/ppermute | solution.py:17
  100.0 11.4 %collective-permute-done.20.refs_6_ = f32[512,256]{1,0:T(8,128)S(1)} collective-permute-done((f32[512,256]{1,0:T(8,128)S(1)}, f32[512,256]{1,0:T(8,128)S(1)}, u32[]{:S(2)}, u32[]{:S(2)}) %collective-permute-start.20) | collective-permute-done | bytes 524320 | tf_op jit(solution)/shard_map/ppermute | solution.py:17
  116.4 3.6 %shard_map.44 = (bf16[1024,2048]{1,0:T(8,128)(2,1)S(1)}, bf16[2048,1024]{1,0:T(8,128)(2,1)S(1)}) custom-call(bf16[1024,256]{1,0:T(8,128)(2,1)S(1)} %copy-done.3, f32[1024,256]{1,0:T(8,128)S(1)} %collective-permute-done.17.refs_1_, f32[1024,256]{1,0:T(8,128)S(1)} %collective-permute-done.14.refs_2_, f32[1024,256]{1,0:T(8,128)S(1)} %collective-permute-done.18.refs_3_, ...), custom_call_target="tpu_custom_call" | custom-call | tf_op jit(solution)/shard_map/pallas_call | solution.py:69
  120.0 3.2 %collective-permute-done.16 = f32[128,2048]{1,0:T(8,128)S(1)} collective-permute-done((f32[128,2048]{1,0:T(8,128)S(1)}, f32[128,2048]{1,0:T(8,128)S(1)}, u32[]{:S(2)}, u32[]{:S(2)}) %collective-permute-start.16) | collective-permute-done | bytes 1048608 | tf_op jit(solution)/shard_map/ppermute | solution.py:17
  126.8 13.6 %collective-permute-done.25.token_ref = f32[8,128]{1,0:T(8,128)S(1)} collective-permute-done((f32[8,128]{1,0:T(8,128)S(1)}, f32[8,128]{1,0:T(8,128)S(1)}, u32[]{:S(2)}, u32[]{:S(2)}) %collective-permute-start.25) | collective-permute-done | bytes 4128 | tf_op jit(solution)/shard_map/ppermute | solution.py:288
  140.4 4.7 %collective-permute-start.26 = (f32[128,1024]{1,0:T(8,128)S(1)}, f32[128,1024]{1,0:T(8,128)S(1)}, u32[]{:S(2)}, u32[]{:S(2)}) collective-permute-start(f32[128,1024]{1,0:T(8,128)S(1)} %shard_map.45), channel_id=1, source_target_pairs={{1,9},{9,1},{3,11},{11,3},{5,13},{13,5},{7,15},{15,7},{17,25},{25,... | collective-permute-start | bytes 1572872 | tf_op jit(solution)/shard_map/ppermute | solution.py:289
  145.1 6.8 %collective-permute-done.26 = f32[128,1024]{1,0:T(8,128)S(1)} collective-permute-done((f32[128,1024]{1,0:T(8,128)S(1)}, f32[128,1024]{1,0:T(8,128)S(1)}, u32[]{:S(2)}, u32[]{:S(2)}) %collective-permute-start.26) | collective-permute-done | bytes 524320 | tf_op jit(solution)/shard_map/ppermute | solution.py:289
  155.5 4.3 %copy-done = f32[8192,256]{1,0:T(8,128)S(1)} copy-done((f32[8192,256]{1,0:T(8,128)S(1)}, f32[8192,256]{1,0:T(8,128)}, u32[]{:S(2)}) %copy-start) | copy-done | bytes 8388632
  162.5 6.6 %collective-permute-done.27 = f32[128,2048]{1,0:T(8,128)S(1)} collective-permute-done((f32[128,2048]{1,0:T(8,128)S(1)}, f32[128,2048]{1,0:T(8,128)S(1)}, u32[]{:S(2)}, u32[]{:S(2)}) %collective-permute-start.27) | collective-permute-done | bytes 1048608 | tf_op jit(solution)/shard_map/ppermute | solution.py:17
  170.7 2.8 %collective-permute-start.28 = (f32[128,1024]{1,0:T(8,128)S(1)}, f32[128,1024]{1,0:T(8,128)S(1)}, u32[]{:S(2)}, u32[]{:S(2)}) collective-permute-start(f32[128,1024]{1,0:T(8,128)S(1)} %slice_add_fusion.5), channel_id=1, source_target_pairs={{0,8},{8,0},{1,9},{9,1},{2,10},{10,2},{3,11},{11,3},{4,12},{12,4},... | collective-permute-start | bytes 1572872 | tf_op jit(solution)/shard_map/ppermute | solution.py:17
  173.5 7.1 %collective-permute-done.28 = f32[128,1024]{1,0:T(8,128)S(1)} collective-permute-done((f32[128,1024]{1,0:T(8,128)S(1)}, f32[128,1024]{1,0:T(8,128)S(1)}, u32[]{:S(2)}, u32[]{:S(2)}) %collective-permute-start.28) | collective-permute-done | bytes 524320 | tf_op jit(solution)/shard_map/ppermute | solution.py:17
  183.5 3.4 %collective-permute-start.29 = (f32[128,2048]{1,0:T(8,128)S(1)}, f32[128,2048]{1,0:T(8,128)S(1)}, u32[]{:S(2)}, u32[]{:S(2)}) collective-permute-start(f32[128,2048]{1,0:T(8,128)S(1)} %fusion.6), channel_id=1, source_target_pairs={{0,64},{32,96},{64,0},{96,32},{1,65},{33,97},{65,1},{97,33},{2,66}... | collective-permute-start | bytes 3145736 | tf_op jit(solution)/shard_map/ppermute | solution.py:17
  186.9 10.4 %all-gather.7.cloned.1.call-done = f32[8192,256]{1,0:T(8,128)} async-done(((f32[1024,256]{1,0:T(8,128)}), f32[8192,256]{1,0:T(8,128)}) %all-gather.7.cloned.1.call-update) | async-done | bytes 8388624 | tf_op jit(solution)/shard_map/all_gather | solution.py:322
  197.3 4.9 %shard_map.47 = (bf16[1024,2048]{1,0:T(8,128)(2,1)S(1)}, bf16[2048,1024]{1,0:T(8,128)(2,1)S(1)}) custom-call(s32[8]{0:T(128)S(1)} %iota_xor_fusion.order_ref, f32[8,1024,256]{2,1,0:T(8,128)} %bitcast.55, f32[8,1024,256]{2,1,0:T(8,128)} %bitcast.56, f32[8,1024,256]{2,1,0:T(8,128)} %bitcast.57, f32[8,1024,256]{2,1,0:T(8,128)} %bitcast.58, ...), custom_call_target="tpu_custom_call" | custom-call | tf_op jit(solution)/shard_map/pallas_call | solution.py:99
  203.8 2.8 %collective-permute-start.30 = (f32[128,1024]{1,0:T(8,128)S(1)}, f32[128,1024]{1,0:T(8,128)S(1)}, u32[]{:S(2)}, u32[]{:S(2)}) collective-permute-start(f32[128,1024]{1,0:T(8,128)S(1)} %slice_add_fusion.4), channel_id=1, source_target_pairs={{0,8},{8,0},{1,9},{9,1},{2,10},{10,2},{3,11},{11,3},{4,12},{12,4},... | collective-permute-start | bytes 1572872 | tf_op jit(solution)/shard_map/ppermute | solution.py:17
  206.6 12.1 %collective-permute-done.30 = f32[128,1024]{1,0:T(8,128)S(1)} collective-permute-done((f32[128,1024]{1,0:T(8,128)S(1)}, f32[128,1024]{1,0:T(8,128)S(1)}, u32[]{:S(2)}, u32[]{:S(2)}) %collective-permute-start.30) | collective-permute-done | bytes 524320 | tf_op jit(solution)/shard_map/ppermute | solution.py:17
  229.2 6.2 %collective-permute-done.36 = f32[128,512]{1,0:T(8,128)S(1)} collective-permute-done((f32[128,512]{1,0:T(8,128)S(1)}, f32[128,512]{1,0:T(8,128)S(1)}, u32[]{:S(2)}, u32[]{:S(2)}) %collective-permute-start.36) | collective-permute-done | bytes 262176 | tf_op jit(solution)/shard_map/ppermute | solution.py:17
  243.5 5.0 %collective-permute-done.37 = f32[128,512]{1,0:T(8,128)S(1)} collective-permute-done((f32[128,512]{1,0:T(8,128)S(1)}, f32[128,512]{1,0:T(8,128)S(1)}, u32[]{:S(2)}, u32[]{:S(2)}) %collective-permute-start.37) | collective-permute-done | bytes 262176 | tf_op jit(solution)/shard_map/ppermute | solution.py:17
  (130 shorter events, 93.6 us)
Async XLA Ops:
  6.5 149.0 %all-gather.5.cloned.1.call-start = ((), (), s32[]{:S(2)}) async-start(), calls=%async_computation | async-start | bytes 9437184 | tf_op jit(solution)/shard_map/all_gather | solution.py:322
  8.2 24.8 %collective-permute-start.1 = (f32[1024,256]{1,0:T(8,128)S(1)}, f32[1024,256]{1,0:T(8,128)}, u32[]{:S(2)}, u32[]{:S(2)}) collective-permute-start(f32[1024,256]{1,0:T(8,128)S(1)} %shard_map.37), channel_id=1, source_target_pairs={{0,2},{2,0},{4,6},{6,4},{1,3},{3,1},{5,7},{7,5},{8,10},{10,8},{12,... | collective-permute-start | bytes 3145736 | tf_op jit(solution)/shard_map/ppermute | solution.py:17
  10.4 26.5 %collective-permute-start.3 = (f32[1024,256]{1,0:T(8,128)S(1)}, f32[1024,256]{1,0:T(8,128)}, u32[]{:S(2)}, u32[]{:S(2)}) collective-permute-start(f32[1024,256]{1,0:T(8,128)S(1)} %shard_map.37), channel_id=1, source_target_pairs={{0,6},{2,4},{4,2},{6,0},{1,7},{3,5},{5,3},{7,1},{8,14},{10,12},{12... | collective-permute-start | bytes 3145736 | tf_op jit(solution)/shard_map/ppermute | solution.py:17
  17.4 21.2 %collective-permute-start.6 = (f32[2,128,256]{2,1,0:T(8,128)S(1)}, f32[2,128,256]{2,1,0:T(8,128)S(1)}, u32[]{:S(2)}, u32[]{:S(2)}) collective-permute-start(f32[2,128,256]{2,1,0:T(8,128)S(1)} %get-tuple-element.101), channel_id=1, source_target_pairs={{0,2},{2,0},{4,6},{6,4},{1,3},{3,1},{5,7},{7,5},{8,10},{10,8},{12,... | collective-permute-start | bytes 786440 | tf_op jit(solution)/shard_map/ppermute | solution.py:17
  17.9 29.0 %collective-permute-start.7 = (f32[2,128,256]{2,1,0:T(8,128)S(1)}, f32[2,128,256]{2,1,0:T(8,128)S(1)}, u32[]{:S(2)}, u32[]{:S(2)}) collective-permute-start(f32[2,128,256]{2,1,0:T(8,128)S(1)} %get-tuple-element.102), channel_id=1, source_target_pairs={{0,4},{2,6},{4,0},{6,2},{1,5},{3,7},{5,1},{7,3},{8,12},{10,14},{12... | collective-permute-start | bytes 786440 | tf_op jit(solution)/shard_map/ppermute | solution.py:17
  19.4 27.4 %collective-permute-start.8 = (f32[2,128,256]{2,1,0:T(8,128)S(1)}, f32[2,128,256]{2,1,0:T(8,128)S(1)}, u32[]{:S(2)}, u32[]{:S(2)}) collective-permute-start(f32[2,128,256]{2,1,0:T(8,128)S(1)} %get-tuple-element.99), channel_id=1, source_target_pairs={{0,6},{2,4},{4,2},{6,0},{1,7},{3,5},{5,3},{7,1},{8,14},{10,12},{12... | collective-permute-start | bytes 786440 | tf_op jit(solution)/shard_map/ppermute | solution.py:17
  33.0 29.8 %collective-permute-start = (f32[1024,256]{1,0:T(8,128)S(1)}, f32[1024,256]{1,0:T(8,128)S(1)}, u32[]{:S(2)}, u32[]{:S(2)}) collective-permute-start(f32[1024,256]{1,0:T(8,128)S(1)} %shard_map.37), channel_id=1, source_target_pairs={{0,1},{1,0},{2,3},{3,2},{4,5},{5,4},{6,7},{7,6},{8,9},{9,8},{10,11... | collective-permute-start | bytes 3145736 | tf_op jit(solution)/shard_map/ppermute | solution.py:17
  48.5 18.0 %collective-permute-start.2 = (f32[1024,256]{1,0:T(8,128)}, f32[1024,256]{1,0:T(8,128)S(1)}, u32[]{:S(2)}, u32[]{:S(2)}) collective-permute-start(f32[1024,256]{1,0:T(8,128)} %collective-permute-done.1.refs_2_), channel_id=1, source_target_pairs={{0,1},{1,0},{2,3},{3,2},{4,5},{5,4},{6,7},{7,6},{8,9},{9,8},{10,11... | collective-permute-start | bytes 3145736 | tf_op jit(solution)/shard_map/ppermute | solution.py:17
  50.6 15.8 %collective-permute-start.4 = (f32[1024,256]{1,0:T(8,128)}, f32[1024,256]{1,0:T(8,128)S(1)}, u32[]{:S(2)}, u32[]{:S(2)}) collective-permute-start(f32[1024,256]{1,0:T(8,128)} %collective-permute-done.3.refs_4_), channel_id=1, source_target_pairs={{0,1},{1,0},{2,3},{3,2},{4,5},{5,4},{6,7},{7,6},{8,9},{9,8},{10,11... | collective-permute-start | bytes 3145736 | tf_op jit(solution)/shard_map/ppermute | solution.py:17
  62.8 25.0 %collective-permute-start.14 = (f32[1024,256]{1,0:T(8,128)}, f32[1024,256]{1,0:T(8,128)S(1)}, u32[]{:S(2)}, u32[]{:S(2)}) collective-permute-start(f32[1024,256]{1,0:T(8,128)} %shard_map.38), channel_id=1, source_target_pairs={{0,2},{2,0},{4,6},{6,4},{1,3},{3,1},{5,7},{7,5},{8,10},{10,8},{12,... | collective-permute-start | bytes 3145736 | tf_op jit(solution)/shard_map/ppermute | solution.py:17
  63.9 25.9 %collective-permute-start.15 = (f32[1024,256]{1,0:T(8,128)}, f32[1024,256]{1,0:T(8,128)}, u32[]{:S(2)}, u32[]{:S(2)}) collective-permute-start(f32[1024,256]{1,0:T(8,128)} %shard_map.38), channel_id=1, source_target_pairs={{0,6},{2,4},{4,2},{6,0},{1,7},{3,5},{5,3},{7,1},{8,14},{10,12},{12... | collective-permute-start | bytes 3145736 | tf_op jit(solution)/shard_map/ppermute | solution.py:17
  74.9 15.0 %collective-permute-start.13 = (f32[128,1024]{1,0:T(8,128)}, f32[128,1024]{1,0:T(8,128)}, u32[]{:S(2)}, u32[]{:S(2)}) collective-permute-start(f32[128,1024]{1,0:T(8,128)} %get-tuple-element.50), channel_id=1, source_target_pairs={{0,8},{8,0},{1,9},{9,1},{2,10},{10,2},{3,11},{11,3},{4,12},{12,4},... | collective-permute-start | bytes 1572872 | tf_op jit(solution)/shard_map/ppermute | solution.py:17
  89.9 107.5 %all-gather.7.cloned.1.call-start = ((), (), s32[]{:S(2)}) async-start(), calls=%async_computation.1 | async-start | bytes 9437184 | tf_op jit(solution)/shard_map/all_gather | solution.py:322
  92.0 24.5 %collective-permute-start.18 = (f32[1024,256]{1,0:T(8,128)S(1)}, f32[1024,256]{1,0:T(8,128)S(1)}, u32[]{:S(2)}, u32[]{:S(2)}) collective-permute-start(f32[1024,256]{1,0:T(8,128)S(1)} %collective-permute-done.14.refs_2_), channel_id=1, source_target_pairs={{0,1},{1,0},{2,3},{3,2},{4,5},{5,4},{6,7},{7,6},{8,9},{9,8},{10,11... | collective-permute-start | bytes 3145736 | tf_op jit(solution)/shard_map/ppermute | solution.py:17
  93.1 23.3 %collective-permute-start.19 = (f32[1024,256]{1,0:T(8,128)}, f32[1024,256]{1,0:T(8,128)S(1)}, u32[]{:S(2)}, u32[]{:S(2)}) collective-permute-start(f32[1024,256]{1,0:T(8,128)} %collective-permute-done.15.refs_4_), channel_id=1, source_target_pairs={{0,1},{1,0},{2,3},{3,2},{4,5},{5,4},{6,7},{7,6},{8,9},{9,8},{10,11... | collective-permute-start | bytes 3145736 | tf_op jit(solution)/shard_map/ppermute | solution.py:17
  94.1 17.3 %collective-permute-start.20 = (f32[512,256]{1,0:T(8,128)S(1)}, f32[512,256]{1,0:T(8,128)S(1)}, u32[]{:S(2)}, u32[]{:S(2)}) collective-permute-start(f32[512,256]{1,0:T(8,128)S(1)} %slice.116), channel_id=1, source_target_pairs={{0,6},{2,4},{4,2},{6,0},{1,7},{3,5},{5,3},{7,1},{8,14},{10,12},{12... | collective-permute-start | bytes 1572872 | tf_op jit(solution)/shard_map/ppermute | solution.py:17
  95.7 17.4 %collective-permute-start.22 = (f32[512,256]{1,0:T(8,128)S(1)}, f32[512,256]{1,0:T(8,128)S(1)}, u32[]{:S(2)}, u32[]{:S(2)}) collective-permute-start(f32[512,256]{1,0:T(8,128)S(1)} %slice.117), channel_id=1, source_target_pairs={{0,2},{2,0},{4,6},{6,4},{1,3},{3,1},{5,7},{7,5},{8,10},{10,8},{12,... | collective-permute-start | bytes 1572872 | tf_op jit(solution)/shard_map/ppermute | solution.py:17
  98.7 24.6 %collective-permute-start.16 = (f32[128,2048]{1,0:T(8,128)S(1)}, f32[128,2048]{1,0:T(8,128)S(1)}, u32[]{:S(2)}, u32[]{:S(2)}) collective-permute-start(f32[128,2048]{1,0:T(8,128)S(1)} %fusion.10), channel_id=1, source_target_pairs={{0,16},{16,0},{1,17},{17,1},{2,18},{18,2},{3,19},{19,3},{4,20},{20... | collective-permute-start | bytes 3145736 | tf_op jit(solution)/shard_map/ppermute | solution.py:17
  125.5 14.9 %collective-permute-start.25 = (f32[8,128]{1,0:T(8,128)S(1)}, f32[8,128]{1,0:T(8,128)S(1)}, u32[]{:S(2)}, u32[]{:S(2)}) collective-permute-start(f32[8,128]{1,0:T(8,128)S(1)} %slice.152), channel_id=1, source_target_pairs={{0,1},{2,3},{4,5},{6,7},{8,9},{10,11},{12,13},{14,15},{16,17},{18,... | collective-permute-start | bytes 12296 | tf_op jit(solution)/shard_map/ppermute | solution.py:288
  153.8 15.3 %collective-permute-start.27 = (f32[128,2048]{1,0:T(8,128)S(1)}, f32[128,2048]{1,0:T(8,128)S(1)}, u32[]{:S(2)}, u32[]{:S(2)}) collective-permute-start(f32[128,2048]{1,0:T(8,128)S(1)} %fusion.8), channel_id=1, source_target_pairs={{0,32},{32,0},{64,96},{96,64},{1,33},{33,1},{65,97},{97,65},{2,34}... | collective-permute-start | bytes 3145736 | tf_op jit(solution)/shard_map/ppermute | solution.py:17
  183.5 18.8 %collective-permute-start.29 = (f32[128,2048]{1,0:T(8,128)S(1)}, f32[128,2048]{1,0:T(8,128)S(1)}, u32[]{:S(2)}, u32[]{:S(2)}) collective-permute-start(f32[128,2048]{1,0:T(8,128)S(1)} %fusion.6), channel_id=1, source_target_pairs={{0,64},{32,96},{64,0},{96,32},{1,65},{33,97},{65,1},{97,33},{2,66}... | collective-permute-start | bytes 3145736 | tf_op jit(solution)/shard_map/ppermute | solution.py:17
  203.8 14.9 %collective-permute-start.30 = (f32[128,1024]{1,0:T(8,128)S(1)}, f32[128,1024]{1,0:T(8,128)S(1)}, u32[]{:S(2)}, u32[]{:S(2)}) collective-permute-start(f32[128,1024]{1,0:T(8,128)S(1)} %slice_add_fusion.4), channel_id=1, source_target_pairs={{0,8},{8,0},{1,9},{9,1},{2,10},{10,2},{3,11},{11,3},{4,12},{12,4},... | collective-permute-start | bytes 1572872 | tf_op jit(solution)/shard_map/ppermute | solution.py:17
  224.2 18.6 %collective-permute-start.34 = (f32[128,512]{1,0:T(8,128)S(1)}, f32[128,512]{1,0:T(8,128)S(1)}, u32[]{:S(2)}, u32[]{:S(2)}) collective-permute-start(f32[128,512]{1,0:T(8,128)S(1)} %get-tuple-element.97), channel_id=1, source_target_pairs={{0,2},{2,0},{4,6},{6,4},{1,3},{3,1},{5,7},{7,5},{8,10},{10,8},{12,... | collective-permute-start | bytes 786440 | tf_op jit(solution)/shard_map/ppermute | solution.py:17
  228.0 14.9 %collective-permute-start.33 = (f32[128,512]{1,0:T(8,128)S(1)}, f32[128,512]{1,0:T(8,128)S(1)}, u32[]{:S(2)}, u32[]{:S(2)}) collective-permute-start(f32[128,512]{1,0:T(8,128)S(1)} %get-tuple-element.98), channel_id=1, source_target_pairs={{0,16},{2,18},{4,20},{6,22},{16,0},{18,2},{20,4},{22,6},{1,17},{3,... | collective-permute-start | bytes 786440 | tf_op jit(solution)/shard_map/ppermute | solution.py:21
  (27 other events, 205.7 us)
Sparse Core Ops, SparseCore 0:
  90.0 55.1 all-gather.4
  146.9 50.4 all-gather.6
